TPU v7x, 32 devices: a whole 2x2x4 slice. The times are simulated.
32 devices in a mesh: lat: 2 (over x), lon: 16 (over z, y, core).
Axes of the slice: x: 2, y: 2, z: 4, core: 2. Of those that a mesh axis runs over, the one named last changes fastest.
Arguments:
- grid_state: bfloat16 [84, 32, 2048], P(None, 'lat', 'lon'), may hold values from -6 to 6
- mesh_feat: bfloat16 [8192, 1024], P(('lat', 'lon')), may hold values from -6 to 6
- enc_src: int32 [16, 8192], P(None, ('lat', 'lon')), may hold values from 0 to 5119, as said below
- enc_count: int32 [8192], P(('lat', 'lon')), may hold values from 1 to 16, as said below
- nbr_ids: int32 [32, 8192], P(None, ('lat', 'lon')), may hold values from 0 to 8191, as said below
- nbr_count: int32 [8192], P(('lat', 'lon')), may hold values from 2 to 32, as said below
- dec_src: int32 [3, 32, 2048], P(None, 'lat', 'lon'), may hold values from 0 to 8191, as said below
- w_embed: bfloat16 [84, 1024], replicated, may hold values from -0.625 to 0.625
- w_encode: bfloat16 [1024, 1024], replicated, may hold values from -0.1875 to 0.1875
- w_query: bfloat16 [1024, 1024], replicated, may hold values from -4 to 4
- w_key: bfloat16 [1024, 1024], replicated, may hold values from -4 to 4
- w_value: bfloat16 [1024, 1024], replicated, may hold values from -0.1875 to 0.1875
- w_output: bfloat16 [1024, 1024], replicated, may hold values from -0.1875 to 0.1875
- w_decode: bfloat16 [1024, 1024], replicated, may hold values from -0.1875 to 0.1875
- w_readout: bfloat16 [1024, 84], replicated, may hold values from -0.1875 to 0.1875
- norm_attn: float32 [1024], replicated, may hold values from 0.5 to 1.5
- norm_dec: float32 [1024], replicated, may hold values from 0.5 to 1.5
Outputs:
- denoised: float32 [84, 32, 2048], P(None, 'lat', 'lon')
Inputs may be any that keep to these rules, and one draw needn't show every extreme that they name: `enc_src`: mesh node j belongs to block j // 256, numbered lat index times the number of lon indices plus lon index. Every entry of column j, padding included, names a cell of the window of 160 columns around that lon index's sector, in any row. `enc_count`: some node of every block has 16. `nbr_ids`: slot 0 of node j is j itself. The 32 slots of a node, padding included, are distinct mesh nodes whose block has the same or a cyclically adjacent lon index, and any lat index. `nbr_count`: some node of every block has 32. `dec_src`: the mesh nodes feeding cell (r, c) lie in blocks whose lon index is c // 128 or cyclically adjacent to it, any lat index.
All inputs are finite; a program needn't handle non-finite values.
Results may differ from a plain program's by a relative error of at most 0.0039.
Values may be sent and summed in bfloat16 or wider, within the bound.
No kernel may reach another device: no remote copies, remote signals or barrier semaphores. Data moves between devices by JAX's collectives and lax.ppermute only.
A program may use at most 128 MiB of HBM per device.

v0:
```python
import jax
import jax.numpy as jnp
from jax import lax
from jax.sharding import PartitionSpec as P

HEADS = 16
HALO = 16
KM = 32


def with_halo(block, sides, width):
    for axis, dim in sides:
        count = lax.axis_size(axis)
        forward = [(i, i + 1) for i in range(count - 1)]
        forward.append((count - 1, 0))
        backward = [(target, source) for source, target in forward]
        low = lax.ppermute(
            lax.slice_in_dim(block, block.shape[dim] - width, None, axis=dim), axis, forward
        )
        high = lax.ppermute(lax.slice_in_dim(block, 0, width, axis=dim), axis, backward)
        block = jnp.concatenate([low, block, high], axis=dim)
    return block


def passed_along(value, axis, steps):
    count = lax.axis_size(axis)
    pairs = [(source, (source + steps) % count) for source in range(count)]
    return lax.ppermute(value, axis, pairs)


def layer_norm(inputs_f, gain):
    centre = inputs_f - jnp.mean(inputs_f, axis=-1, keepdims=True)
    spread = jnp.mean(centre * centre, axis=-1, keepdims=True)
    return centre * lax.rsqrt(spread + 1e-05) * gain


def window_index(global_ids, node_count, lon_count, sector):
    device = global_ids // node_count
    band_index = device // lon_count
    offset = (device % lon_count - sector + 1) % lon_count
    return (band_index * 3 + offset) * node_count + global_ids % node_count


def arrange(from_west, own_part, from_east, node_count, axis_pos):
    full_shape = own_part.shape
    band_count = full_shape[axis_pos] // node_count
    parted = full_shape[:axis_pos] + (band_count, 1, node_count) + full_shape[axis_pos + 1 :]
    joined = jnp.concatenate(
        [from_west.reshape(parted), own_part.reshape(parted), from_east.reshape(parted)],
        axis=axis_pos + 1,
    )
    return joined.reshape(
        full_shape[:axis_pos] + (band_count * 3 * node_count,) + full_shape[axis_pos + 1 :]
    )


def body(
    grid_state,
    mesh_feat,
    enc_src,
    enc_count,
    nbr_ids,
    nbr_count,
    dec_src,
    w_embed,
    w_encode,
    w_query,
    w_key,
    w_value,
    w_output,
    w_decode,
    w_readout,
    norm_attn,
    norm_dec,
):
    lon_count = lax.axis_size("lon")
    sector = lax.axis_index("lon")
    variables, lat_rows, lon_cols = grid_state.shape
    node_count, feature_count = mesh_feat.shape
    head_count = HEADS
    head_width = feature_count // head_count
    padded = with_halo(grid_state, (("lon", 2),), HALO)
    grid_window = lax.all_gather(padded, "lat", axis=1, tiled=True)
    flat_grid = grid_window.reshape(variables, -1)
    picked = jnp.take(flat_grid, enc_src, axis=1).astype(jnp.float32)
    live_edge = lax.broadcasted_iota(jnp.int32, enc_src.shape, 0) < enc_count[None, :]
    summed = jnp.sum(jnp.where(live_edge[None], picked, 0.0), axis=1)
    mean_cells = (summed / enc_count.astype(jnp.float32)[None, :]).astype(jnp.bfloat16)
    embedded = jax.nn.silu(
        lax.dot_general(
            mean_cells, w_embed, (((0,), (0,)), ((), ())), preferred_element_type=jnp.float32
        )
    ).astype(jnp.bfloat16)
    latent = mesh_feat.astype(jnp.float32) + jnp.dot(
        embedded, w_encode, preferred_element_type=jnp.float32
    )
    normed = layer_norm(latent, norm_attn).astype(jnp.bfloat16)
    queries = jnp.dot(normed, w_query, preferred_element_type=jnp.float32).astype(jnp.bfloat16)
    banded = lax.all_gather(normed, "lat", axis=0, tiled=True)
    from_west = passed_along(banded, "lon", 1)
    from_east = passed_along(banded, "lon", -1)
    normed_window = arrange(from_west, banded, from_east, node_count, 0)
    key_window = jnp.dot(normed_window, w_key, preferred_element_type=jnp.float32).astype(
        jnp.bfloat16
    )
    value_window = jnp.dot(normed_window, w_value, preferred_element_type=jnp.float32).astype(
        jnp.bfloat16
    )
    neighbour = window_index(nbr_ids, node_count, lon_count, sector)
    live_slot = lax.broadcasted_iota(jnp.int32, nbr_ids.shape, 0) < nbr_count[None, :]
    block_rows = min(node_count, 512)
    blocks = node_count // block_rows
    score_scale = head_width ** (-0.5)
    query_blocks = queries.reshape(blocks, block_rows, head_count, head_width)
    index_blocks = neighbour.reshape(KM, blocks, block_rows).transpose(1, 0, 2)
    live_blocks = live_slot.reshape(KM, blocks, block_rows).transpose(1, 0, 2)

    def attend(operands):
        query_block, index_block, live_block = operands
        near_keys = jnp.take(key_window, index_block, axis=0).reshape(
            KM, block_rows, head_count, head_width
        )
        near_values = jnp.take(value_window, index_block, axis=0).reshape(
            KM, block_rows, head_count, head_width
        )
        scores = (
            jnp.einsum("bhd,kbhd->kbh", query_block, near_keys, preferred_element_type=jnp.float32)
            * score_scale
        )
        scores = jnp.where(live_block[:, :, None], scores, -jnp.inf)
        peak_score = jnp.max(scores, axis=0, keepdims=True)
        expo_score = jnp.where(live_block[:, :, None], jnp.exp(scores - peak_score), 0.0)
        weights = (expo_score / jnp.sum(expo_score, axis=0, keepdims=True)).astype(jnp.bfloat16)
        context = jnp.einsum(
            "kbh,kbhd->bhd", weights, near_values, preferred_element_type=jnp.float32
        )
        return context.astype(jnp.bfloat16).reshape(block_rows, feature_count)

    context = lax.map(attend, (query_blocks, index_blocks, live_blocks)).reshape(
        node_count, feature_count
    )
    mixed = latent + jnp.dot(context, w_output, preferred_element_type=jnp.float32)
    normed_out = layer_norm(mixed, norm_dec).astype(jnp.bfloat16)
    decoded = jax.nn.silu(jnp.dot(normed_out, w_decode, preferred_element_type=jnp.float32)).astype(
        jnp.bfloat16
    )
    local_read = lax.dot_general(
        w_readout, decoded, (((0,), (1,)), ((), ())), preferred_element_type=jnp.float32
    ).astype(jnp.bfloat16)
    banded = lax.all_gather(local_read, "lat", axis=1, tiled=True)
    from_west = passed_along(banded, "lon", 1)
    from_east = passed_along(banded, "lon", -1)
    readout = arrange(from_west, banded, from_east, node_count, 1)
    targets = window_index(dec_src, node_count, lon_count, sector)
    picked_out = jnp.take(readout, targets.reshape(-1), axis=1).reshape(
        variables, 3, lat_rows, lon_cols
    )
    update = jnp.sum(picked_out.astype(jnp.float32), axis=1) / 3.0
    return grid_state.astype(jnp.float32) + update


def solution(mesh):
    in_specs = (
        P(None, "lat", "lon"),
        P(("lat", "lon"), None),
        P(None, ("lat", "lon")),
        P(("lat", "lon")),
        P(None, ("lat", "lon")),
        P(("lat", "lon")),
        P(None, "lat", "lon"),
        P(),
        P(),
        P(),
        P(),
        P(),
        P(),
        P(),
        P(),
        P(),
        P(),
    )
    out_specs = P(None, "lat", "lon")
    return jax.shard_map(body, mesh=mesh, in_specs=in_specs, out_specs=out_specs, check_vma=False)
```

profile of v0, /device:TPU:0, one launch (start us, length us, event | category | flops | bytes accessed | tf_op | source)
XLA Modules:
  0.0 324.7 jit_solution(1549361710363902972)
XLA Ops:
  6.5 1.4 fusion.56
  7.9 0.5 collective-permute-start
  8.4 5.1 %collective-permute-start.1 = (bf16[84,16,16]{2,1,0:T(8,128)(2,1)S(1)}, bf16[84,16,16]{2,1,0:T(8,128)(2,1)S(1)}, u32[]{:S(2)}, u32[]{:S(2)}) collective-permute-start(bf16[84,16,16]{2,1,0:T(8,128)(2,1)S(1)} %get-tuple-element.32), channel_id=1, source_target_pairs={{1,0},{2,1},{3,2},{4,3},{5,4},{6,5},{7,6},{8,7},{9,8},{10,9},{11,1... | collective-permute-start | bytes 129032 | tf_op jit(solution)/shard_map/ppermute | solution.py:20
  13.5 0.7 fusion.45
  14.2 1.4 compare_and_fusion.1
  15.6 0.7 iota_compare_fusion.1
  16.4 0.7 convert_element_type.56
  17.1 1.4 collective-permute-done
  18.5 1.4 pad_maximum_fusion.1
  19.9 17.0 %all_gather.9 = bf16[84,32,160]{2,1,0:T(8,128)(2,1)} all-gather(bf16[84,16,160]{2,1,0:T(8,128)(2,1)S(1)} %pad_maximum_fusion.1), channel_id=1, replica_groups=mesh['lat'=2,'lon'=16] {'lat'}, dimensions={1}, use_global_device_ids=true | all-gather | bytes 1290240 | tf_op jit(solution)/shard_map/all_gather | solution.py:83
  36.9 2.7 copy.50
  39.6 14.9 %gather_fusion = bf16[4096,84]{1,0:T(8,128)(2,1)} fusion(bf16[84,5120]{0,1:T(8,128)(2,1)S(1)} %bitcast.64, s32[4096]{0:T(1024)S(1)} %broadcast_clamp_fusion.2), kind=kCustom, calls=%fused_computation.2 | custom fusion | bytes 1392640 | tf_op jit(solution)/shard_map/jit(_take)/gather | solution.py:85
  54.5 3.0 select_reduce_fusion
  57.5 2.8 fusion.57
  60.6 1.0 multiply_convert_fusion.2
  61.7 24.5 %all-gather.2.cloned.1.call-done = bf16[512,1024]{1,0:T(8,128)(2,1)} async-done(((bf16[256,1024]{1,0:T(8,128)(2,1)}), bf16[512,1024]{1,0:T(8,128)(2,1)}) %all-gather.2.cloned.1.call-update) | async-done | bytes 1048592 | tf_op jit(solution)/shard_map/all_gather | solution.py:99
  86.1 3.7 %collective-permute-start.3 = (bf16[512,1024]{1,0:T(8,128)(2,1)}, bf16[512,1024]{1,0:T(8,128)(2,1)}, u32[]{:S(2)}, u32[]{:S(2)}) collective-permute-start(bf16[512,1024]{1,0:T(8,128)(2,1)} %all-gather.2.cloned.1.call-done), channel_id=1, source_target_pairs={{0,15},{1,0},{2,1},{3,2},{4,3},{5,4},{6,5},{7,6},{8,7},{9,8},{10,9... | collective-permute-start | bytes 3145736 | tf_op jit(solution)/shard_map/ppermute | solution.py:28
  90.0 3.3 %convolution_convert_fusion.2 = bf16[256,1024]{1,0:T(8,128)(2,1)} fusion(bf16[256,1024]{1,0:T(8,128)(2,1)} %multiply_convert_fusion.2, bf16[1024,1024]{1,0:T(8,128)(2,1)} %param.28), kind=kOutput, calls=%fused_computation.17 | convolution fusion | flops 537133056 | bytes 3145728 | tf_op jit(solution)/shard_map/dot_general | solution.py:98
  93.3 2.0 copy.55
  95.3 1.1 bitcast_convert_fusion
  96.5 6.0 %collective-permute-done.3 = bf16[512,1024]{1,0:T(8,128)(2,1)} collective-permute-done((bf16[512,1024]{1,0:T(8,128)(2,1)}, bf16[512,1024]{1,0:T(8,128)(2,1)}, u32[]{:S(2)}, u32[]{:S(2)}) %collective-permute-start.3) | collective-permute-done | bytes 1048608 | tf_op jit(solution)/shard_map/ppermute | solution.py:28
  102.5 4.7 %collective-permute-done.2 = bf16[512,1024]{1,0:T(8,128)(2,1)} collective-permute-done((bf16[512,1024]{1,0:T(8,128)(2,1)}, bf16[512,1024]{1,0:T(8,128)(2,1)}, u32[]{:S(2)}, u32[]{:S(2)}) %collective-permute-start.2) | collective-permute-done | bytes 1048608 | tf_op jit(solution)/shard_map/ppermute | solution.py:28
  107.2 2.2 pad_maximum_fusion
  109.4 1.6 copy-done.5
  111.0 4.7 %convolution_convert_fusion.1 = bf16[1536,1024]{1,0:T(8,128)(2,1)} fusion(bf16[1536,1024]{1,0:T(8,128)(2,1)S(1)} %bitcast.66, bf16[1024,1024]{1,0:T(8,128)(2,1)S(1)} %copy-done), kind=kOutput, calls=%fused_computation.11 | convolution fusion | flops 3222798336 | bytes 8388608 | tf_op jit(solution)/shard_map/dot_general | solution.py:103
  115.7 43.0 %gather_fusion.2 = bf16[8192,1024]{1,0:T(8,128)(2,1)} fusion(bf16[1536,1024]{1,0:T(8,128)(2,1)} %convolution_convert_fusion.1, s32[8192]{0:T(1024)S(1)} %broadcast_clamp_fusion), kind=kCustom, calls=%fused_computation.clone | custom fusion | bytes 33587200 | tf_op jit(solution)/shard_map/while/body/eval_jaxpr/jit(_take)/gather | solution.py:120
  158.7 22.5 %copy.54 = bf16[32,256,1024]{1,2,0:T(8,128)(2,1)} copy(bf16[32,256,1024]{2,1,0:T(8,128)(2,1)} %bitcast.62) | data formatting | bytes 33554432 | tf_op jit(solution)/shard_map/while/body/eval_jaxpr/jit(_take)/gather | solution.py:120
  181.2 12.0 %multiply_reduce_fusion.1 = f32[256,16,32]{0,1,2:T(8,128)S(1)} fusion(f32[256,16,64]{0,2,1:T(8,128)S(1)} %bitcast_convert_fusion, bf16[32,256,1024]{1,2,0:T(8,128)(2,1)} %copy.54, pred[32,256]{1,0:T(8,128)(4,1)S(1)} %get-tuple-element.20), kind=kLoop, calls=%fused_computation.7 | loop fusion | flops 33423360 | bytes 18358272
  193.2 0.4 fusion.8
  193.7 1.1 copy.78
  194.8 6.0 %convolution_convert_fusion = bf16[1536,1024]{1,0:T(8,128)(2,1)S(1)} fusion(bf16[1536,1024]{1,0:T(8,128)(2,1)} %bitcast.67, bf16[1024,1024]{1,0:T(8,128)(2,1)} %param.30), kind=kOutput, calls=%fused_computation.10 | convolution fusion | flops 3222798336 | bytes 8388608 | tf_op jit(solution)/shard_map/dot_general | solution.py:106
  200.7 35.4 %gather_fusion.3 = bf16[8192,1024]{1,0:T(8,128)(2,1)} fusion(bf16[1536,1024]{1,0:T(8,128)(2,1)S(1)} %convolution_convert_fusion, s32[8192]{0:T(1024)S(1)} %broadcast_clamp_fusion), kind=kCustom, calls=%fused_computation.1.clone | custom fusion | bytes 33587200 | tf_op jit(solution)/shard_map/while/body/eval_jaxpr/jit(_take)/gather | solution.py:123
  236.2 22.5 %copy.58 = bf16[32,256,1024]{1,2,0:T(8,128)(2,1)} copy(bf16[32,256,1024]{2,1,0:T(8,128)(2,1)} %bitcast.61) | data formatting | bytes 33554432 | tf_op jit(solution)/shard_map/while/body/eval_jaxpr/jit(_take)/gather | solution.py:123
  258.7 8.9 %broadcast_select_fusion = bf16[32,256,1024]{1,2,0:T(8,128)(2,1)S(1)} fusion(bf16[32,256,1024]{1,2,0:T(8,128)(2,1)} %copy.58, pred[32,256]{1,0:T(8,128)(4,1)S(1)} %get-tuple-element.20), kind=kLoop, calls=%fused_computation.8 | loop fusion | flops 8388608 | bytes 33562624 | tf_op jit(solution)/shard_map/while/body/eval_jaxpr/jit(_take)/select_n | solution.py:123
  267.6 5.4 %multiply_reduce_fusion = bf16[256,16,64]{0,2,1:T(8,128)(2,1)S(1)} fusion(bf16[256,16,32,64]{0,3,1,2:T(8,128)(2,1)S(1)} %bitcast.63, f32[256,16,32]{0,1,2:T(8,128)S(1)} %copy-done.7), kind=kLoop, calls=%fused_computation.6 | loop fusion | flops 24903680 | bytes 17825792 | tf_op jit(solution)/shard_map/while/body/eval_jaxpr/kbh,kbhd->bhd/dot_general | solution.py:134
  273.1 0.8 fusion.58
  274.2 2.6 fusion.9
  276.8 4.7 %all_gather.11 = bf16[84,512]{1,0:T(8,128)(2,1)S(1)} all-gather(bf16[84,256]{1,0:T(8,128)(2,1)S(1)} %fusion.9), channel_id=1, replica_groups=mesh['lat'=2,'lon'=16] {'lat'}, dimensions={1}, use_global_device_ids=true | all-gather | bytes 129024 | tf_op jit(solution)/shard_map/all_gather | solution.py:150
  281.6 3.5 %collective-permute-start.4 = (bf16[84,512]{1,0:T(8,128)(2,1)S(1)}, bf16[84,512]{1,0:T(8,128)(2,1)S(1)}, u32[]{:S(2)}, u32[]{:S(2)}) collective-permute-start(bf16[84,512]{1,0:T(8,128)(2,1)S(1)} %all_gather.11), channel_id=1, source_target_pairs={{0,1},{1,2},{2,3},{3,4},{4,5},{5,6},{6,7},{7,8},{8,9},{9,10},{10,1... | collective-permute-start | bytes 258056 | tf_op jit(solution)/shard_map/ppermute | solution.py:28
  285.0 1.0 collective-permute-start.5
  286.0 2.2 collective-permute-done.4
  288.2 0.5 collective-permute-done.5
  288.7 0.4 pad_maximum_fusion.2
  289.1 0.3 copy.59
  289.5 22.1 %gather_fusion.1 = bf16[6144,84]{1,0:T(8,128)(2,1)} fusion(bf16[84,1536]{0,1:T(8,128)(2,1)S(1)} %bitcast.60, s32[6144]{0:T(1024)S(1)} %broadcast_clamp_fusion.1), kind=kCustom, calls=%fused_computation.3 | custom fusion | bytes 2088960 | tf_op jit(solution)/shard_map/jit(_take)/gather | solution.py:155
  311.6 3.0 convert_reduce_fusion
  314.6 1.2 copy.60
  315.8 2.0 multiply_add_fusion
  (48 shorter events, 0.9 us)
Async XLA Ops:
  6.5 104.5 %copy-start = (bf16[1024,1024]{1,0:T(8,128)(2,1)S(1)}, bf16[1024,1024]{1,0:T(8,128)(2,1)}, u32[]{:S(2)}) copy-start(bf16[1024,1024]{1,0:T(8,128)(2,1)} %param.29) | copy-start | bytes 6291460
  6.5 79.6 %all-gather.2.cloned.1.call-start = ((), (), s32[]{:S(2)}) async-start(), calls=%async_computation | async-start | bytes 1572864 | tf_op jit(solution)/shard_map/all_gather | solution.py:99
  7.9 10.5 %collective-permute-start = (bf16[84,16,16]{2,1,0:T(8,128)(2,1)S(1)}, bf16[84,16,16]{2,1,0:T(8,128)(2,1)S(1)}, u32[]{:S(2)}, u32[]{:S(2)}) collective-permute-start(bf16[84,16,16]{2,1,0:T(8,128)(2,1)S(1)} %get-tuple-element.30), channel_id=1, source_target_pairs={{0,1},{1,2},{2,3},{3,4},{4,5},{5,6},{6,7},{7,8},{8,9},{9,10},{10,1... | collective-permute-start | bytes 129032 | tf_op jit(solution)/shard_map/ppermute | solution.py:17
  8.4 10.0 %collective-permute-start.1 = (bf16[84,16,16]{2,1,0:T(8,128)(2,1)S(1)}, bf16[84,16,16]{2,1,0:T(8,128)(2,1)S(1)}, u32[]{:S(2)}, u32[]{:S(2)}) collective-permute-start(bf16[84,16,16]{2,1,0:T(8,128)(2,1)S(1)} %get-tuple-element.32), channel_id=1, source_target_pairs={{1,0},{2,1},{3,2},{4,3},{5,4},{6,5},{7,6},{8,7},{9,8},{10,9},{11,1... | collective-permute-start | bytes 129032 | tf_op jit(solution)/shard_map/ppermute | solution.py:20
  57.5 3.1 copy-start.10
  60.3 33.0 %copy-start.2 = (f32[256,1024]{1,0:T(8,128)}, f32[256,1024]{1,0:T(8,128)S(1)}, u32[]{:S(2)}) copy-start(f32[256,1024]{1,0:T(8,128)S(1)} %get-tuple-element.34) | copy-start | bytes 3145732
  60.3 29.5 %copy-start.8 = (s32[32,256]{1,0:T(8,128)S(1)}, s32[32,256]{1,0:T(8,128)}, u32[]{:S(2)}) copy-start(s32[32,256]{1,0:T(8,128)} %param.23) | copy-start | bytes 98308
  60.3 29.6 %copy-start.11 = (s32[256]{0:T(256)S(1)}, s32[256]{0:T(256)}, u32[]{:S(2)}) copy-start(s32[256]{0:T(256)} %param.24) | copy-start | bytes 3076
  86.1 16.3 %collective-permute-start.3 = (bf16[512,1024]{1,0:T(8,128)(2,1)}, bf16[512,1024]{1,0:T(8,128)(2,1)}, u32[]{:S(2)}, u32[]{:S(2)}) collective-permute-start(bf16[512,1024]{1,0:T(8,128)(2,1)} %all-gather.2.cloned.1.call-done), channel_id=1, source_target_pairs={{0,15},{1,0},{2,1},{3,2},{4,3},{5,4},{6,5},{7,6},{8,7},{9,8},{10,9... | collective-permute-start | bytes 3145736 | tf_op jit(solution)/shard_map/ppermute | solution.py:28
  89.8 17.3 %collective-permute-start.2 = (bf16[512,1024]{1,0:T(8,128)(2,1)}, bf16[512,1024]{1,0:T(8,128)(2,1)}, u32[]{:S(2)}, u32[]{:S(2)}) collective-permute-start(bf16[512,1024]{1,0:T(8,128)(2,1)} %all-gather.2.cloned.1.call-done), channel_id=1, source_target_pairs={{0,1},{1,2},{2,3},{3,4},{4,5},{5,6},{6,7},{7,8},{8,9},{9,10},{10,1... | collective-permute-start | bytes 3145736 | tf_op jit(solution)/shard_map/ppermute | solution.py:28
  109.4 1.6 copy-start.5
  258.7 8.9 %copy-start.7 = (f32[256,16,32]{0,1,2:T(8,128)S(1)}, f32[256,16,32]{0,1,2:T(8,128)}, u32[]{:S(2)}) copy-start(f32[256,16,32]{0,1,2:T(8,128)} %copy.78) | copy-start | bytes 1572868
  267.6 5.5 %copy-start.3 = (f32[256,1024]{1,0:T(8,128)S(1)}, f32[256,1024]{1,0:T(8,128)}, u32[]{:S(2)}) copy-start(f32[256,1024]{1,0:T(8,128)} %copy-done.2) | copy-start | bytes 3145732
  267.6 5.5 %copy-start.6 = (bf16[1024,1024]{1,0:T(8,128)(2,1)S(1)}, bf16[1024,1024]{1,0:T(8,128)(2,1)}, u32[]{:S(2)}) copy-start(bf16[1024,1024]{1,0:T(8,128)(2,1)} %param.31) | copy-start | bytes 6291460
  273.1 1.1 copy-start.12
  273.1 1.1 copy-start.13
  281.6 6.7 %collective-permute-start.4 = (bf16[84,512]{1,0:T(8,128)(2,1)S(1)}, bf16[84,512]{1,0:T(8,128)(2,1)S(1)}, u32[]{:S(2)}, u32[]{:S(2)}) collective-permute-start(bf16[84,512]{1,0:T(8,128)(2,1)S(1)} %all_gather.11), channel_id=1, source_target_pairs={{0,1},{1,2},{2,3},{3,4},{4,5},{5,6},{6,7},{7,8},{8,9},{9,10},{10,1... | collective-permute-start | bytes 258056 | tf_op jit(solution)/shard_map/ppermute | solution.py:28
  285.0 3.7 %collective-permute-start.5 = (bf16[84,512]{1,0:T(8,128)(2,1)S(1)}, bf16[84,512]{1,0:T(8,128)(2,1)S(1)}, u32[]{:S(2)}, u32[]{:S(2)}) collective-permute-start(bf16[84,512]{1,0:T(8,128)(2,1)S(1)} %all_gather.11), channel_id=1, source_target_pairs={{0,15},{1,0},{2,1},{3,2},{4,3},{5,4},{6,5},{7,6},{8,7},{9,8},{10,9... | collective-permute-start | bytes 258056 | tf_op jit(solution)/shard_map/ppermute | solution.py:28
  289.5 22.1 %copy-start.9 = (pred[3,16,128]{2,1,0:T(8,128)(4,1)S(1)}, pred[3,16,128]{2,1,0:T(8,128)(4,1)}, u32[]{:S(2)}) copy-start(pred[3,16,128]{2,1,0:T(8,128)(4,1)} %get-tuple-element.18) | copy-start | bytes 18436
  289.5 28.4 %copy-start.1 = (bf16[1024,1024]{1,0:T(8,128)(2,1)S(1)}, bf16[1024,1024]{1,0:T(8,128)(2,1)}, u32[]{:S(2)}) copy-start(bf16[1024,1024]{1,0:T(8,128)(2,1)} %param.29) | copy-start | bytes 6291460
  311.6 4.3 %copy-start.4 = (bf16[84,16,128]{2,1,0:T(8,128)(2,1)S(1)}, bf16[84,16,128]{2,1,0:T(8,128)(2,1)}, u32[]{:S(2)}) copy-start(bf16[84,16,128]{2,1,0:T(8,128)(2,1)} %param.19) | copy-start | bytes 1032196
Sparse Core Ops, SparseCore 0:
  61.8 24.3 all-gather.1
where the time goes:
time: 329 us; the launch traced here: 325 us
  local copies, waits for them, and re-layouts  171 us (52%)
  other arithmetic  45.2 us (14%)
  waiting for transfers between devices  39.2 us (12%)
  blocking collectives  21.8 us (7%)
  matrix products  20.2 us (6%)
  starting transfers between devices  13.7 us (4%)
  between operations  13.7 us (4%)
    gather x2, local copies, waits for them, and re-layouts, attend(): jnp.take(key_window, index_block, axis=0)  65.5 us
    gather x2, local copies, waits for them, and re-layouts, attend(): jnp.take(value_window, index_block, axis=0)  57.9 us
    all_gather x1, waiting for transfers between devices, body(): banded = lax.all_gather(normed, 'lat', axis=0, tiled=True)  24.5 us
    gather x1, local copies, waits for them, and re-layouts, body(): jnp.take(readout, targets.reshape(-1), axis=1)  22.1 us
    all_gather x1, blocking collectives, body(): grid_window = lax.all_gather(padded, 'lat', axis=1, tiled=True)  17 us
    gather x1, local copies, waits for them, and re-layouts, body(): picked = jnp.take(flat_grid, enc_src, axis=1).astype(jnp.float32)  14.9 us
    unnamed x3, other arithmetic  13.9 us
    ppermute x4, waiting for transfers between devices, passed_along(): return lax.ppermute(value, axis, pairs)  13.3 us
  transfers between devices with their start and end apart: 7, of which 6 were waited for; matrix products, arithmetic and copies ran while one was open for 3% of the time, Pallas kernels for 0%

commit v1 on v0

v1 whole, which is shorter than its diff:
```python
import functools

import jax
import jax.numpy as jnp
from jax import lax
from jax.experimental import pallas as pl
from jax.experimental.pallas import tpu as pltpu
from jax.sharding import PartitionSpec as P

HEADS = 16
HALO = 16
BF16 = jnp.bfloat16
F32 = jnp.float32
MIB = 1024 * 1024


def params(mib):
    return pltpu.CompilerParams(vmem_limit_bytes=mib * MIB)


def whole(memory=pltpu.VMEM):
    return pl.BlockSpec(memory_space=memory)


def silu(value):
    return 0.5 * value * (1.0 + jnp.tanh(0.5 * value))


def layer_norm(inputs_f, gain):
    centre = inputs_f - jnp.mean(inputs_f, axis=-1, keepdims=True)
    spread = jnp.mean(centre * centre, axis=-1, keepdims=True)
    return centre * lax.rsqrt(spread + 1e-05) * gain


def from_bands(value):
    count = lax.axis_size("lat")
    return [
        lax.ppermute(value, "lat", [(i, (i - step) % count) for i in range(count)])
        for step in range(1, count)
    ]


def from_sides(value):
    count = lax.axis_size("lon")
    west = lax.ppermute(value, "lon", [(i, (i + 1) % count) for i in range(count)])
    east = lax.ppermute(value, "lon", [(i, (i - 1) % count) for i in range(count)])
    return west, east


def quotient(value_f, divisor):
    return jnp.floor((value_f + 0.5) * (1.0 / divisor))


def prep_kernel(grid_ref, src_ref, count_ref, flat_ref, low_ref, high_ref, live_ref, wide):
    rows, cols = grid_ref.shape[1:]
    wide[...] = grid_ref[...].astype(F32)
    for row in range(rows):
        line = wide[:, row, :]
        flat_ref[:, row * cols : (row + 1) * cols] = line.astype(BF16)
        low_ref[:, row * HALO : (row + 1) * HALO] = line[:, :HALO].astype(BF16)
        high_ref[:, row * HALO : (row + 1) * HALO] = line[:, cols - HALO :].astype(BF16)
    slot = lax.broadcasted_iota(jnp.int32, src_ref.shape, 0)
    live_ref[...] = jnp.where(slot < count_ref[...], src_ref[...], -1)


def encode_kernel(place_ref, src_ref, flat_ref, west_ref, east_ref, out_ref, counts):
    slots, nodes = src_ref.shape
    cells = flat_ref.shape[1]
    rows = west_ref.shape[1] // HALO
    cols = cells // rows
    span = cols + 2 * HALO
    lanes = 128
    source = src_ref[...].astype(F32)
    row_of = quotient(source, span)
    col_of = source - row_of * span
    row_of = row_of - (place_ref[0] * rows).astype(F32)
    iota = lax.broadcasted_iota(jnp.int32, (span, lanes), 0).astype(F32).astype(BF16)
    one = jnp.ones((span, lanes), BF16)
    none = jnp.zeros((span, lanes), BF16)
    for row in range(rows):
        code = jnp.where(row_of == row, col_of, -1.0).astype(BF16)
        for tile in range(nodes // lanes):
            at = slice(tile * lanes, (tile + 1) * lanes)
            total = none
            for slot in range(slots):
                total = total + jnp.where(iota == code[slot : slot + 1, at], one, none)
            counts[row * cols : (row + 1) * cols, at] = total[HALO : HALO + cols]
            counts[cells + row * HALO : cells + (row + 1) * HALO, at] = total[:HALO]
            counts[cells + (rows + row) * HALO : cells + (rows + row + 1) * HALO, at] = total[
                HALO + cols :
            ]
    rim = rows * HALO
    summed = jnp.dot(flat_ref[...], counts[:cells], preferred_element_type=F32)
    summed += jnp.dot(west_ref[...], counts[cells : cells + rim], preferred_element_type=F32)
    summed += jnp.dot(east_ref[...], counts[cells + rim :], preferred_element_type=F32)
    out_ref[...] = summed


def mean_kernel(src_ref, own_ref, *refs):
    others, out_ref = refs[:-1], refs[-1]
    bands = len(others) + 1
    nodes = own_ref.shape[1] // bands
    count = jnp.sum(jnp.where(src_ref[...] >= 0, 1.0, 0.0), axis=0, keepdims=True)
    for band in range(bands):
        at = slice(band * nodes, (band + 1) * nodes)
        total = own_ref[:, at]
        for step, other in enumerate(others, 1):
            there = (band - step) % bands
            total = total + other[:, there * nodes : (there + 1) * nodes]
        out_ref[:, at] = (total / count[:, at]).astype(BF16)


def place_of(ids, place_ref, node_count, bands, sectors):
    ids_f = ids.astype(F32)
    device = quotient(ids_f, node_count)
    member = ids_f - device * node_count
    band = quotient(device, sectors)
    away = device - band * sectors - place_ref[1].astype(F32)
    side = jnp.where(away == 0, 0.0, 2.0)
    side = jnp.where((away == -1) | (away == sectors - 1), 1.0, side)
    band = band - place_ref[0].astype(F32)
    band = jnp.where(band < 0, band + bands, band)
    return side * bands + band, member


def bias_kernel(bands, sectors, place_ref, ids_ref, count_ref, out_ref):
    slots, nodes = ids_ref.shape
    lanes = 128
    block, member = place_of(ids_ref[...], place_ref, nodes, bands, sectors)
    slot_of = lax.broadcasted_iota(jnp.int32, (slots, nodes), 0)
    block = jnp.where(slot_of < count_ref[...], block, -1.0)
    iota = lax.broadcasted_iota(jnp.int32, (nodes, lanes), 0).astype(F32).astype(BF16)
    shut = jnp.full((nodes, lanes), -1e30, BF16)
    opened = jnp.zeros((nodes, lanes), BF16)
    for part in range(3 * bands):
        code = jnp.where(block == part, member, -1.0).astype(BF16)
        for tile in range(nodes // lanes):
            at = slice(tile * lanes, (tile + 1) * lanes)
            total = shut
            for slot in range(slots):
                total = jnp.where(iota == code[slot : slot + 1, at], opened, total)
            out_ref[at, part * nodes : (part + 1) * nodes] = total.astype(F32).T


def latent_of(mean, feat, w_embed, w_encode):
    embedded = silu(
        lax.dot_general(mean, w_embed, (((0,), (0,)), ((), ())), preferred_element_type=F32)
    ).astype(BF16)
    return feat.astype(F32) + jnp.dot(embedded, w_encode, preferred_element_type=F32)


def sector_kernel(
    mean_ref, feat_ref, gain_ref, w_embed, w_encode, w_query, w_key, w_value,
    latent_ref, query_ref, key_ref, value_ref,
):
    nodes = latent_ref.shape[0]
    for part in range(feat_ref.shape[0] // nodes):
        at = slice(part * nodes, (part + 1) * nodes)
        latent = latent_of(mean_ref[:, at], feat_ref[at], w_embed[...], w_encode[...])
        normed = layer_norm(latent, gain_ref[...]).astype(BF16)
        if part == 0:
            latent_ref[...] = latent
            query_ref[...] = jnp.dot(normed, w_query[...], preferred_element_type=F32).astype(BF16)
        key_ref[at] = jnp.dot(normed, w_key[...], preferred_element_type=F32).astype(BF16)
        value_ref[at] = jnp.dot(normed, w_value[...], preferred_element_type=F32).astype(BF16)


def attend_kernel(
    mean_w, mean_e, feat_w, feat_e, bias_ref, latent_ref, query_ref, key_own, value_own,
    gain_ref, gain_dec_ref, w_embed, w_encode, w_key, w_value, w_output, w_decode, w_read,
    out_ref, key_ref, value_ref, score_ref, weight_ref, context_ref,
):
    nodes, features = latent_ref.shape
    sector_nodes = feat_w.shape[0]
    key_ref[:sector_nodes] = key_own[...]
    value_ref[:sector_nodes] = value_own[...]
    for side, (mean_ref, feat_ref) in enumerate(((mean_w, feat_w), (mean_e, feat_e)), 1):
        for part in range(sector_nodes // nodes):
            at = slice(part * nodes, (part + 1) * nodes)
            to = slice(side * sector_nodes + part * nodes, side * sector_nodes + (part + 1) * nodes)
            latent = latent_of(mean_ref[:, at], feat_ref[at], w_embed[...], w_encode[...])
            normed = layer_norm(latent, gain_ref[...]).astype(BF16)
            key_ref[to] = jnp.dot(normed, w_key[...], preferred_element_type=F32).astype(BF16)
            value_ref[to] = jnp.dot(normed, w_value[...], preferred_element_type=F32).astype(BF16)

    width = features // HEADS
    group = 256
    per_group = group // width
    scale = width**-0.5
    chunk = 16
    head_of = lax.broadcasted_iota(jnp.int32, (nodes, group), 1) // width

    def attend(step, carry):
        at = pl.ds(pl.multiple_of(step * group, group), group)
        query = (query_ref[:, at].astype(F32) * scale)
        keys = key_ref[:, at]
        values = value_ref[:, at]
        gathered = jnp.zeros((nodes, group), F32)
        for head in range(per_group):
            own = jnp.where(head_of == head, query, 0.0).astype(BF16)
            score_ref[head] = lax.dot_general(
                own, keys, (((1,), (1,)), ((), ())), preferred_element_type=F32
            )
            sums = []
            for start in range(0, nodes, chunk):
                rows = slice(start, start + chunk)
                scores = score_ref[head, rows] + bias_ref[rows]
                peak = jnp.max(scores, axis=1, keepdims=True)
                expo = jnp.exp(scores - peak)
                sums.append(jnp.sum(expo, axis=1, keepdims=True))
                weight_ref[head, rows] = expo.astype(BF16)
            total = jnp.concatenate(sums, axis=0)
            mixed = jnp.dot(weight_ref[head], values, preferred_element_type=F32)
            gathered = jnp.where(head_of == head, mixed / total, gathered)
        context_ref[:, at] = gathered.astype(BF16)
        return carry

    lax.fori_loop(0, features // group, attend, 0)
    mixed = latent_ref[...] + jnp.dot(context_ref[...], w_output[...], preferred_element_type=F32)
    normed_out = layer_norm(mixed, gain_dec_ref[...]).astype(BF16)
    decoded = silu(jnp.dot(normed_out, w_decode[...], preferred_element_type=F32)).astype(BF16)
    out_ref[...] = lax.dot_general(
        w_read[...], decoded, (((0,), (1,)), ((), ())), preferred_element_type=F32
    ).astype(BF16)


def decode_kernel(bands, sectors, nodes, place_ref, dec_ref, own_ref, west_ref, east_ref, grid_ref, out_ref):
    rows, cols = grid_ref.shape[1:]
    iota = lax.broadcasted_iota(jnp.int32, (nodes, cols), 0).astype(F32).astype(BF16)
    one = jnp.ones((nodes, cols), BF16)
    none = jnp.zeros((nodes, cols), BF16)
    block, member = place_of(dec_ref[...], place_ref, nodes, bands, sectors)
    for row in range(rows):
        update = jnp.zeros((grid_ref.shape[0], cols), F32)
        for part in range(3 * bands):
            code = jnp.where(block[:, row] == part, member[:, row], -1.0).astype(BF16)
            counts = none
            for slot in range(code.shape[0]):
                counts = counts + jnp.where(iota == code[slot : slot + 1], one, none)
            side, band = divmod(part, bands)
            ref = (own_ref, west_ref, east_ref)[side]
            update += jnp.dot(
                ref[:, band * nodes : (band + 1) * nodes], counts, preferred_element_type=F32
            )
        out_ref[:, row, :] = update / 3.0
    out_ref[...] += grid_ref[...].astype(F32)


def call(kernel, outs, operands, scratch=(), scalars=0, mib=48, flops=0, moved=0):
    specs = [whole(pltpu.SMEM)] * scalars + [whole()] * (len(operands) - scalars)
    single = not isinstance(outs, (list, tuple))
    return pl.pallas_call(
        kernel,
        out_shape=outs,
        in_specs=specs,
        out_specs=whole() if single else [whole()] * len(outs),
        scratch_shapes=list(scratch),
        compiler_params=params(mib),
        cost_estimate=pl.CostEstimate(flops=flops, bytes_accessed=moved, transcendentals=0),
    )(*operands)


def body(
    grid_state, mesh_feat, enc_src, enc_count, nbr_ids, nbr_count, dec_src,
    w_embed, w_encode, w_query, w_key, w_value, w_output, w_decode, w_readout, norm_attn, norm_dec,
):
    shape = jax.ShapeDtypeStruct
    bands, sectors = lax.axis_size("lat"), lax.axis_size("lon")
    place = jnp.stack([lax.axis_index("lat"), lax.axis_index("lon")]).astype(jnp.int32)
    variables, rows, cols = grid_state.shape
    nodes, features = mesh_feat.shape
    slots = enc_src.shape[0]
    cells, rim = rows * cols, rows * HALO
    sector_nodes = bands * nodes
    window = 3 * sector_nodes

    flat, low, high, live = call(
        prep_kernel,
        [
            shape((variables, cells), BF16),
            shape((variables, rim), BF16),
            shape((variables, rim), BF16),
            shape((slots, nodes), jnp.int32),
        ],
        (grid_state, enc_src, enc_count[None]),
        [pltpu.VMEM((variables, rows, cols), F32)],
    )
    sources = jnp.concatenate([live] + from_bands(live), axis=1)
    west_rim = from_sides(high)[0]
    east_rim = from_sides(low)[1]
    feats = jnp.concatenate([mesh_feat] + from_bands(mesh_feat), axis=0)
    feat_w, feat_e = from_sides(feats)
    bias = call(
        functools.partial(bias_kernel, bands, sectors),
        shape((nodes, window), F32),
        (place, nbr_ids, nbr_count[None]),
        scalars=1,
        flops=10_000_000,
        moved=8_000_000,
    )
    summed = call(
        encode_kernel,
        shape((variables, sector_nodes), F32),
        (place, sources, flat, west_rim, east_rim),
        [pltpu.VMEM((cells + 2 * rim, sector_nodes), BF16)],
        scalars=1,
    )
    mean = call(
        mean_kernel,
        shape((variables, sector_nodes), BF16),
        (sources, summed, *from_bands(summed)),
    )
    mean_w, mean_e = from_sides(mean)
    gain = norm_attn[None]
    latent, query, key, value = call(
        sector_kernel,
        [
            shape((nodes, features), F32),
            shape((nodes, features), BF16),
            shape((sector_nodes, features), BF16),
            shape((sector_nodes, features), BF16),
        ],
        (mean, feats, gain, w_embed, w_encode, w_query, w_key, w_value),
        flops=4_000_000_000,
        moved=12_000_000,
    )
    per_group = 256 * HEADS // features
    readout = call(
        attend_kernel,
        shape((variables, nodes), BF16),
        (
            mean_w, mean_e, feat_w, feat_e, bias, latent, query, key, value,
            gain, norm_dec[None], w_embed, w_encode, w_key, w_value, w_output, w_decode, w_readout,
        ),
        [
            pltpu.VMEM((window, features), BF16),
            pltpu.VMEM((window, features), BF16),
            pltpu.VMEM((per_group, nodes, window), F32),
            pltpu.VMEM((per_group, nodes, window), BF16),
            pltpu.VMEM((nodes, features), BF16),
        ],
        mib=60,
    )
    reads = jnp.concatenate([readout] + from_bands(readout), axis=1)
    read_w, read_e = from_sides(reads)
    return call(
        functools.partial(decode_kernel, bands, sectors, nodes),
        shape(grid_state.shape, F32),
        (place, dec_src, reads, read_w, read_e, grid_state),
        scalars=1,
    )


def solution(mesh):
    in_specs = (
        P(None, "lat", "lon"),
        P(("lat", "lon"), None),
        P(None, ("lat", "lon")),
        P(("lat", "lon")),
        P(None, ("lat", "lon")),
        P(("lat", "lon")),
        P(None, "lat", "lon"),
    ) + (P(),) * 10
    out_specs = P(None, "lat", "lon")
    return jax.shard_map(body, mesh=mesh, in_specs=in_specs, out_specs=out_specs, check_vma=False)
```

time: 329 us -> 116 us (0.35); the launches traced: 325 us -> 116 us
  local copies, waits for them, and re-layouts: 171 us -> 8.89 us
  Pallas kernels: 0 us -> 51.7 us
  other arithmetic: 45.2 us -> 0.87 us
  blocking collectives: 21.8 us -> 0 us
  matrix products: 20.2 us -> 0 us
  starting transfers between devices: 13.7 us -> 31.1 us
  waiting for transfers between devices: 39.2 us -> 23 us
  between operations: 13.7 us -> 0.14 us
    gather x6 -> x0, local copies, waits for them, and re-layouts: 160 us -> none  [the longest x2 65.5 us: attend(): jnp.take(key_window, index_block, axis=0)]
    pallas_call x0 -> x7, Pallas kernels: none -> 51.7 us  [call(): pl.pallas_call(kernel, out_shape=outs, in_specs=specs, out_specs=whole()...]
    all_gather x1 -> x0, waiting for transfers between devices: 24.5 us -> none  [body(): banded = lax.all_gather(normed, 'lat', axis=0, tiled=True)]
    all_gather x2 -> x0, blocking collectives: 21.8 us -> none  [the longest x1 17 us: body(): grid_window = lax.all_gather(padded, 'lat', axis=1, tiled=True)]
    dot_general x6 -> x0, matrix products: 20.2 us -> none  [the longest x1 5.98 us: body(): jnp.dot(normed_window, w_value, preferred_element_type=jnp.float32)]
    ppermute x6 -> x12, starting transfers between devices: 13.7 us -> 31.1 us  [the longest x4 13.3 us: from_sides(): lax.ppermute(value, 'lon', [(i, (i - 1) % count) for i in range(count)])]
    unnamed x3 -> x0, other arithmetic: 13.9 us -> none
    select_n x2 -> x0, other arithmetic: 8.92 us -> none  [the longest x1 8.89 us: attend(): jnp.take(value_window, index_block, axis=0)]
  transfers between devices with their start and end apart: 7 -> 12, of which waited for: 6 -> 4; matrix products, arithmetic and copies ran while one was open for 3% -> 3% of each run, Pallas kernels for 0% -> 15%
where the time goes in v1:
time: 116 us
  Pallas kernels  51.7 us (45%)
  starting transfers between devices  31.1 us (27%)
  waiting for transfers between devices  23 us (20%)
  local copies, waits for them, and re-layouts  8.89 us (8%)
    pallas_call x7, Pallas kernels, call(): pl.pallas_call(kernel, out_shape=outs, in_specs=specs, out_specs=whole()...  51.7 us
    ppermute x4, waiting for transfers between devices, from_bands(): lax.ppermute(value, 'lat', [(i, (i - step) % count) for i in range(count)])  14.7 us
    ppermute x4, starting transfers between devices, from_sides(): lax.ppermute(value, 'lon', [(i, (i - 1) % count) for i in range(count)])  13.3 us
    ppermute x4, starting transfers between devices, from_sides(): lax.ppermute(value, 'lon', [(i, (i + 1) % count) for i in range(count)])  10.7 us
    unnamed x35, local copies, waits for them, and re-layouts  8.86 us
    ppermute x4, waiting for transfers between devices, from_sides(): lax.ppermute(value, 'lon', [(i, (i + 1) % count) for i in range(count)])  8.24 us
    ppermute x4, starting transfers between devices, from_bands(): lax.ppermute(value, 'lat', [(i, (i - step) % count) for i in range(count)])  7.14 us
  transfers between devices with their start and end apart: 12, of which 4 were waited for; matrix products, arithmetic and copies ran while one was open for 3% of the time, Pallas kernels for 15%

profile of v1, /device:TPU:0, one launch (start us, length us, event | category | flops | bytes accessed | tf_op | source)
XLA Modules:
  0.0 115.7 jit_solution(3383145197541325933)
XLA Ops:
  0.0 3.0 %collective-permute-start.6 = (bf16[256,1024]{1,0:T(8,128)(2,1)}, bf16[256,1024]{1,0:T(8,128)(2,1)S(1)}, u32[]{:S(2)}, u32[]{:S(2)}) collective-permute-start(bf16[256,1024]{1,0:T(8,128)(2,1)} %param.18), channel_id=1, source_target_pairs={{0,16},{16,0},{1,17},{17,1},{2,18},{18,2},{3,19},{19,3},{4,20},{20... | collective-permute-start | bytes 1572872 | tf_op jit(solution)/shard_map/ppermute | solution.py:38
  3.0 1.1 constant_dynamic-update-slice_fusion.3
  4.1 0.0 copy-start.6
  4.2 0.0 copy-start.10
  4.2 11.0 %collective-permute-done.6 = bf16[256,1024]{1,0:T(8,128)(2,1)S(1)} collective-permute-done((bf16[256,1024]{1,0:T(8,128)(2,1)}, bf16[256,1024]{1,0:T(8,128)(2,1)S(1)}, u32[]{:S(2)}, u32[]{:S(2)}) %collective-permute-start.6) | collective-permute-done | bytes 524320 | tf_op jit(solution)/shard_map/ppermute | solution.py:38
  15.2 0.1 collective-permute-start.7
  15.3 4.4 %collective-permute-start.8 = (bf16[512,1024]{1,0:T(8,128)(2,1)S(1)}, bf16[512,1024]{1,0:T(8,128)(2,1)}, u32[]{:S(2)}, u32[]{:S(2)}) collective-permute-start(bf16[512,1024]{1,0:T(8,128)(2,1)S(1)} %constant_dynamic-update-slice_fusion.2.feat_ref), channel_id=1, source_target_pairs={{0,15},{1,0},{2,1},{3,2},{4,3},{5,4},{6,5},{7,6},{8,7},{9,8},{10,9... | collective-permute-start | bytes 3145736 | tf_op jit(solution)/shard_map/ppermute | solution.py:46
  19.7 0.0 copy-done.11
  19.7 0.8 shard_map.163
  20.5 1.8 %collective-permute-start = (s32[16,256]{1,0:T(8,128)S(1)}, s32[16,256]{1,0:T(8,128)S(1)}, u32[]{:S(2)}, u32[]{:S(2)}) collective-permute-start(s32[16,256]{1,0:T(8,128)S(1)} %get-tuple-element.13), channel_id=1, source_target_pairs={{0,16},{16,0},{1,17},{17,1},{2,18},{18,2},{3,19},{19,3},{4,20},{20... | collective-permute-start | bytes 49160 | tf_op jit(solution)/shard_map/ppermute | solution.py:38
  22.3 0.0 collective-permute-start.1
  22.3 4.4 %collective-permute-start.2 = (bf16[84,256]{1,0:T(8,128)(2,1)S(1)}, bf16[84,256]{1,0:T(8,128)(2,1)S(1)}, u32[]{:S(2)}, u32[]{:S(2)}) collective-permute-start(bf16[84,256]{1,0:T(8,128)(2,1)S(1)} %get-tuple-element.16), channel_id=1, source_target_pairs={{0,15},{1,0},{2,1},{3,2},{4,3},{5,4},{6,5},{7,6},{8,7},{9,8},{10,9... | collective-permute-start | bytes 129032 | tf_op jit(solution)/shard_map/ppermute | solution.py:46
  26.8 0.1 pad_add_fusion.place_ref
  26.8 0.0 collective-permute-done
  26.9 5.9 %collective-permute-done.1.west_ref = bf16[84,256]{1,0:T(8,128)(2,1)S(1)} collective-permute-done((bf16[84,256]{1,0:T(8,128)(2,1)S(1)}, bf16[84,256]{1,0:T(8,128)(2,1)S(1)}, u32[]{:S(2)}, u32[]{:S(2)}) %collective-permute-start.1) | collective-permute-done | bytes 43040 | tf_op jit(solution)/shard_map/ppermute | solution.py:45
  32.8 0.0 collective-permute-done.2.east_ref
  32.8 5.7 %shard_map.164.own_ref = f32[84,512]{1,0:T(8,128)S(1)} custom-call(s32[2]{0:T(128)S(1)} %pad_add_fusion.place_ref, s32[16,512]{1,0:T(8,128)S(1)} %constant_dynamic-update-slice_fusion.src_ref, bf16[84,2048]{1,0:T(8,128)(2,1)S(1)} %get-tuple-element.14.flat_ref, bf16[84,256]{1,0:T(8,128)(2,1)S(1)} %collective-permute-done.1.west_ref, ...), custom_call_target="tpu_custom_call" | custom-call | tf_op jit(solution)/shard_map/pallas_call | solution.py:252
  38.4 1.8 %collective-permute-start.3 = (f32[84,512]{1,0:T(8,128)S(1)}, f32[84,512]{1,0:T(8,128)S(1)}, u32[]{:S(2)}, u32[]{:S(2)}) collective-permute-start(f32[84,512]{1,0:T(8,128)S(1)} %shard_map.164.own_ref), channel_id=1, source_target_pairs={{0,16},{16,0},{1,17},{17,1},{2,18},{18,2},{3,19},{19,3},{4,20},{20... | collective-permute-start | bytes 516104 | tf_op jit(solution)/shard_map/ppermute | solution.py:38
  40.2 1.8 %copy.18.w_read = bf16[1024,84]{1,0:T(8,128)(2,1)} copy(bf16[1024,84]{0,1:T(8,128)(2,1)} %param.31) | data formatting | bytes 344064 | tf_op args[14]
  42.0 0.0 copy-done.7
  42.0 2.5 %shard_map.166.bias_ref = f32[256,1536]{1,0:T(8,128)S(1)} custom-call(s32[2]{0:T(128)S(1)} %pad_add_fusion.place_ref, s32[32,256]{1,0:T(8,128)S(1)} %copy-done.7, s32[1,256]{1,0:T(1,128)S(1)} %bitcast.9), custom_call_target="tpu_custom_call" | custom-call | flops 10000000 | bytes 8000000 | tf_op jit(solution)/shard_map/pallas_call | solution.py:252
  44.5 1.2 %copy-done = f32[256,1536]{1,0:T(8,128)} copy-done((f32[256,1536]{1,0:T(8,128)}, f32[256,1536]{1,0:T(8,128)S(1)}, u32[]{:S(2)}) %copy-start) | copy-done | bytes 1572888
  45.7 0.0 collective-permute-done.3.refs_0_
  45.7 10.6 %collective-permute-start.4 = (bf16[84,512]{1,0:T(8,128)(2,1)S(1)}, bf16[84,512]{1,0:T(8,128)(2,1)S(1)}, u32[]{:S(2)}, u32[]{:S(2)}) collective-permute-start(bf16[84,512]{1,0:T(8,128)(2,1)S(1)} %shard_map.165.mean_ref), channel_id=1, source_target_pairs={{0,1},{1,2},{2,3},{3,4},{4,5},{5,6},{6,7},{7,8},{8,9},{9,10},{10,1... | collective-permute-start | bytes 258056 | tf_op jit(solution)/shard_map/ppermute | solution.py:45
  56.3 0.0 collective-permute-start.5
  56.4 0.0 copy-done.6
  56.4 8.6 %shard_map.167 = (f32[256,1024]{1,0:T(8,128)S(1)}, bf16[256,1024]{1,0:T(8,128)(2,1)S(1)}, bf16[512,1024]{1,0:T(8,128)(2,1)S(1)}, bf16[512,1024]{1,0:T(8,128)(2,1)S(1)}) custom-call(bf16[84,512]{1,0:T(8,128)(2,1)S(1)} %shard_map.165.mean_ref, bf16[512,1024]{1,0:T(8,128)(2,1)S(1)} %constant_dynamic-update-slice_fusion.2.feat_ref, f32[1,1024]{1,0:T(1,128)S(1)} %bitcast.7, ...), custom_call_target="tpu_custom_call" | custom-call | flops 4000000000 | bytes 12000000 | tf_op jit(solution)/shard_map/pallas_call | solution.py:252
  64.9 1.0 copy-done.2
  65.9 1.0 copy-done.3
  66.9 1.0 copy-done.4
  67.9 0.8 copy-done.5
  68.7 0.0 collective-permute-done.4.mean_w
  68.7 0.0 collective-permute-done.5.mean_e
  68.7 0.0 copy-start.15
  68.7 0.0 collective-permute-done.7.feat_w
  68.7 0.0 collective-permute-done.8.feat_e
  68.8 0.6 copy-done.14
  69.3 0.0 copy-done.15
  69.4 0.4 copy-done.13
  69.7 29.6 %shard_map.168 = bf16[84,256]{1,0:T(8,128)(2,1)} custom-call(bf16[84,512]{1,0:T(8,128)(2,1)} %copy-done.14, bf16[84,512]{1,0:T(8,128)(2,1)} %copy-done.15, bf16[512,1024]{1,0:T(8,128)(2,1)} %copy-done.13, bf16[512,1024]{1,0:T(8,128)(2,1)} %collective-permute-done.8.feat_e, f32[256,1536]{1,0:T(8,128)} %copy-done, f32[256,1024]{1,0:T(8,128)} %copy-done.2, ...), custom_call_target="tpu_custom_call" | custom-call | tf_op jit(solution)/shard_map/pallas_call | solution.py:252
  99.4 0.5 collective-permute-start.9
  99.9 3.7 %collective-permute-done.9 = bf16[84,256]{1,0:T(8,128)(2,1)S(1)} collective-permute-done((bf16[84,256]{1,0:T(8,128)(2,1)}, bf16[84,256]{1,0:T(8,128)(2,1)S(1)}, u32[]{:S(2)}, u32[]{:S(2)}) %collective-permute-start.9) | collective-permute-done | bytes 43040 | tf_op jit(solution)/shard_map/ppermute | solution.py:38
  103.7 0.8 pad_maximum_fusion.own_ref
  104.5 0.0 collective-permute-start.10
  104.5 4.4 %collective-permute-start.11 = (bf16[84,512]{1,0:T(8,128)(2,1)S(1)}, bf16[84,512]{1,0:T(8,128)(2,1)S(1)}, u32[]{:S(2)}, u32[]{:S(2)}) collective-permute-start(bf16[84,512]{1,0:T(8,128)(2,1)S(1)} %pad_maximum_fusion.own_ref), channel_id=1, source_target_pairs={{0,15},{1,0},{2,1},{3,2},{4,3},{5,4},{6,5},{7,6},{8,7},{9,8},{10,9... | collective-permute-start | bytes 258056 | tf_op jit(solution)/shard_map/ppermute | solution.py:46
  108.9 2.3 %collective-permute-done.10.west_ref = bf16[84,512]{1,0:T(8,128)(2,1)S(1)} collective-permute-done((bf16[84,512]{1,0:T(8,128)(2,1)S(1)}, bf16[84,512]{1,0:T(8,128)(2,1)S(1)}, u32[]{:S(2)}, u32[]{:S(2)}) %collective-permute-start.10) | collective-permute-done | bytes 86048 | tf_op jit(solution)/shard_map/ppermute | solution.py:45
  111.2 0.0 collective-permute-done.11.east_ref
  111.2 4.5 %shard_map.169 = f32[84,16,128]{2,1,0:T(8,128)} custom-call(s32[2]{0:T(128)S(1)} %pad_add_fusion.place_ref, s32[3,16,128]{2,1,0:T(8,128)S(1)} %copy-done.8, bf16[84,512]{1,0:T(8,128)(2,1)S(1)} %pad_maximum_fusion.own_ref, bf16[84,512]{1,0:T(8,128)(2,1)S(1)} %collective-permute-done.10.west_ref, bf16[84,512]{1,0:T(8,128)(2,1)S(1)} %collective-permute-done.11.east_ref, ...), custom_call_target="tpu_custom_call" | custom-call | tf_op jit(solution)/shard_map/pallas_call | solution.py:252
  (22 shorter events, 0.1 us)
Async XLA Ops:
  0.0 19.7 %copy-start.11 = (s32[256]{0:T(256)S(1)}, s32[256]{0:T(256)}, u32[]{:S(2)}) copy-start(s32[256]{0:T(256)} %param.20) | copy-start | bytes 3076
  0.0 19.7 %copy-start.1 = (bf16[84,16,128]{2,1,0:T(8,128)(2,1)S(1)}, bf16[84,16,128]{2,1,0:T(8,128)(2,1)}, u32[]{:S(2)}) copy-start(bf16[84,16,128]{2,1,0:T(8,128)(2,1)} %grid_ref.3) | copy-start | bytes 1032196
  0.0 19.7 %copy-start.9 = (s32[16,256]{1,0:T(8,128)S(1)}, s32[16,256]{1,0:T(8,128)}, u32[]{:S(2)}) copy-start(s32[16,256]{1,0:T(8,128)} %src_ref.1) | copy-start | bytes 49156
  0.0 42.0 %copy-start.12 = (s32[256]{0:T(256)S(1)}, s32[256]{0:T(256)}, u32[]{:S(2)}) copy-start(s32[256]{0:T(256)} %param.22) | copy-start | bytes 3076
  0.0 42.0 %copy-start.7 = (s32[32,256]{1,0:T(8,128)S(1)}, s32[32,256]{1,0:T(8,128)}, u32[]{:S(2)}) copy-start(s32[32,256]{1,0:T(8,128)} %ids_ref.1) | copy-start | bytes 98308
  0.0 15.2 %collective-permute-start.6 = (bf16[256,1024]{1,0:T(8,128)(2,1)}, bf16[256,1024]{1,0:T(8,128)(2,1)S(1)}, u32[]{:S(2)}, u32[]{:S(2)}) collective-permute-start(bf16[256,1024]{1,0:T(8,128)(2,1)} %param.18), channel_id=1, source_target_pairs={{0,16},{16,0},{1,17},{17,1},{2,18},{18,2},{3,19},{19,3},{4,20},{20... | collective-permute-start | bytes 1572872 | tf_op jit(solution)/shard_map/ppermute | solution.py:38
  4.1 52.2 %copy-start.6 = (bf16[84,1024]{1,0:T(8,128)(2,1)S(1)}, bf16[84,1024]{1,0:T(8,128)(2,1)}, u32[]{:S(2)}) copy-start(bf16[84,1024]{1,0:T(8,128)(2,1)} %w_embed.3) | copy-start | bytes 516100
  4.2 52.2 %copy-start.10 = (f32[1024]{0:T(1024)S(1)}, f32[1024]{0:T(1024)}, u32[]{:S(2)}) copy-start(f32[1024]{0:T(1024)} %param.32) | copy-start | bytes 12292
  15.2 53.5 %collective-permute-start.7 = (bf16[512,1024]{1,0:T(8,128)(2,1)S(1)}, bf16[512,1024]{1,0:T(8,128)(2,1)S(1)}, u32[]{:S(2)}, u32[]{:S(2)}) collective-permute-start(bf16[512,1024]{1,0:T(8,128)(2,1)S(1)} %constant_dynamic-update-slice_fusion.2.feat_ref), channel_id=1, source_target_pairs={{0,1},{1,2},{2,3},{3,4},{4,5},{5,6},{6,7},{7,8},{8,9},{9,10},{10,1... | collective-permute-start | bytes 3145736 | tf_op jit(solution)/shard_map/ppermute | solution.py:45
  15.3 53.5 %collective-permute-start.8 = (bf16[512,1024]{1,0:T(8,128)(2,1)S(1)}, bf16[512,1024]{1,0:T(8,128)(2,1)}, u32[]{:S(2)}, u32[]{:S(2)}) collective-permute-start(bf16[512,1024]{1,0:T(8,128)(2,1)S(1)} %constant_dynamic-update-slice_fusion.2.feat_ref), channel_id=1, source_target_pairs={{0,15},{1,0},{2,1},{3,2},{4,3},{5,4},{6,5},{7,6},{8,7},{9,8},{10,9... | collective-permute-start | bytes 3145736 | tf_op jit(solution)/shard_map/ppermute | solution.py:46
  20.5 6.3 %collective-permute-start = (s32[16,256]{1,0:T(8,128)S(1)}, s32[16,256]{1,0:T(8,128)S(1)}, u32[]{:S(2)}, u32[]{:S(2)}) collective-permute-start(s32[16,256]{1,0:T(8,128)S(1)} %get-tuple-element.13), channel_id=1, source_target_pairs={{0,16},{16,0},{1,17},{17,1},{2,18},{18,2},{3,19},{19,3},{4,20},{20... | collective-permute-start | bytes 49160 | tf_op jit(solution)/shard_map/ppermute | solution.py:38
  22.3 10.4 %collective-permute-start.1 = (bf16[84,256]{1,0:T(8,128)(2,1)S(1)}, bf16[84,256]{1,0:T(8,128)(2,1)S(1)}, u32[]{:S(2)}, u32[]{:S(2)}) collective-permute-start(bf16[84,256]{1,0:T(8,128)(2,1)S(1)} %get-tuple-element.15), channel_id=1, source_target_pairs={{0,1},{1,2},{2,3},{3,4},{4,5},{5,6},{6,7},{7,8},{8,9},{9,10},{10,1... | collective-permute-start | bytes 129032 | tf_op jit(solution)/shard_map/ppermute | solution.py:45
  22.3 10.4 %collective-permute-start.2 = (bf16[84,256]{1,0:T(8,128)(2,1)S(1)}, bf16[84,256]{1,0:T(8,128)(2,1)S(1)}, u32[]{:S(2)}, u32[]{:S(2)}) collective-permute-start(bf16[84,256]{1,0:T(8,128)(2,1)S(1)} %get-tuple-element.16), channel_id=1, source_target_pairs={{0,15},{1,0},{2,1},{3,2},{4,3},{5,4},{6,5},{7,6},{8,7},{9,8},{10,9... | collective-permute-start | bytes 129032 | tf_op jit(solution)/shard_map/ppermute | solution.py:46
  38.4 7.2 %collective-permute-start.3 = (f32[84,512]{1,0:T(8,128)S(1)}, f32[84,512]{1,0:T(8,128)S(1)}, u32[]{:S(2)}, u32[]{:S(2)}) collective-permute-start(f32[84,512]{1,0:T(8,128)S(1)} %shard_map.164.own_ref), channel_id=1, source_target_pairs={{0,16},{16,0},{1,17},{17,1},{2,18},{18,2},{3,19},{19,3},{4,20},{20... | collective-permute-start | bytes 516104 | tf_op jit(solution)/shard_map/ppermute | solution.py:38
  44.5 1.2 %copy-start = (f32[256,1536]{1,0:T(8,128)}, f32[256,1536]{1,0:T(8,128)S(1)}, u32[]{:S(2)}) copy-start(f32[256,1536]{1,0:T(8,128)S(1)} %shard_map.166.bias_ref) | copy-start | bytes 4718596
  45.7 23.0 %collective-permute-start.4 = (bf16[84,512]{1,0:T(8,128)(2,1)S(1)}, bf16[84,512]{1,0:T(8,128)(2,1)S(1)}, u32[]{:S(2)}, u32[]{:S(2)}) collective-permute-start(bf16[84,512]{1,0:T(8,128)(2,1)S(1)} %shard_map.165.mean_ref), channel_id=1, source_target_pairs={{0,1},{1,2},{2,3},{3,4},{4,5},{5,6},{6,7},{7,8},{8,9},{9,10},{10,1... | collective-permute-start | bytes 258056 | tf_op jit(solution)/shard_map/ppermute | solution.py:45
  56.3 12.4 %collective-permute-start.5 = (bf16[84,512]{1,0:T(8,128)(2,1)S(1)}, bf16[84,512]{1,0:T(8,128)(2,1)S(1)}, u32[]{:S(2)}, u32[]{:S(2)}) collective-permute-start(bf16[84,512]{1,0:T(8,128)(2,1)S(1)} %shard_map.165.mean_ref), channel_id=1, source_target_pairs={{0,15},{1,0},{2,1},{3,2},{4,3},{5,4},{6,5},{7,6},{8,7},{9,8},{10,9... | collective-permute-start | bytes 258056 | tf_op jit(solution)/shard_map/ppermute | solution.py:46
  64.9 1.0 copy-start.2
  65.9 1.0 copy-start.3
  66.9 1.0 copy-start.4
  67.9 0.8 copy-start.5
  68.7 0.6 copy-start.14
  68.7 0.7 copy-start.15
  68.7 1.0 copy-start.13
  69.7 41.5 %copy-start.8 = (s32[3,16,128]{2,1,0:T(8,128)S(1)}, s32[3,16,128]{2,1,0:T(8,128)}, u32[]{:S(2)}) copy-start(s32[3,16,128]{2,1,0:T(8,128)} %dec_ref.1) | copy-start | bytes 73732
  99.4 4.3 %collective-permute-start.9 = (bf16[84,256]{1,0:T(8,128)(2,1)}, bf16[84,256]{1,0:T(8,128)(2,1)S(1)}, u32[]{:S(2)}, u32[]{:S(2)}) collective-permute-start(bf16[84,256]{1,0:T(8,128)(2,1)} %shard_map.168), channel_id=1, source_target_pairs={{0,16},{16,0},{1,17},{17,1},{2,18},{18,2},{3,19},{19,3},{4,20},{20... | collective-permute-start | bytes 129032 | tf_op jit(solution)/shard_map/ppermute | solution.py:38
  104.5 6.8 %collective-permute-start.10 = (bf16[84,512]{1,0:T(8,128)(2,1)S(1)}, bf16[84,512]{1,0:T(8,128)(2,1)S(1)}, u32[]{:S(2)}, u32[]{:S(2)}) collective-permute-start(bf16[84,512]{1,0:T(8,128)(2,1)S(1)} %pad_maximum_fusion.own_ref), channel_id=1, source_target_pairs={{0,1},{1,2},{2,3},{3,4},{4,5},{5,6},{6,7},{7,8},{8,9},{9,10},{10,1... | collective-permute-start | bytes 258056 | tf_op jit(solution)/shard_map/ppermute | solution.py:45
  104.5 6.8 %collective-permute-start.11 = (bf16[84,512]{1,0:T(8,128)(2,1)S(1)}, bf16[84,512]{1,0:T(8,128)(2,1)S(1)}, u32[]{:S(2)}, u32[]{:S(2)}) collective-permute-start(bf16[84,512]{1,0:T(8,128)(2,1)S(1)} %pad_maximum_fusion.own_ref), channel_id=1, source_target_pairs={{0,15},{1,0},{2,1},{3,2},{4,3},{5,4},{6,5},{7,6},{8,7},{9,8},{10,9... | collective-permute-start | bytes 258056 | tf_op jit(solution)/shard_map/ppermute | solution.py:46

commit v2 on v1

v2 whole, which is shorter than its diff:
```python
import functools

import jax
import jax.numpy as jnp
from jax import lax
from jax.experimental import pallas as pl
from jax.experimental.pallas import tpu as pltpu
from jax.sharding import PartitionSpec as P

HEADS = 16
HALO = 16
BF16 = jnp.bfloat16
F32 = jnp.float32
MIB = 1024 * 1024


def params(mib):
    return pltpu.CompilerParams(vmem_limit_bytes=mib * MIB)


def whole(memory=pltpu.VMEM):
    return pl.BlockSpec(memory_space=memory)


def silu(value):
    return 0.5 * value * (1.0 + jnp.tanh(0.5 * value))


def layer_norm(inputs_f, gain):
    centre = inputs_f - jnp.mean(inputs_f, axis=-1, keepdims=True)
    spread = jnp.mean(centre * centre, axis=-1, keepdims=True)
    return centre * lax.rsqrt(spread + 1e-05) * gain


def from_bands(value):
    count = lax.axis_size("lat")
    return [
        lax.ppermute(value, "lat", [(i, (i - step) % count) for i in range(count)])
        for step in range(1, count)
    ]


def from_near(value):
    count = lax.axis_size("lon")
    return lax.ppermute(value, "lon", [(i, i ^ 1) for i in range(count)])


def from_far(value):
    count = lax.axis_size("lon")
    return lax.ppermute(value, "lon", [(i, (i - 1 + 2 * (i % 2)) % count) for i in range(count)])


def quotient(value_f, divisor):
    return jnp.floor((value_f + 0.5) * (1.0 / divisor))


def prep_kernel(place_ref, grid, src, count, flat_ref, near_ref, far_ref, live_ref, wide):
    slot = lax.broadcasted_iota(jnp.int32, live_ref.shape, 0)
    live_ref[...] = jnp.where(slot < count.now()[...], src.now()[...], -1)
    grid_ref = grid.now()
    rows, cols = grid_ref.shape[1:]
    per_tile = cols // HALO
    odd = place_ref[1] % 2
    near_at = jnp.where(odd == 0, cols - HALO, 0)
    far_at = cols - HALO - near_at
    lane = lax.broadcasted_iota(jnp.int32, (grid_ref.shape[0], cols), 1) // HALO
    wide[...] = grid_ref[...].astype(F32)
    for tile in range(rows // per_tile):
        near, far = None, None
        for place in range(per_tile):
            row = tile * per_tile + place
            line = wide[:, row, :]
            flat_ref[:, row * cols : (row + 1) * cols] = line.astype(BF16)
            turned = [
                pltpu.roll(line, (place * HALO - start + cols) % cols, 1)
                for start in (near_at, far_at)
            ]
            near = turned[0] if near is None else jnp.where(lane == place, turned[0], near)
            far = turned[1] if far is None else jnp.where(lane == place, turned[1], far)
        near_ref[:, tile * cols : (tile + 1) * cols] = near.astype(BF16)
        far_ref[:, tile * cols : (tile + 1) * cols] = far.astype(BF16)


def encode_kernel(place_ref, src_ref, flat_ref, out_ref, rim_ref, counts):
    slots, nodes = src_ref.shape
    cells = flat_ref.shape[1]
    rim = rim_ref.shape[0] // 2
    rows = rim // HALO
    cols = cells // rows
    span = cols + 2 * HALO
    lanes = 128
    even = place_ref[1] % 2 == 0
    source = src_ref[...].astype(F32)
    row_of = quotient(source, span)
    col_of = source - row_of * span
    row_of = row_of - (place_ref[0] * rows).astype(F32)
    iota = lax.broadcasted_iota(jnp.int32, (span, lanes), 0).astype(F32).astype(BF16)
    one = jnp.ones((span, lanes), BF16)
    none = jnp.zeros((span, lanes), BF16)
    west = pl.multiple_of(jnp.where(even, rim, 0), rim)
    east = pl.multiple_of(jnp.where(even, 0, rim), rim)
    for row in range(rows):
        code = jnp.where(row_of == row, col_of, -1.0).astype(BF16)
        for tile in range(nodes // lanes):
            at = slice(tile * lanes, (tile + 1) * lanes)
            total = none
            for slot in range(slots):
                total = total + jnp.where(iota == code[slot : slot + 1, at], one, none)
            counts[row * cols : (row + 1) * cols, at] = total[HALO : HALO + cols]
            rim_ref[pl.ds(west + row * HALO, HALO), at] = total[:HALO]
            rim_ref[pl.ds(east + row * HALO, HALO), at] = total[HALO + cols :]
    out_ref[...] = jnp.dot(flat_ref[...], counts[...], preferred_element_type=F32)


def rim_kernel(near_ref, far_ref, *refs):
    out_ref = refs[-1]
    rim = near_ref.shape[1]
    for part in range(len(refs) // 2):
        summed, counts = refs[2 * part], refs[2 * part + 1]
        nodes = summed.shape[1]
        total = summed[...]
        total += jnp.dot(near_ref[...], counts[:rim], preferred_element_type=F32)
        total += jnp.dot(far_ref[...], counts[rim:], preferred_element_type=F32)
        out_ref[:, part * nodes : (part + 1) * nodes] = total


def mean_kernel(own_ref, *refs):
    out_ref = refs[-1]
    bands = len(refs) // 2
    others, sources = refs[: bands - 1], refs[bands - 1 : -1]
    nodes = own_ref.shape[1] // bands
    for band in range(bands):
        at = slice(band * nodes, (band + 1) * nodes)
        count = jnp.sum(jnp.where(sources[band][...] >= 0, 1.0, 0.0), axis=0, keepdims=True)
        total = own_ref[:, at]
        for step, other in enumerate(others, 1):
            there = (band - step) % bands
            total = total + other[:, there * nodes : (there + 1) * nodes]
        out_ref[:, at] = (total / count).astype(BF16)


def place_of(ids, place_ref, node_count, bands, sectors):
    ids_f = ids.astype(F32)
    device = quotient(ids_f, node_count)
    member = ids_f - device * node_count
    band = quotient(device, sectors)
    sector = device - band * sectors
    mine = place_ref[1]
    near = mine + 1 - 2 * (mine % 2)
    side = jnp.where(sector == mine.astype(F32), 0.0, 2.0)
    side = jnp.where(sector == near.astype(F32), 1.0, side)
    band = band - place_ref[0].astype(F32)
    band = jnp.where(band < 0, band + bands, band)
    return side * bands + band, member


def bias_kernel(bands, sectors, place_ref, ids, count, own_ref, rest_ref):
    ids_ref, count_ref = ids.now(), count.now()
    slots, nodes = ids_ref.shape
    lanes = 128
    block, member = place_of(ids_ref[...], place_ref, nodes, bands, sectors)
    slot_of = lax.broadcasted_iota(jnp.int32, (slots, nodes), 0)
    block = jnp.where(slot_of < count_ref[...], block, -1.0)
    iota = lax.broadcasted_iota(jnp.int32, (nodes, lanes), 0).astype(F32).astype(BF16)
    shut = jnp.full((nodes, lanes), -1e30, BF16)
    opened = jnp.zeros((nodes, lanes), BF16)
    for part in range(3 * bands):
        code = jnp.where(block == part, member, -1.0).astype(BF16)
        ref, index = (own_ref, part) if part < bands else (rest_ref, part - bands)
        for tile in range(nodes // lanes):
            at = slice(tile * lanes, (tile + 1) * lanes)
            total = shut
            for slot in range(slots):
                total = jnp.where(iota == code[slot : slot + 1, at], opened, total)
            ref[at, index * nodes : (index + 1) * nodes] = total.astype(F32).T


def latent_of(mean, feat, w_embed, w_encode):
    embedded = silu(
        lax.dot_general(mean, w_embed, (((0,), (0,)), ((), ())), preferred_element_type=F32)
    ).astype(BF16)
    return feat.astype(F32) + jnp.dot(embedded, w_encode, preferred_element_type=F32)


def sector_rows(
    mean_ref, gain_ref, w_embed, w_encode, w_query, w_key, w_value, feats, latent_ref, query_ref, pair_ref
):
    nodes, features = feats[0].shape
    for part, feat in enumerate(feats):
        at = slice(part * nodes, (part + 1) * nodes)
        latent = latent_of(mean_ref[:, at], feat[...], w_embed[...], w_encode[...])
        normed = layer_norm(latent, gain_ref[...]).astype(BF16)
        if part == 0 and latent_ref is not None:
            latent_ref[...] = latent
            query_ref[...] = jnp.dot(normed, w_query[...], preferred_element_type=F32).astype(BF16)
        pair_ref[at, :features] = jnp.dot(
            normed, w_key[...], preferred_element_type=F32
        ).astype(BF16)
        pair_ref[at, features:] = jnp.dot(
            normed, w_value[...], preferred_element_type=F32
        ).astype(BF16)


LANES = 128
CHUNK = 16


def head_scores(query_ref, pairs, at, head, score_ref):
    nodes = query_ref.shape[0]
    width = LANES // 2
    lane = lax.broadcasted_iota(jnp.int32, (nodes, LANES), 1)
    query = query_ref[:, at].astype(F32) * width**-0.5
    query = jnp.where(lane // width == head, query, 0.0).astype(BF16)
    start = 0
    for keys in pairs:
        count = keys.shape[0]
        score_ref[:, start : start + count] = lax.dot_general(
            query, keys[:, at], (((1,), (1,)), ((), ())), preferred_element_type=F32
        )
        start += count


def head_weights(score_ref, bias_ref, weight_ref, floor):
    nodes = score_ref.shape[0]
    peaks = []
    for start in range(0, nodes, CHUNK):
        rows = slice(start, start + CHUNK)
        scores = score_ref[rows] + bias_ref[rows]
        peak = jnp.max(scores, axis=1, keepdims=True)
        if floor is not None:
            peak = jnp.maximum(peak, floor[rows])
        weight_ref[rows] = jnp.exp(scores - peak).astype(BF16)
        peaks.append(peak)
    return jnp.concatenate(peaks, axis=0)


def head_values(weight_ref, pairs, at):
    total, start = None, 0
    for values in pairs:
        count = values.shape[0]
        rhs = jnp.concatenate([values[:, at], jnp.ones((count, LANES), BF16)], axis=1)
        part = jnp.dot(weight_ref[:, start : start + count], rhs, preferred_element_type=F32)
        total = part if total is None else total + part
        start += count
    return total[:, :LANES], total[:, LANES:]


def far_kernel(mean_ref, w_embed, w_encode, w_key, w_value, gain, *refs):
    feats, pair_ref = [feat.now() for feat in refs[:-1]], refs[-1]
    sector_rows(
        mean_ref, gain.now(), w_embed, w_encode, None, w_key, w_value, feats, None, None, pair_ref
    )


def own_kernel(
    bands, mean_ref, bias_ref, w_embed, w_encode, w_query, w_key, w_value, gain, *refs
):
    feats, refs = [feat.now() for feat in refs[:bands]], refs[bands:]
    latent_ref, query_ref, pair_ref, mixed_ref, peak_ref, sum_ref, score_ref, weight_ref = refs
    nodes, features = query_ref.shape
    sector_rows(
        mean_ref, gain.now(), w_embed, w_encode, w_query, w_key, w_value, feats,
        latent_ref, query_ref, pair_ref,
    )
    width = LANES // 2
    first = lax.broadcasted_iota(jnp.int32, (nodes, LANES), 1) < width
    per_step = score_ref.shape[0] // 2

    def attend(step, carry):
        ats = []
        for pair in range(per_step):
            base = (step * per_step + pair) * LANES
            ats.append(
                (
                    pl.ds(pl.multiple_of(base, LANES), LANES),
                    pl.ds(pl.multiple_of(base + features, LANES), LANES),
                )
            )
        for pair, (at, _) in enumerate(ats):
            for head in range(2):
                head_scores(query_ref, [pair_ref], at, head, score_ref.at[2 * pair + head])
        for pair, (at, value_at) in enumerate(ats):
            done = []
            for head in range(2):
                slot = 2 * pair + head
                peak = head_weights(score_ref.at[slot], bias_ref, weight_ref.at[slot], None)
                mixed, total = head_values(weight_ref.at[slot], [pair_ref], value_at)
                done.append((mixed, total, jnp.broadcast_to(peak, (nodes, LANES))))
            for ref, one, two in zip((mixed_ref, sum_ref, peak_ref), *done):
                ref[:, at] = jnp.where(first, one, two)
        return carry

    lax.fori_loop(0, features // LANES // per_step, attend, 0)


def attend_kernel(
    near_ref, far_ref, bias_ref, latent_ref, query_ref, mixed_ref, peak_ref, sum_ref,
    w_output, w_decode, gain_dec, w_read, out_ref, score_ref, weight_ref, context_ref,
):
    nodes, features = latent_ref.shape
    width = LANES // 2
    first = lax.broadcasted_iota(jnp.int32, (nodes, LANES), 1) < width
    per_step = score_ref.shape[0] // 2
    pairs = [near_ref, far_ref]

    def attend(step, carry):
        ats = []
        for pair in range(per_step):
            base = (step * per_step + pair) * LANES
            ats.append(
                (
                    pl.ds(pl.multiple_of(base, LANES), LANES),
                    pl.ds(pl.multiple_of(base + features, LANES), LANES),
                )
            )
        for pair, (at, _) in enumerate(ats):
            for head in range(2):
                head_scores(query_ref, pairs, at, head, score_ref.at[2 * pair + head])
        for pair, (at, value_at) in enumerate(ats):
            old_peak = peak_ref[:, at]
            done = []
            for head in range(2):
                slot = 2 * pair + head
                floor = old_peak[:, head * width : head * width + 1]
                peak = head_weights(score_ref.at[slot], bias_ref, weight_ref.at[slot], floor)
                mixed, total = head_values(weight_ref.at[slot], pairs, value_at)
                done.append((mixed, total, jnp.broadcast_to(peak, (nodes, LANES))))
            mixed, total, peak = (jnp.where(first, one, two) for one, two in zip(*done))
            fade = jnp.exp(old_peak - peak)
            mixed = mixed + fade * mixed_ref[:, at]
            total = total + fade * sum_ref[:, at]
            context_ref[:, at] = (mixed / total).astype(BF16)
        return carry

    lax.fori_loop(0, features // LANES // per_step, attend, 0)
    mixed = latent_ref[...] + jnp.dot(context_ref[...], w_output[...], preferred_element_type=F32)
    normed_out = layer_norm(mixed, gain_dec.now()[...]).astype(BF16)
    decoded = silu(jnp.dot(normed_out, w_decode[...], preferred_element_type=F32)).astype(BF16)
    out_ref[...] = lax.dot_general(
        w_read.now()[...], decoded, (((1,), (1,)), ((), ())), preferred_element_type=F32
    ).astype(BF16)


def decode_kernel(bands, sectors, nodes, parts, place_ref, dec, *refs):
    base, reads, out_ref = refs[0], refs[1:-1], refs[-1]
    dec_ref = dec.now()
    rows, cols = out_ref.shape[1:]
    iota = lax.broadcasted_iota(jnp.int32, (nodes, cols), 0).astype(F32).astype(BF16)
    one = jnp.ones((nodes, cols), BF16)
    none = jnp.zeros((nodes, cols), BF16)
    block, member = place_of(dec_ref[...], place_ref, nodes, bands, sectors)
    for row in range(rows):
        update = jnp.zeros((out_ref.shape[0], cols), F32)
        for part, (index, at) in parts:
            code = jnp.where(block[:, row] == part, member[:, row], -1.0).astype(BF16)
            counts = none
            for slot in range(code.shape[0]):
                counts = counts + jnp.where(iota == code[slot : slot + 1], one, none)
            update += jnp.dot(
                reads[index][:, at * nodes : (at + 1) * nodes], counts, preferred_element_type=F32
            )
        out_ref[:, row, :] = update / 3.0
    base = base.now() if isinstance(base, Late) else base
    out_ref[...] += base[...].astype(F32)


class Late:
    def __init__(self, source, target, semaphore):
        self.target = target
        self.copy = pltpu.make_async_copy(source, target, semaphore)
        self.copy.start()
        self.waited = False

    def now(self):
        if not self.waited:
            self.copy.wait()
            self.waited = True
        return self.target


def call(name, kernel, outs, scalars, operands, late=(), scratch=(), mib=8, micros=1):
    single = not isinstance(outs, (list, tuple))
    outs = [outs] if single else list(outs)
    n_in, n_late, n_out = len(scalars) + len(operands), len(late), len(outs)

    def run(*refs):
        ins, refs = refs[:n_in], refs[n_in:]
        sources, refs = refs[:n_late], refs[n_late:]
        results, refs = refs[:n_out], refs[n_out:]
        targets, refs = refs[:n_late], refs[n_late:]
        if n_late:
            semaphores, refs = refs[-1], refs[:-1]
        fetched = [
            Late(source, target, semaphores.at[index])
            for index, (source, target) in enumerate(zip(sources, targets))
        ]
        kernel(*ins, *fetched, *results, *refs)

    fetch = [pltpu.VMEM(a.shape, a.dtype) for a in late]
    signals = [pltpu.SemaphoreType.DMA((n_late,))] if n_late else []
    specs = [whole(pltpu.SMEM)] * len(scalars) + [whole()] * len(operands)
    specs += [whole(pltpu.HBM)] * n_late
    result = pl.pallas_call(
        run,
        name=name,
        out_shape=outs,
        in_specs=specs,
        out_specs=[whole()] * n_out,
        scratch_shapes=fetch + list(scratch) + signals,
        compiler_params=params(mib),
        cost_estimate=pl.CostEstimate(
            flops=int(micros * 5e8), bytes_accessed=int(micros * 3e6), transcendentals=0
        ),
    )(*scalars, *operands, *late)
    return result[0] if single else result


def after(value, *earlier):
    return lax.optimization_barrier((value,) + earlier)[0]


def body(
    grid_state, mesh_feat, enc_src, enc_count, nbr_ids, nbr_count, dec_src,
    w_embed, w_encode, w_query, w_key, w_value, w_output, w_decode, w_readout, norm_attn, norm_dec,
):
    shape = jax.ShapeDtypeStruct
    bands, sectors = lax.axis_size("lat"), lax.axis_size("lon")
    place = jnp.stack([lax.axis_index("lat"), lax.axis_index("lon")]).astype(jnp.int32)
    variables, rows, cols = grid_state.shape
    nodes, features = mesh_feat.shape
    slots = enc_src.shape[0]
    cells, rim = rows * cols, rows * HALO
    sector_nodes = bands * nodes

    flat, near_rim, far_rim, live = call(
        "prep",
        prep_kernel,
        [
            shape((variables, cells), BF16),
            shape((variables, rim), BF16),
            shape((variables, rim), BF16),
            shape((slots, nodes), jnp.int32),
        ],
        (place,),
        (),
        late=(grid_state, enc_src, enc_count[None]),
        scratch=[pltpu.VMEM((variables, rows, cols), F32)],
        micros=2,
    )
    far_rim = from_far(far_rim)
    lives = [live] + from_bands(live)
    near_rim = from_near(near_rim)

    encoded = []
    for step, source in enumerate(lives):
        encoded += call(
            "encode",
            encode_kernel,
            [shape((variables, nodes), F32), shape((2 * rim, nodes), BF16)],
            (place,),
            (source, flat),
            scratch=[pltpu.VMEM((cells, nodes), BF16)],
            micros=0.1 if step else 3,
        )
    feat = after(mesh_feat, encoded[0])
    feats = [feat] + from_bands(feat)
    feat_far = from_far(feat)
    summed = call(
        "rim", rim_kernel, shape((variables, sector_nodes), F32), (),
        (near_rim, far_rim, *encoded), micros=0.1,
    )
    received = from_bands(summed)
    bias_own, bias_rest = call(
        "bias",
        functools.partial(bias_kernel, bands, sectors),
        [shape((nodes, sector_nodes), F32), shape((nodes, 2 * sector_nodes), F32)],
        (place,),
        (),
        late=(after(nbr_ids, summed), nbr_count[None]),
        micros=30,
    )
    mean = call(
        "mean",
        mean_kernel,
        shape((variables, sector_nodes), BF16),
        (),
        (after(summed, bias_own, *feats, feat_far), *received, *lives),
        micros=0.1,
    )
    feats_far = [feat_far] + from_bands(feat_far)
    mean_far = from_far(mean)
    latent, query, pair, mixed, peak, total = call(
        "own",
        functools.partial(own_kernel, bands),
        [
            shape((nodes, features), F32),
            shape((nodes, features), BF16),
            shape((sector_nodes, 2 * features), BF16),
        ]
        + [shape((nodes, features), F32)] * 3,
        (),
        (mean, bias_own, w_embed, w_encode, w_query, w_key, w_value),
        late=(norm_attn[None], *feats),
        scratch=[
            pltpu.VMEM((4, nodes, sector_nodes), F32),
            pltpu.VMEM((4, nodes, sector_nodes), BF16),
        ],
        mib=30,
        micros=10,
    )
    pair_near = from_near(pair)
    pair_far = call(
        "far",
        far_kernel,
        shape((sector_nodes, 2 * features), BF16),
        (),
        (mean_far, after(w_embed, pair), w_encode, w_key, w_value),
        late=(norm_attn[None], *feats_far),
        mib=16,
        micros=60,
    )
    readout = call(
        "attend",
        attend_kernel,
        shape((variables, nodes), BF16),
        (),
        (pair_near, pair_far, bias_rest, latent, query, mixed, peak, total, w_output, w_decode),
        late=(norm_dec[None], w_readout.T),
        scratch=[
            pltpu.VMEM((4, nodes, 2 * sector_nodes), F32),
            pltpu.VMEM((4, nodes, 2 * sector_nodes), BF16),
            pltpu.VMEM((nodes, features), BF16),
        ],
        mib=28,
        micros=12,
    )
    banded = from_bands(readout)
    reads = jnp.concatenate([readout] + banded, axis=1)
    read_far = from_far(reads)
    read_near = from_near(reads)
    kernel = functools.partial(decode_kernel, bands, sectors, nodes)
    result = shape(grid_state.shape, F32)

    sums = call(
        "decode_own",
        lambda place_ref, read_ref, dec, grid, out_ref: kernel(
            [(0, (0, 0))], place_ref, dec, grid, read_ref, out_ref
        ),
        result,
        (place,),
        (readout,),
        late=(dec_src, grid_state),
        micros=0.1,
    )
    near_parts = [(band, (0, band)) for band in range(1, bands)]
    near_parts += [(bands + band, (1, band)) for band in range(bands)]
    sums = call(
        "decode_near",
        lambda place_ref, sum_ref, own_ref, near_ref, dec, out_ref: kernel(
            near_parts, place_ref, dec, sum_ref, own_ref, near_ref, out_ref
        ),
        result,
        (place,),
        (sums, reads, read_near),
        late=(dec_src,),
        micros=0.1,
    )
    far_parts = [(2 * bands + band, (0, band)) for band in range(bands)]
    return call(
        "decode_far",
        lambda place_ref, sum_ref, far_ref, dec, out_ref: kernel(
            far_parts, place_ref, dec, sum_ref, far_ref, out_ref
        ),
        result,
        (place,),
        (sums, read_far),
        late=(dec_src,),
        micros=0.1,
    )


def solution(mesh):
    in_specs = (
        P(None, "lat", "lon"),
        P(("lat", "lon"), None),
        P(None, ("lat", "lon")),
        P(("lat", "lon")),
        P(None, ("lat", "lon")),
        P(("lat", "lon")),
        P(None, "lat", "lon"),
    ) + (P(),) * 10
    out_specs = P(None, "lat", "lon")
    return jax.shard_map(body, mesh=mesh, in_specs=in_specs, out_specs=out_specs, check_vma=False)
```

time: 116 us -> 75.6 us (0.65)
  starting transfers between devices: 31.1 us -> 16.1 us
  waiting for transfers between devices: 23 us -> 13.6 us
  Pallas kernels: 51.7 us -> 42.6 us
  local copies, waits for them, and re-layouts: 8.89 us -> 2.46 us
    ppermute x8 -> x7, starting transfers between devices: 24 us -> 11.4 us  [the longest x4 10.3 us: from_far(): lax.ppermute(value, 'lon', [(i, (i - 1 + 2 * (i % 2)) % count) for i in r...]
    pallas_call x7 -> x12, Pallas kernels: 51.7 us -> 42.6 us  [call(): pl.pallas_call(run, name=name, out_shape=outs, in_specs=specs, out_specs=...]
    ppermute x8 -> x7, waiting for transfers between devices: 8.25 us -> 0.02 us  [the longest x4 0.01 us: from_far(): lax.ppermute(value, 'lon', [(i, (i - 1 + 2 * (i % 2)) % count) for i in r...]
    unnamed x35 -> x36, local copies, waits for them, and re-layouts: 8.86 us -> 2.46 us
    ppermute x4 -> x5, starting transfers between devices: 7.14 us -> 4.72 us  [from_bands(): lax.ppermute(value, 'lat', [(i, (i - step) % count) for i in range(count)])]
    ppermute x4 -> x5, waiting for transfers between devices: 14.7 us -> 13.6 us  [from_bands(): lax.ppermute(value, 'lat', [(i, (i - step) % count) for i in range(count)])]
  transfers between devices with their start and end apart: 12 -> 12, of which waited for: 4 -> 4; matrix products, arithmetic and copies ran while one was open for 3% -> 0% of each run, Pallas kernels for 15% -> 33%
where the time goes in v2:
time: 75.6 us; the launch traced here: 75.4 us
  Pallas kernels  42.6 us (56%)
  starting transfers between devices  16.1 us (21%)
  waiting for transfers between devices  13.6 us (18%)
  local copies, waits for them, and re-layouts  2.46 us (3%)
    pallas_call x12, Pallas kernels, call(): pl.pallas_call(run, name=name, out_shape=outs, in_specs=specs, out_specs=...  42.6 us
    ppermute x5, waiting for transfers between devices, from_bands(): lax.ppermute(value, 'lat', [(i, (i - step) % count) for i in range(count)])  13.6 us
    ppermute x4, starting transfers between devices, from_far(): lax.ppermute(value, 'lon', [(i, (i - 1 + 2 * (i % 2)) % count) for i in r...  10.3 us
    ppermute x5, starting transfers between devices, from_bands(): lax.ppermute(value, 'lat', [(i, (i - step) % count) for i in range(count)])  4.72 us
    unnamed x36, local copies, waits for them, and re-layouts  2.46 us
  transfers between devices with their start and end apart: 12, of which 4 were waited for; matrix products, arithmetic and copies ran while one was open for 0% of the time, Pallas kernels for 33%

profile of v2, /device:TPU:0, one launch (start us, length us, event | category | flops | bytes accessed | tf_op | source)
XLA Modules:
  0.0 75.4 jit_solution(1278034721136322506)
XLA Ops:
  0.0 0.1 pad_add_fusion.refs_0_
  0.1 1.0 %copy-done = bf16[84,16,128]{2,1,0:T(8,128)(2,1)S(1)} copy-done((bf16[84,16,128]{2,1,0:T(8,128)(2,1)S(1)}, bf16[84,16,128]{2,1,0:T(8,128)(2,1)}, u32[]{:S(2)}) %copy-start) | copy-done | bytes 344088
  1.1 0.7 copy-done.13
  1.8 0.7 copy-done.16
  2.5 1.9 %prep.1 = (bf16[84,2048]{1,0:T(8,128)(2,1)S(1)}, bf16[84,256]{1,0:T(8,128)(2,1)S(1)}, bf16[84,256]{1,0:T(8,128)(2,1)S(1)}, s32[16,256]{1,0:T(8,128)S(1)}) custom-call(s32[2]{0:T(128)S(1)} %pad_add_fusion.refs_0_, bf16[84,16,128]{2,1,0:T(8,128)(2,1)S(1)} %copy-done, s32[16,256]{1,0:T(8,128)S(1)} %copy-done.13, s32[1,256]{1,0:T(1,128)S(1)} %bitcast.11), custom_call_target="tpu_custom_call" | custom-call | flops 1000000000 | bytes 6000000 | tf_op jit(solution)/shard_map/prep/pallas_call | solution.py:403
  4.4 0.0 copy-start.9
  4.4 0.0 copy-start.12
  4.4 0.0 copy-start.17
  4.4 3.2 %encode.2 = (f32[84,256]{1,0:T(8,128)S(1)}, bf16[512,256]{1,0:T(8,128)(2,1)S(1)}) custom-call(s32[2]{0:T(128)S(1)} %pad_add_fusion.refs_0_, s32[16,256]{1,0:T(8,128)S(1)} %get-tuple-element.27.refs_1_.refs_2_, bf16[84,2048]{1,0:T(8,128)(2,1)S(1)} %get-tuple-element.28.refs_2_), custom_call_target="tpu_custom_call" | custom-call | flops 1500000000 | bytes 9000000 | tf_op jit(solution)/shard_map/encode/pallas_call | solution.py:403
  7.6 5.5 %collective-permute-start.4 = (bf16[256,1024]{1,0:T(8,128)(2,1)S(1)}, bf16[256,1024]{1,0:T(8,128)(2,1)S(1)}, u32[]{:S(2)}, u32[]{:S(2)}) collective-permute-start(bf16[256,1024]{1,0:T(8,128)(2,1)S(1)} %copy-done.9), channel_id=1, source_target_pairs={{0,15},{1,2},{2,1},{3,4},{4,3},{5,6},{6,5},{7,8},{8,7},{9,10},{10,... | collective-permute-start | bytes 1572872 | tf_op jit(solution)/shard_map/ppermute | solution.py:50
  13.1 0.0 collective-permute-start
  13.1 0.8 collective-permute-start.1
  13.8 1.5 %collective-permute-start.2 = (s32[16,256]{1,0:T(8,128)S(1)}, s32[16,256]{1,0:T(8,128)S(1)}, u32[]{:S(2)}, u32[]{:S(2)}) collective-permute-start(s32[16,256]{1,0:T(8,128)S(1)} %get-tuple-element.27.refs_1_.refs_2_), channel_id=1, source_target_pairs={{0,16},{16,0},{1,17},{17,1},{2,18},{18,2},{3,19},{19,3},{4,20},{20... | collective-permute-start | bytes 49160 | tf_op jit(solution)/shard_map/ppermute | solution.py:38
  15.3 0.5 collective-permute-start.3
  15.9 1.9 %collective-permute-done.2.refs_1_.refs_3_ = s32[16,256]{1,0:T(8,128)S(1)} collective-permute-done((s32[16,256]{1,0:T(8,128)S(1)}, s32[16,256]{1,0:T(8,128)S(1)}, u32[]{:S(2)}, u32[]{:S(2)}) %collective-permute-start.2) | collective-permute-done | bytes 16416 | tf_op jit(solution)/shard_map/ppermute | solution.py:38
  17.7 3.2 %encode.3 = (f32[84,256]{1,0:T(8,128)S(1)}, bf16[512,256]{1,0:T(8,128)(2,1)S(1)}) custom-call(s32[2]{0:T(128)S(1)} %pad_add_fusion.refs_0_, s32[16,256]{1,0:T(8,128)S(1)} %collective-permute-done.2.refs_1_.refs_3_, bf16[84,2048]{1,0:T(8,128)(2,1)S(1)} %get-tuple-element.28.refs_2_), custom_call_target="tpu_custom_call" | custom-call | flops 50000000 | bytes 300000 | tf_op jit(solution)/shard_map/encode/pallas_call | solution.py:403
  20.9 0.0 collective-permute-done.refs_0_
  20.9 0.2 rim.1.refs_0_
  21.2 1.6 %collective-permute-start.5 = (f32[84,512]{1,0:T(8,128)S(1)}, f32[84,512]{1,0:T(8,128)S(1)}, u32[]{:S(2)}, u32[]{:S(2)}) collective-permute-start(f32[84,512]{1,0:T(8,128)S(1)} %rim.1.refs_0_), channel_id=1, source_target_pairs={{0,16},{16,0},{1,17},{17,1},{2,18},{18,2},{3,19},{19,3},{4,20},{20... | collective-permute-start | bytes 516104 | tf_op jit(solution)/shard_map/ppermute | solution.py:38
  22.8 0.0 collective-permute-done.4.refs_6_
  22.8 0.5 collective-permute-start.8
  23.3 0.0 copy-start.5
  23.3 0.0 copy-start.6
  23.3 0.0 copy-start.10
  23.3 0.0 copy-start.14
  23.3 2.5 %bias.1 = (f32[256,512]{1,0:T(8,128)S(1)}, f32[256,1024]{1,0:T(8,128)S(1)}) custom-call(s32[2]{0:T(128)S(1)} %pad_add_fusion.refs_0_, s32[32,256]{1,0:T(8,128)S(1)} %copy-done.12, s32[1,256]{1,0:T(1,128)S(1)} %bitcast.12), custom_call_target="tpu_custom_call" | custom-call | flops 15000000512 | bytes 90000000 | tf_op jit(solution)/shard_map/bias/pallas_call | solution.py:403
  25.9 4.3 %collective-permute-done.3.refs_9_ = bf16[256,1024]{1,0:T(8,128)(2,1)S(1)} collective-permute-done((bf16[256,1024]{1,0:T(8,128)(2,1)S(1)}, bf16[256,1024]{1,0:T(8,128)(2,1)S(1)}, u32[]{:S(2)}, u32[]{:S(2)}) %collective-permute-start.3) | collective-permute-done | bytes 524320 | tf_op jit(solution)/shard_map/ppermute | solution.py:38
  30.2 3.9 %collective-permute-done.5.refs_1_ = f32[84,512]{1,0:T(8,128)S(1)} collective-permute-done((f32[84,512]{1,0:T(8,128)S(1)}, f32[84,512]{1,0:T(8,128)S(1)}, u32[]{:S(2)}, u32[]{:S(2)}) %collective-permute-start.5) | collective-permute-done | bytes 172064 | tf_op jit(solution)/shard_map/ppermute | solution.py:38
  34.1 0.6 collective-permute-start.7
  34.7 9.7 %own.1 = (f32[256,1024]{1,0:T(8,128)S(1)}, bf16[256,1024]{1,0:T(8,128)(2,1)S(1)}, bf16[512,2048]{1,0:T(8,128)(2,1)S(1)}, f32[256,1024]{1,0:T(8,128)S(1)}, f32[25...) custom-call(bf16[84,512]{1,0:T(8,128)(2,1)S(1)} %mean.1.refs_0_, f32[256,512]{1,0:T(8,128)S(1)} %get-tuple-element.34.refs_1_, ...), custom_call_target="tpu_custom_call" | custom-call | flops 5000000000 | bytes 30000000 | tf_op jit(solution)/shard_map/own/pallas_call | solution.py:403
  44.4 0.0 copy-start.7
  44.4 0.0 copy-start.8
  44.4 0.0 copy-start.11
  44.4 0.0 copy-start.15
  44.5 1.1 %collective-permute-start.6 = (bf16[512,2048]{1,0:T(8,128)(2,1)S(1)}, bf16[512,2048]{1,0:T(8,128)(2,1)S(1)}, u32[]{:S(2)}, u32[]{:S(2)}) collective-permute-start(bf16[512,2048]{1,0:T(8,128)(2,1)S(1)} %get-tuple-element.37), channel_id=1, source_target_pairs={{0,1},{1,0},{2,3},{3,2},{4,5},{5,4},{6,7},{7,6},{8,9},{9,8},{10,11... | collective-permute-start | bytes 6291464 | tf_op jit(solution)/shard_map/ppermute | solution.py:45
  45.5 0.0 collective-permute-done.7.refs_0_
  45.5 0.0 collective-permute-done.8.refs_7_
  45.5 4.7 %far.1.refs_1_ = bf16[512,2048]{1,0:T(8,128)(2,1)S(1)} custom-call(bf16[84,512]{1,0:T(8,128)(2,1)S(1)} %collective-permute-done.7.refs_0_, bf16[84,1024]{1,0:T(8,128)(2,1)S(1)} %copy-done.10, bf16[1024,1024]{1,0:T(8,128)(2,1)S(1)} %copy-done.4, bf16[1024,1024]{1,0:T(8,128)(2,1)S(1)} %copy-done.5, bf16[1024,1024]{1,0:T(8,128)(2,1)S(1)} %copy-done.6, ...), custom_call_target="tpu_custom_call" | custom-call | flops 30000001024 | bytes 180000000 | tf_op jit(solution)/shard_map/far/pallas_call | solution.py:403
  50.3 0.0 copy-start.1
  50.3 0.0 copy-start.2
  50.3 10.2 %attend.1.refs_1_ = bf16[84,256]{1,0:T(8,128)(2,1)S(1)} custom-call(bf16[512,2048]{1,0:T(8,128)(2,1)S(1)} %collective-permute-done.6.refs_0_, bf16[512,2048]{1,0:T(8,128)(2,1)S(1)} %far.1.refs_1_, f32[256,1024]{1,0:T(8,128)S(1)} %get-tuple-element.39.refs_2_, f32[256,1024]{1,0:T(8,128)S(1)} %get-tuple-element.40.refs_3_, ...), custom_call_target="tpu_custom_call" | custom-call | flops 6000000000 | bytes 36000000 | tf_op jit(solution)/shard_map/attend/pallas_call | solution.py:403
  60.5 0.6 collective-permute-start.9
  61.1 3.5 %collective-permute-done.9 = bf16[84,256]{1,0:T(8,128)(2,1)S(1)} collective-permute-done((bf16[84,256]{1,0:T(8,128)(2,1)S(1)}, bf16[84,256]{1,0:T(8,128)(2,1)S(1)}, u32[]{:S(2)}, u32[]{:S(2)}) %collective-permute-start.9) | collective-permute-done | bytes 43040 | tf_op jit(solution)/shard_map/ppermute | solution.py:38
  64.6 0.1 collective-permute-start.10
  64.7 3.4 %collective-permute-start.11 = (bf16[84,512]{1,0:T(8,128)(2,1)S(1)}, bf16[84,512]{1,0:T(8,128)(2,1)S(1)}, u32[]{:S(2)}, u32[]{:S(2)}) collective-permute-start(bf16[84,512]{1,0:T(8,128)(2,1)S(1)} %pad_maximum_fusion.refs_2_), channel_id=1, source_target_pairs={{0,15},{1,2},{2,1},{3,4},{4,3},{5,6},{6,5},{7,8},{8,7},{9,10},{10,... | collective-permute-start | bytes 258056 | tf_op jit(solution)/shard_map/ppermute | solution.py:50
  68.1 1.9 %decode_own.1.refs_1_ = f32[84,16,128]{2,1,0:T(8,128)S(1)} custom-call(s32[2]{0:T(128)S(1)} %pad_add_fusion.refs_0_, bf16[84,256]{1,0:T(8,128)(2,1)S(1)} %attend.1.refs_1_, s32[3,16,128]{2,1,0:T(8,128)S(1)} %copy-done.2, bf16[84,16,128]{2,1,0:T(8,128)(2,1)S(1)} %copy-done.1), custom_call_target="tpu_custom_call" | custom-call | flops 50000000 | bytes 300000 | tf_op jit(solution)/shard_map/decode_own/pallas_call | solution.py:403
  70.0 2.4 %decode_near.1.refs_1_ = f32[84,16,128]{2,1,0:T(8,128)S(1)} custom-call(s32[2]{0:T(128)S(1)} %pad_add_fusion.refs_0_, f32[84,16,128]{2,1,0:T(8,128)S(1)} %decode_own.1.refs_1_, bf16[84,512]{1,0:T(8,128)(2,1)S(1)} %pad_maximum_fusion.refs_2_, bf16[84,512]{1,0:T(8,128)(2,1)S(1)} %collective-permute-done.10.refs_3_, s32[3,16,128]{2,1,0:T(8,128)S(1)} %copy-done.2), custom_call_target="tpu_custom_call" | custom-call | flops 50000000 | bytes 300000 | tf_op jit(solution)/shard_map/decode_near/pallas_call | solution.py:403
  72.4 2.8 %decode_far.1 = f32[84,16,128]{2,1,0:T(8,128)} custom-call(s32[2]{0:T(128)S(1)} %pad_add_fusion.refs_0_, f32[84,16,128]{2,1,0:T(8,128)S(1)} %decode_near.1.refs_1_, bf16[84,512]{1,0:T(8,128)(2,1)S(1)} %collective-permute-done.11.refs_2_, s32[3,16,128]{2,1,0:T(8,128)S(1)} %copy-done.2), custom_call_target="tpu_custom_call" | custom-call | flops 50000000 | bytes 300000 | tf_op jit(solution)/shard_map/decode_far/pallas_call | solution.py:403
  (26 shorter events, 0.1 us)
Async XLA Ops:
  0.1 1.0 %copy-start = (bf16[84,16,128]{2,1,0:T(8,128)(2,1)S(1)}, bf16[84,16,128]{2,1,0:T(8,128)(2,1)}, u32[]{:S(2)}) copy-start(bf16[84,16,128]{2,1,0:T(8,128)(2,1)} %refs_3_.6) | copy-start | bytes 1032196
  1.1 0.7 copy-start.13
  1.8 0.7 copy-start.16
  4.4 3.2 %copy-start.9 = (bf16[256,1024]{1,0:T(8,128)(2,1)S(1)}, bf16[256,1024]{1,0:T(8,128)(2,1)}, u32[]{:S(2)}) copy-start(bf16[256,1024]{1,0:T(8,128)(2,1)} %refs_8_.1) | copy-start | bytes 1572868
  4.4 18.9 %copy-start.12 = (s32[32,256]{1,0:T(8,128)S(1)}, s32[32,256]{1,0:T(8,128)}, u32[]{:S(2)}) copy-start(s32[32,256]{1,0:T(8,128)} %refs_1_.2) | copy-start | bytes 98308
  4.4 18.9 %copy-start.17 = (s32[256]{0:T(256)S(1)}, s32[256]{0:T(256)}, u32[]{:S(2)}) copy-start(s32[256]{0:T(256)} %param.22) | copy-start | bytes 3076
  7.6 15.2 %collective-permute-start.4 = (bf16[256,1024]{1,0:T(8,128)(2,1)S(1)}, bf16[256,1024]{1,0:T(8,128)(2,1)S(1)}, u32[]{:S(2)}, u32[]{:S(2)}) collective-permute-start(bf16[256,1024]{1,0:T(8,128)(2,1)S(1)} %copy-done.9), channel_id=1, source_target_pairs={{0,15},{1,2},{2,1},{3,4},{4,3},{5,6},{6,5},{7,8},{8,7},{9,10},{10,... | collective-permute-start | bytes 1572872 | tf_op jit(solution)/shard_map/ppermute | solution.py:50
  13.1 7.8 %collective-permute-start = (bf16[84,256]{1,0:T(8,128)(2,1)S(1)}, bf16[84,256]{1,0:T(8,128)(2,1)S(1)}, u32[]{:S(2)}, u32[]{:S(2)}) collective-permute-start(bf16[84,256]{1,0:T(8,128)(2,1)S(1)} %get-tuple-element.25), channel_id=1, source_target_pairs={{0,1},{1,0},{2,3},{3,2},{4,5},{5,4},{6,7},{7,6},{8,9},{9,8},{10,11... | collective-permute-start | bytes 129032 | tf_op jit(solution)/shard_map/ppermute | solution.py:45
  13.1 7.8 %collective-permute-start.1 = (bf16[84,256]{1,0:T(8,128)(2,1)S(1)}, bf16[84,256]{1,0:T(8,128)(2,1)S(1)}, u32[]{:S(2)}, u32[]{:S(2)}) collective-permute-start(bf16[84,256]{1,0:T(8,128)(2,1)S(1)} %get-tuple-element.26), channel_id=1, source_target_pairs={{0,15},{1,2},{2,1},{3,4},{4,3},{5,6},{6,5},{7,8},{8,7},{9,10},{10,... | collective-permute-start | bytes 129032 | tf_op jit(solution)/shard_map/ppermute | solution.py:50
  13.8 3.9 %collective-permute-start.2 = (s32[16,256]{1,0:T(8,128)S(1)}, s32[16,256]{1,0:T(8,128)S(1)}, u32[]{:S(2)}, u32[]{:S(2)}) collective-permute-start(s32[16,256]{1,0:T(8,128)S(1)} %get-tuple-element.27.refs_1_.refs_2_), channel_id=1, source_target_pairs={{0,16},{16,0},{1,17},{17,1},{2,18},{18,2},{3,19},{19,3},{4,20},{20... | collective-permute-start | bytes 49160 | tf_op jit(solution)/shard_map/ppermute | solution.py:38
  15.3 14.9 %collective-permute-start.3 = (bf16[256,1024]{1,0:T(8,128)(2,1)S(1)}, bf16[256,1024]{1,0:T(8,128)(2,1)S(1)}, u32[]{:S(2)}, u32[]{:S(2)}) collective-permute-start(bf16[256,1024]{1,0:T(8,128)(2,1)S(1)} %copy-done.9), channel_id=1, source_target_pairs={{0,16},{16,0},{1,17},{17,1},{2,18},{18,2},{3,19},{19,3},{4,20},{20... | collective-permute-start | bytes 1572872 | tf_op jit(solution)/shard_map/ppermute | solution.py:38
  21.2 12.9 %collective-permute-start.5 = (f32[84,512]{1,0:T(8,128)S(1)}, f32[84,512]{1,0:T(8,128)S(1)}, u32[]{:S(2)}, u32[]{:S(2)}) collective-permute-start(f32[84,512]{1,0:T(8,128)S(1)} %rim.1.refs_0_), channel_id=1, source_target_pairs={{0,16},{16,0},{1,17},{17,1},{2,18},{18,2},{3,19},{19,3},{4,20},{20... | collective-permute-start | bytes 516104 | tf_op jit(solution)/shard_map/ppermute | solution.py:38
  22.8 22.8 %collective-permute-start.8 = (bf16[256,1024]{1,0:T(8,128)(2,1)S(1)}, bf16[256,1024]{1,0:T(8,128)(2,1)S(1)}, u32[]{:S(2)}, u32[]{:S(2)}) collective-permute-start(bf16[256,1024]{1,0:T(8,128)(2,1)S(1)} %collective-permute-done.4.refs_6_), channel_id=1, source_target_pairs={{0,16},{16,0},{1,17},{17,1},{2,18},{18,2},{3,19},{19,3},{4,20},{20... | collective-permute-start | bytes 1572872 | tf_op jit(solution)/shard_map/ppermute | solution.py:38
  23.3 11.4 %copy-start.3 = (bf16[1024,1024]{1,0:T(8,128)(2,1)S(1)}, bf16[1024,1024]{1,0:T(8,128)(2,1)}, u32[]{:S(2)}) copy-start(bf16[1024,1024]{1,0:T(8,128)(2,1)} %refs_4_.3) | copy-start | bytes 6291460
  23.3 11.4 %copy-start.4 = (bf16[1024,1024]{1,0:T(8,128)(2,1)S(1)}, bf16[1024,1024]{1,0:T(8,128)(2,1)}, u32[]{:S(2)}) copy-start(bf16[1024,1024]{1,0:T(8,128)(2,1)} %refs_2_.6) | copy-start | bytes 6291460
  23.3 11.4 %copy-start.5 = (bf16[1024,1024]{1,0:T(8,128)(2,1)S(1)}, bf16[1024,1024]{1,0:T(8,128)(2,1)}, u32[]{:S(2)}) copy-start(bf16[1024,1024]{1,0:T(8,128)(2,1)} %refs_3_.5) | copy-start | bytes 6291460
  23.3 11.4 %copy-start.6 = (bf16[1024,1024]{1,0:T(8,128)(2,1)S(1)}, bf16[1024,1024]{1,0:T(8,128)(2,1)}, u32[]{:S(2)}) copy-start(bf16[1024,1024]{1,0:T(8,128)(2,1)} %refs_4_.4) | copy-start | bytes 6291460
  23.3 11.4 %copy-start.10 = (bf16[84,1024]{1,0:T(8,128)(2,1)S(1)}, bf16[84,1024]{1,0:T(8,128)(2,1)}, u32[]{:S(2)}) copy-start(bf16[84,1024]{1,0:T(8,128)(2,1)} %refs_1_.3) | copy-start | bytes 516100
  23.3 11.4 %copy-start.14 = (f32[1024]{0:T(1024)S(1)}, f32[1024]{0:T(1024)}, u32[]{:S(2)}) copy-start(f32[1024]{0:T(1024)} %param.32) | copy-start | bytes 12292
  34.1 11.5 %collective-permute-start.7 = (bf16[84,512]{1,0:T(8,128)(2,1)S(1)}, bf16[84,512]{1,0:T(8,128)(2,1)S(1)}, u32[]{:S(2)}, u32[]{:S(2)}) collective-permute-start(bf16[84,512]{1,0:T(8,128)(2,1)S(1)} %mean.1.refs_0_), channel_id=1, source_target_pairs={{0,15},{1,2},{2,1},{3,4},{4,3},{5,6},{6,5},{7,8},{8,7},{9,10},{10,... | collective-permute-start | bytes 258056 | tf_op jit(solution)/shard_map/ppermute | solution.py:50
  44.4 5.9 %copy-start.7 = (bf16[1024,1024]{1,0:T(8,128)(2,1)S(1)}, bf16[1024,1024]{1,0:T(8,128)(2,1)}, u32[]{:S(2)}) copy-start(bf16[1024,1024]{1,0:T(8,128)(2,1)} %refs_8_.2) | copy-start | bytes 6291460
  44.4 5.9 %copy-start.8 = (bf16[1024,1024]{1,0:T(8,128)(2,1)S(1)}, bf16[1024,1024]{1,0:T(8,128)(2,1)}, u32[]{:S(2)}) copy-start(bf16[1024,1024]{1,0:T(8,128)(2,1)} %refs_9_.1) | copy-start | bytes 6291460
  44.4 5.8 %copy-start.11 = (bf16[1024,84]{0,1:T(8,128)(2,1)S(1)}, bf16[1024,84]{0,1:T(8,128)(2,1)}, u32[]{:S(2)}) copy-start(bf16[1024,84]{0,1:T(8,128)(2,1)} %param.31) | copy-start | bytes 516100
  44.4 5.8 %copy-start.15 = (f32[1024]{0:T(1024)S(1)}, f32[1024]{0:T(1024)}, u32[]{:S(2)}) copy-start(f32[1024]{0:T(1024)} %param.33) | copy-start | bytes 12292
  44.5 5.8 %collective-permute-start.6 = (bf16[512,2048]{1,0:T(8,128)(2,1)S(1)}, bf16[512,2048]{1,0:T(8,128)(2,1)S(1)}, u32[]{:S(2)}, u32[]{:S(2)}) collective-permute-start(bf16[512,2048]{1,0:T(8,128)(2,1)S(1)} %get-tuple-element.37), channel_id=1, source_target_pairs={{0,1},{1,0},{2,3},{3,2},{4,5},{5,4},{6,7},{7,6},{8,9},{9,8},{10,11... | collective-permute-start | bytes 6291464 | tf_op jit(solution)/shard_map/ppermute | solution.py:45
  50.3 17.8 %copy-start.1 = (bf16[84,16,128]{2,1,0:T(8,128)(2,1)S(1)}, bf16[84,16,128]{2,1,0:T(8,128)(2,1)}, u32[]{:S(2)}) copy-start(bf16[84,16,128]{2,1,0:T(8,128)(2,1)} %refs_3_.6) | copy-start | bytes 1032196
  50.3 17.8 %copy-start.2 = (s32[3,16,128]{2,1,0:T(8,128)S(1)}, s32[3,16,128]{2,1,0:T(8,128)}, u32[]{:S(2)}) copy-start(s32[3,16,128]{2,1,0:T(8,128)} %refs_3_.7) | copy-start | bytes 73732
  60.5 4.1 %collective-permute-start.9 = (bf16[84,256]{1,0:T(8,128)(2,1)S(1)}, bf16[84,256]{1,0:T(8,128)(2,1)S(1)}, u32[]{:S(2)}, u32[]{:S(2)}) collective-permute-start(bf16[84,256]{1,0:T(8,128)(2,1)S(1)} %attend.1.refs_1_), channel_id=1, source_target_pairs={{0,16},{16,0},{1,17},{17,1},{2,18},{18,2},{3,19},{19,3},{4,20},{20... | collective-permute-start | bytes 129032 | tf_op jit(solution)/shard_map/ppermute | solution.py:38
  64.6 5.4 %collective-permute-start.10 = (bf16[84,512]{1,0:T(8,128)(2,1)S(1)}, bf16[84,512]{1,0:T(8,128)(2,1)S(1)}, u32[]{:S(2)}, u32[]{:S(2)}) collective-permute-start(bf16[84,512]{1,0:T(8,128)(2,1)S(1)} %pad_maximum_fusion.refs_2_), channel_id=1, source_target_pairs={{0,1},{1,0},{2,3},{3,2},{4,5},{5,4},{6,7},{7,6},{8,9},{9,8},{10,11... | collective-permute-start | bytes 258056 | tf_op jit(solution)/shard_map/ppermute | solution.py:45
  64.7 7.7 %collective-permute-start.11 = (bf16[84,512]{1,0:T(8,128)(2,1)S(1)}, bf16[84,512]{1,0:T(8,128)(2,1)S(1)}, u32[]{:S(2)}, u32[]{:S(2)}) collective-permute-start(bf16[84,512]{1,0:T(8,128)(2,1)S(1)} %pad_maximum_fusion.refs_2_), channel_id=1, source_target_pairs={{0,15},{1,2},{2,1},{3,4},{4,3},{5,6},{6,5},{7,8},{8,7},{9,10},{10,... | collective-permute-start | bytes 258056 | tf_op jit(solution)/shard_map/ppermute | solution.py:50

commit v3 on v2

v3 whole, which is shorter than its diff:
```python
import functools

import jax
import jax.numpy as jnp
from jax import lax
from jax.experimental import pallas as pl
from jax.experimental.pallas import tpu as pltpu
from jax.sharding import PartitionSpec as P

HEADS = 16
HALO = 16
BF16 = jnp.bfloat16
F32 = jnp.float32
MIB = 1024 * 1024


def params(mib):
    return pltpu.CompilerParams(vmem_limit_bytes=mib * MIB)


def whole(memory=pltpu.VMEM):
    return pl.BlockSpec(memory_space=memory)


def silu(value):
    return 0.5 * value * (1.0 + jnp.tanh(0.5 * value))


def layer_norm(inputs_f, gain):
    centre = inputs_f - jnp.mean(inputs_f, axis=-1, keepdims=True)
    spread = jnp.mean(centre * centre, axis=-1, keepdims=True)
    return centre * lax.rsqrt(spread + 1e-05) * gain


def from_bands(value):
    count = lax.axis_size("lat")
    return [
        lax.ppermute(value, "lat", [(i, (i - step) % count) for i in range(count)])
        for step in range(1, count)
    ]


def from_near(value):
    count = lax.axis_size("lon")
    return lax.ppermute(value, "lon", [(i, i ^ 1) for i in range(count)])


def from_far(value):
    count = lax.axis_size("lon")
    return lax.ppermute(value, "lon", [(i, (i - 1 + 2 * (i % 2)) % count) for i in range(count)])


def quotient(value_f, divisor):
    return jnp.floor((value_f + 0.5) * (1.0 / divisor))


def prep_kernel(grid, src, count, near_ref, far_ref, live_ref, wide):
    slot = lax.broadcasted_iota(jnp.int32, live_ref.shape, 0)
    live_ref[...] = jnp.where(slot < count.now()[...], src.now()[...], -1)
    grid_ref = grid.now()
    rows, cols = grid_ref.shape[1:]
    per_tile = cols // HALO
    odd = lax.axis_index("lon") % 2
    near_at = jnp.where(odd == 0, cols - HALO, 0)
    far_at = cols - HALO - near_at
    lane = lax.broadcasted_iota(jnp.int32, (grid_ref.shape[0], cols), 1) // HALO
    wide[...] = grid_ref[...].astype(F32)
    for tile in range(rows // per_tile):
        near, far = None, None
        for place in range(per_tile):
            line = wide[:, tile * per_tile + place, :]
            turned = [
                pltpu.roll(line, (place * HALO - start + cols) % cols, 1)
                for start in (near_at, far_at)
            ]
            near = turned[0] if near is None else jnp.where(lane == place, turned[0], near)
            far = turned[1] if far is None else jnp.where(lane == place, turned[1], far)
        near_ref[:, tile * cols : (tile + 1) * cols] = near.astype(BF16)
        far_ref[:, tile * cols : (tile + 1) * cols] = far.astype(BF16)


def flat_kernel(grid, flat_ref, wide):
    grid_ref = grid.now()
    rows, cols = grid_ref.shape[1:]
    wide[...] = grid_ref[...].astype(F32)
    for row in range(rows):
        flat_ref[:, row * cols : (row + 1) * cols] = wide[:, row, :].astype(BF16)


def encode_kernel(src_ref, flat_ref, out_ref, rim_ref, counts):
    slots, nodes = src_ref.shape
    cells = flat_ref.shape[1]
    rim = rim_ref.shape[0] // 2
    rows = rim // HALO
    cols = cells // rows
    span = cols + 2 * HALO
    lanes = 128
    even = lax.axis_index("lon") % 2 == 0
    source = src_ref[...].astype(F32)
    row_of = quotient(source, span)
    col_of = source - row_of * span
    row_of = row_of - (lax.axis_index("lat") * rows).astype(F32)
    iota = lax.broadcasted_iota(jnp.int32, (span, lanes), 0).astype(F32).astype(BF16)
    one = jnp.ones((span, lanes), BF16)
    none = jnp.zeros((span, lanes), BF16)
    west = pl.multiple_of(jnp.where(even, rim, 0), rim)
    east = pl.multiple_of(jnp.where(even, 0, rim), rim)
    for row in range(rows):
        code = jnp.where(row_of == row, col_of, -1.0).astype(BF16)
        for tile in range(nodes // lanes):
            at = slice(tile * lanes, (tile + 1) * lanes)
            total = none
            for slot in range(slots):
                total = total + jnp.where(iota == code[slot : slot + 1, at], one, none)
            counts[row * cols : (row + 1) * cols, at] = total[HALO : HALO + cols]
            rim_ref[pl.ds(west + row * HALO, HALO), at] = total[:HALO]
            rim_ref[pl.ds(east + row * HALO, HALO), at] = total[HALO + cols :]
        if row % 2 == 1:
            part = slice((row - 1) * cols, (row + 1) * cols)
            summed = jnp.dot(flat_ref[:, part], counts[part], preferred_element_type=F32)
            out_ref[...] = summed if row == 1 else out_ref[...] + summed


def rim_kernel(near_ref, far_ref, *refs):
    out_ref = refs[-1]
    rim = near_ref.shape[1]
    for part in range(len(refs) // 2):
        summed, counts = refs[2 * part], refs[2 * part + 1]
        nodes = summed.shape[1]
        total = summed[...]
        total += jnp.dot(near_ref[...], counts[:rim], preferred_element_type=F32)
        total += jnp.dot(far_ref[...], counts[rim:], preferred_element_type=F32)
        out_ref[:, part * nodes : (part + 1) * nodes] = total


def mean_kernel(own_ref, *refs):
    out_ref = refs[-1]
    bands = len(refs) // 2
    others, sources = refs[: bands - 1], refs[bands - 1 : -1]
    nodes = own_ref.shape[1] // bands
    for band in range(bands):
        at = slice(band * nodes, (band + 1) * nodes)
        count = jnp.sum(jnp.where(sources[band][...] >= 0, 1.0, 0.0), axis=0, keepdims=True)
        total = own_ref[:, at]
        for step, other in enumerate(others, 1):
            there = (band - step) % bands
            total = total + other[:, there * nodes : (there + 1) * nodes]
        out_ref[:, at] = (total / count).astype(BF16)


def place_of(ids, node_count, bands, sectors):
    ids_f = ids.astype(F32)
    device = quotient(ids_f, node_count)
    member = ids_f - device * node_count
    band = quotient(device, sectors)
    sector = device - band * sectors
    mine = lax.axis_index("lon")
    near = mine + 1 - 2 * (mine % 2)
    side = jnp.where(sector == mine.astype(F32), 0.0, 2.0)
    side = jnp.where(sector == near.astype(F32), 1.0, side)
    band = band - lax.axis_index("lat").astype(F32)
    band = jnp.where(band < 0, band + bands, band)
    return side * bands + band, member


def bias_kernel(bands, sectors, ids, count, own_ref, rest_ref):
    ids_ref, count_ref = ids.now(), count.now()
    slots, nodes = ids_ref.shape
    lanes = 128
    block, member = place_of(ids_ref[...], nodes, bands, sectors)
    slot_of = lax.broadcasted_iota(jnp.int32, (slots, nodes), 0)
    block = jnp.where(slot_of < count_ref[...], block, -1.0)
    iota = lax.broadcasted_iota(jnp.int32, (nodes, lanes), 0).astype(F32).astype(BF16)
    shut = jnp.full((nodes, lanes), -1e30, BF16)
    opened = jnp.zeros((nodes, lanes), BF16)
    for part in range(3 * bands):
        code = jnp.where(block == part, member, -1.0).astype(BF16)
        ref, index = (own_ref, part) if part < bands else (rest_ref, part - bands)
        for tile in range(nodes // lanes):
            at = slice(tile * lanes, (tile + 1) * lanes)
            total = shut
            for slot in range(slots):
                total = jnp.where(iota == code[slot : slot + 1, at], opened, total)
            ref[at, index * nodes : (index + 1) * nodes] = total.astype(F32).T


def latent_of(mean, feat, w_embed, w_encode):
    embedded = silu(
        lax.dot_general(mean, w_embed, (((0,), (0,)), ((), ())), preferred_element_type=F32)
    ).astype(BF16)
    return feat.astype(F32) + jnp.dot(embedded, w_encode, preferred_element_type=F32)


def sector_rows(
    mean_ref, gain_ref, w_embed, w_encode, w_query, w_key, w_value, feats, latent_ref, query_ref, pair_ref
):
    nodes, features = feats[0].shape
    normed = []
    for part, feat in enumerate(feats):
        at = slice(part * nodes, (part + 1) * nodes)
        latent = latent_of(mean_ref[:, at], feat[...], w_embed[...], w_encode[...])
        normed.append(layer_norm(latent, gain_ref[...]).astype(BF16))
        if part == 0 and latent_ref is not None:
            latent_ref[...] = latent
            query_ref[...] = jnp.dot(
                normed[0], w_query[...], preferred_element_type=F32
            ).astype(BF16)
    normed = jnp.concatenate(normed, axis=0)
    pair_ref[:, :features] = jnp.dot(normed, w_key[...], preferred_element_type=F32).astype(BF16)
    pair_ref[:, features:] = jnp.dot(normed, w_value[...], preferred_element_type=F32).astype(BF16)


LANES = 128
CHUNK = 32
SLOTS = 2
PREP_MIB = 62


def pair_scores(query_ref, pairs, at, score_ref):
    nodes = query_ref.shape[0]
    width = LANES // 2
    first = lax.broadcasted_iota(jnp.int32, (nodes, LANES), 1) < width
    query = query_ref[:, at].astype(F32) * width**-0.5
    query = jnp.concatenate(
        [jnp.where(first, query, 0.0).astype(BF16), jnp.where(first, 0.0, query).astype(BF16)], axis=0
    )
    start = 0
    for keys in pairs:
        count = keys.shape[0]
        score_ref[:, start : start + count] = lax.dot_general(
            query, keys[:, at], (((1,), (1,)), ((), ())), preferred_element_type=F32
        )
        start += count


def pair_weights(score_ref, bias_ref, weight_ref, floors):
    nodes = bias_ref.shape[0]
    peaks = []
    for start in range(0, 2 * nodes, CHUNK):
        rows = slice(start, start + CHUNK)
        there = slice(start % nodes, start % nodes + CHUNK)
        scores = score_ref[rows] + bias_ref[there]
        peak = jnp.max(scores, axis=1, keepdims=True)
        if floors is not None:
            peak = jnp.maximum(peak, floors[start // nodes][there])
        weight_ref[rows] = jnp.exp(scores - peak).astype(BF16)
        peaks.append(jnp.broadcast_to(peak, (CHUNK, LANES)))
    return jnp.concatenate(peaks, axis=0)


def pair_values(weight_ref, pairs, at):
    total, start = None, 0
    for values in pairs:
        count = values.shape[0]
        rhs = jnp.concatenate([values[:, at], jnp.ones((count, LANES), BF16)], axis=1)
        part = jnp.dot(weight_ref[:, start : start + count], rhs, preferred_element_type=F32)
        total = part if total is None else total + part
        start += count
    return total[:, :LANES], total[:, LANES:]


def attention(query_ref, pairs, bias_ref, score_ref, weight_ref, peak_ref, store):
    nodes, features = query_ref.shape
    width = LANES // 2
    first = lax.broadcasted_iota(jnp.int32, (nodes, LANES), 1) < width
    ats = [slice(base, base + LANES) for base in range(0, features, LANES)]
    slots = score_ref.shape[0]
    for pair in range(min(slots - 1, len(ats))):
        pair_scores(query_ref, pairs, ats[pair], score_ref.at[pair])
    for pair, at in enumerate(ats):
        ahead = pair + slots - 1
        if ahead < len(ats):
            pair_scores(query_ref, pairs, ats[ahead], score_ref.at[ahead % slots])
        floors = None
        if peak_ref is not None:
            old = peak_ref[:, at]
            floors = [old[:, :1], old[:, width : width + 1]]
        slot = pair % slots
        peaks = pair_weights(score_ref.at[slot], bias_ref, weight_ref.at[slot], floors)
        value_at = slice(at.start + features, at.stop + features)
        values, sums = pair_values(weight_ref.at[slot], pairs, value_at)
        store(at, *(jnp.where(first, a[:nodes], a[nodes:]) for a in (values, sums, peaks)))


def far_kernel(mean_ref, w_embed, w_encode, w_key, w_value, gain, *refs):
    feats, pair_ref = [feat.now() for feat in refs[:-1]], refs[-1]
    sector_rows(
        mean_ref, gain.now(), w_embed, w_encode, None, w_key, w_value, feats, None, None, pair_ref
    )


def own_kernel(
    bands, mean_ref, bias_ref, w_embed, w_encode, w_query, w_key, w_value, gain, *refs
):
    feats, refs = [feat.now() for feat in refs[:bands]], refs[bands:]
    latent_ref, query_ref, pair_ref, mixed_ref, peak_ref, sum_ref, score_ref, weight_ref = refs
    nodes, features = query_ref.shape
    sector_rows(
        mean_ref, gain.now(), w_embed, w_encode, w_query, w_key, w_value, feats,
        latent_ref, query_ref, pair_ref,
    )

    def store(at, values, sums, peaks):
        mixed_ref[:, at] = values
        sum_ref[:, at] = sums
        peak_ref[:, at] = peaks

    attention(query_ref, [pair_ref], bias_ref, score_ref, weight_ref, None, store)


def attend_kernel(
    near_ref, far_ref, bias_ref, latent_ref, query_ref, mixed_ref, peak_ref, sum_ref,
    w_output, w_decode, gain_dec, w_read, out_ref, score_ref, weight_ref, context_ref,
):
    nodes, features = latent_ref.shape

    def store(at, values, sums, peaks):
        fade = jnp.exp(peak_ref[:, at] - peaks)
        values = values + fade * mixed_ref[:, at]
        context_ref[:, at] = (values / (sums + fade * sum_ref[:, at])).astype(BF16)

    attention(query_ref, [near_ref, far_ref], bias_ref, score_ref, weight_ref, peak_ref, store)
    mixed = latent_ref[...] + jnp.dot(context_ref[...], w_output[...], preferred_element_type=F32)
    normed_out = layer_norm(mixed, gain_dec.now()[...]).astype(BF16)
    decoded = silu(jnp.dot(normed_out, w_decode[...], preferred_element_type=F32)).astype(BF16)
    out_ref[...] = lax.dot_general(
        w_read.now()[...], decoded, (((1,), (1,)), ((), ())), preferred_element_type=F32
    ).astype(BF16)


def decode_kernel(bands, sectors, parts, dec, reads, base_ref, out_ref, wide=None, signals=None):
    dec_ref = dec.now()
    rows, cols = dec_ref.shape[1:]
    nodes = parts[0][1].stop - parts[0][1].start
    iota = lax.broadcasted_iota(jnp.int32, (nodes, 2 * cols), 0).astype(F32).astype(BF16)
    one = jnp.ones((nodes, 2 * cols), BF16)
    none = jnp.zeros((nodes, 2 * cols), BF16)
    block, member = place_of(dec_ref[...], nodes, bands, sectors)
    copies, half = [], rows // 2
    for row in range(0, rows, 2):
        at = slice(row * cols, (row + 2) * cols)
        update = None
        for (part, there), read_ref in zip(parts, reads):
            code = jnp.where(block == part, member, -1.0)
            code = jnp.concatenate([code[:, row], code[:, row + 1]], axis=1).astype(BF16)
            counts = none
            for slot in range(code.shape[0]):
                counts = counts + jnp.where(iota == code[slot : slot + 1], one, none)
            share = jnp.dot(read_ref[:, there], counts, preferred_element_type=F32)
            update = share if update is None else update + share
        update = base_ref[:, at].astype(F32) + update / 3.0
        if wide is None:
            out_ref[:, at] = update
            continue
        wide[:, row, :] = update[:, :cols]
        wide[:, row + 1, :] = update[:, cols:]
        if (row + 2) % half == 0:
            done = slice(row + 2 - half, row + 2)
            copies.append(
                pltpu.make_async_copy(
                    wide.at[:, done], out_ref.at[:, done], signals.at[len(copies)]
                )
            )
            copies[-1].start()
    for copy in copies:
        copy.wait()


class Late:
    def __init__(self, source, target, semaphore):
        self.target = target
        self.copy = pltpu.make_async_copy(source, target, semaphore)
        self.copy.start()
        self.waited = False

    def now(self):
        if not self.waited:
            self.copy.wait()
            self.waited = True
        return self.target


def call(name, kernel, outs, operands, late=(), scratch=(), mib=8, micros=1, out_memory=pltpu.VMEM):
    single = not isinstance(outs, (list, tuple))
    outs = [outs] if single else list(outs)
    n_in, n_late, n_out = len(operands), len(late), len(outs)

    def run(*refs):
        ins, refs = refs[:n_in], refs[n_in:]
        sources, refs = refs[:n_late], refs[n_late:]
        results, refs = refs[:n_out], refs[n_out:]
        targets, refs = refs[:n_late], refs[n_late:]
        if n_late:
            semaphores, refs = refs[0], refs[1:]
        fetched = [
            Late(source, target, semaphores.at[index])
            for index, (source, target) in enumerate(zip(sources, targets))
        ]
        kernel(*ins, *fetched, *results, *refs)

    fetch = [pltpu.VMEM(a.shape, a.dtype) for a in late]
    signals = [pltpu.SemaphoreType.DMA((n_late,))] if n_late else []
    specs = [whole()] * n_in + [whole(pltpu.HBM)] * n_late
    result = pl.pallas_call(
        run,
        name=name,
        out_shape=outs,
        in_specs=specs,
        out_specs=[whole(out_memory)] * n_out,
        scratch_shapes=fetch + signals + list(scratch),
        compiler_params=params(mib),
        cost_estimate=pl.CostEstimate(
            flops=int(micros * 5e8), bytes_accessed=int(micros * 3e6), transcendentals=0
        ),
    )(*operands, *late)
    return result[0] if single else result


def after(value, *earlier):
    return lax.optimization_barrier((value,) + earlier)[0]


def body(
    grid_state, mesh_feat, enc_src, enc_count, nbr_ids, nbr_count, dec_src,
    w_embed, w_encode, w_query, w_key, w_value, w_output, w_decode, w_readout, norm_attn, norm_dec,
):
    shape = jax.ShapeDtypeStruct
    bands, sectors = lax.axis_size("lat"), lax.axis_size("lon")
    variables, rows, cols = grid_state.shape
    nodes, features = mesh_feat.shape
    slots = enc_src.shape[0]
    cells, rim = rows * cols, rows * HALO
    sector_nodes = bands * nodes

    near_rim, far_rim, live = call(
        "prep",
        prep_kernel,
        [
            shape((variables, rim), BF16),
            shape((variables, rim), BF16),
            shape((slots, nodes), jnp.int32),
        ],
        (),
        late=(grid_state, enc_src, enc_count[None]),
        scratch=[pltpu.VMEM((variables, rows, cols), F32)],
        mib=PREP_MIB,
        micros=2,
    )
    feat = after(mesh_feat, live)
    far_rim = from_far(far_rim)
    lives = [live] + from_bands(live)
    near_rim = from_near(near_rim)
    flat = call(
        "flat",
        flat_kernel,
        shape((variables, cells), BF16),
        (),
        late=(after(grid_state, live),),
        scratch=[pltpu.VMEM((variables, rows, cols), F32)],
        micros=0.1,
    )
    encoded = []
    for step, source in enumerate(lives):
        encoded += call(
            "encode",
            encode_kernel,
            [shape((variables, nodes), F32), shape((2 * rim, nodes), BF16)],
                (source, flat),
            scratch=[pltpu.VMEM((cells, nodes), BF16)],
            micros=0.1 if step else 3,
        )
    feats = [feat] + from_bands(feat)
    feat_far = from_far(feat)
    summed = call(
        "rim", rim_kernel, shape((variables, sector_nodes), F32),
        (near_rim, far_rim, *encoded), micros=0.1,
    )
    received = from_bands(summed)
    bias_own, bias_rest = call(
        "bias",
        functools.partial(bias_kernel, bands, sectors),
        [shape((nodes, sector_nodes), F32), shape((nodes, 2 * sector_nodes), F32)],
        (),
        late=(after(nbr_ids, summed), nbr_count[None]),
        micros=30,
    )
    mean = call(
        "mean",
        mean_kernel,
        shape((variables, sector_nodes), BF16),
        (after(summed, bias_own), *received, *lives),
        micros=0.1,
    )
    feats_far = [feat_far] + from_bands(after(feat_far, mean))
    mean_far = from_far(mean)
    latent, query, pair, mixed, peak, total = call(
        "own",
        functools.partial(own_kernel, bands),
        [
            shape((nodes, features), F32),
            shape((nodes, features), BF16),
            shape((sector_nodes, 2 * features), BF16),
        ]
        + [shape((nodes, features), F32)] * 3,
        (mean, bias_own, after(w_embed, feat_far), w_encode, w_query, w_key, w_value),
        late=(norm_attn[None], *feats),
        scratch=[
            pltpu.VMEM((SLOTS, 2 * nodes, sector_nodes), F32),
            pltpu.VMEM((SLOTS, 2 * nodes, sector_nodes), BF16),
        ],
        mib=30,
        micros=10,
    )
    pair_near = from_near(pair)
    pair_far = call(
        "far",
        far_kernel,
        shape((sector_nodes, 2 * features), BF16),
        (mean_far, after(w_embed, pair), w_encode, w_key, w_value),
        late=(norm_attn[None], *feats_far),
        mib=16,
        micros=60,
    )
    readout = call(
        "attend",
        attend_kernel,
        shape((variables, nodes), BF16),
        (pair_near, pair_far, bias_rest, latent, query, mixed, peak, total, w_output, w_decode),
        late=(norm_dec[None], w_readout.T),
        scratch=[
            pltpu.VMEM((SLOTS, 2 * nodes, 2 * sector_nodes), F32),
            pltpu.VMEM((SLOTS, 2 * nodes, 2 * sector_nodes), BF16),
            pltpu.VMEM((nodes, features), BF16),
        ],
        mib=28,
        micros=12,
    )
    sums = shape((variables, cells), F32)
    decode = functools.partial(decode_kernel, bands, sectors)
    spots = [slice(band * nodes, (band + 1) * nodes) for band in range(bands)]
    own_sums = call(
        "decode_own",
        lambda read, base, dec, out: decode([(0, spots[0])], dec, [read], base, out),
        sums,
        (readout, flat),
        late=(dec_src,),
        micros=0.1,
    )
    reads = jnp.concatenate([readout] + from_bands(readout), axis=1)
    reads = after(reads, own_sums)
    read_far = from_far(reads)
    read_near = from_near(reads)
    near_sums = call(
        "decode_near",
        lambda base, own, near, dec, out: decode(
            list(enumerate(spots))[1:] + list(enumerate(spots, bands)),
            dec, [own] * (bands - 1) + [near] * bands, base, out,
        ),
        sums,
        (own_sums, reads, read_near),
        late=(dec_src,),
        micros=0.1,
    )
    return call(
        "decode_far",
        lambda base, far, dec, out, *more: decode(
            list(enumerate(spots, 2 * bands)), dec, [far] * bands, base, out, *more
        ),
        shape(grid_state.shape, F32),
        (near_sums, read_far),
        late=(dec_src,),
        scratch=[pltpu.VMEM(grid_state.shape, F32), pltpu.SemaphoreType.DMA((2,))],
        out_memory=pltpu.HBM,
        micros=0.1,
    )


def solution(mesh):
    in_specs = (
        P(None, "lat", "lon"),
        P(("lat", "lon"), None),
        P(None, ("lat", "lon")),
        P(("lat", "lon")),
        P(None, ("lat", "lon")),
        P(("lat", "lon")),
        P(None, "lat", "lon"),
    ) + (P(),) * 10
    out_specs = P(None, "lat", "lon")
    return jax.shard_map(body, mesh=mesh, in_specs=in_specs, out_specs=out_specs, check_vma=False)
```

time: 75.6 us -> 66 us (0.87)
  waiting for transfers between devices: 13.6 us -> 5.26 us
  starting transfers between devices: 16.1 us -> 22.3 us
  Pallas kernels: 42.6 us -> 36.9 us
  local copies, waits for them, and re-layouts: 2.46 us -> 0.8 us
    ppermute x5, waiting for transfers between devices: 13.6 us -> 3.38 us  [from_bands(): lax.ppermute(value, 'lat', [(i, (i - step) % count) for i in range(count)])]
    pallas_call x12 -> x13, Pallas kernels: 42.6 us -> 36.9 us  [call(): pl.pallas_call(run, name=name, out_shape=outs, in_specs=specs, out_specs=...]
    ppermute x5, starting transfers between devices: 4.72 us -> 9.61 us  [from_bands(): lax.ppermute(value, 'lat', [(i, (i - step) % count) for i in range(count)])]
    ppermute x3, starting transfers between devices: 1.15 us -> 3.3 us  [from_near(): return lax.ppermute(value, 'lon', [(i, i ^ 1) for i in range(count)])]
    ppermute x4, waiting for transfers between devices: 0.01 us -> 1.87 us  [from_far(): lax.ppermute(value, 'lon', [(i, (i - 1 + 2 * (i % 2)) % count) for i in r...]
    unnamed x36 -> x34, local copies, waits for them, and re-layouts: 2.46 us -> 0.8 us
    ppermute x4, starting transfers between devices: 10.3 us -> 9.4 us  [from_far(): lax.ppermute(value, 'lon', [(i, (i - 1 + 2 * (i % 2)) % count) for i in r...]
  transfers between devices with their start and end apart: 12 -> 12, of which waited for: 4 -> 3; matrix products, arithmetic and copies ran while one was open for 0% -> 0% of each run, Pallas kernels for 33% -> 35%
where the time goes in v3:
time: 66 us; the launch traced here: 65.8 us
  Pallas kernels  36.9 us (56%)
  starting transfers between devices  22.3 us (34%)
  waiting for transfers between devices  5.26 us (8%)
  local copies, waits for them, and re-layouts  0.8 us (1%)
    pallas_call x13, Pallas kernels, call(): pl.pallas_call(run, name=name, out_shape=outs, in_specs=specs, out_specs=...  36.9 us
    ppermute x5, starting transfers between devices, from_bands(): lax.ppermute(value, 'lat', [(i, (i - step) % count) for i in range(count)])  9.61 us
    ppermute x4, starting transfers between devices, from_far(): lax.ppermute(value, 'lon', [(i, (i - 1 + 2 * (i % 2)) % count) for i in r...  9.4 us
    ppermute x5, waiting for transfers between devices, from_bands(): lax.ppermute(value, 'lat', [(i, (i - step) % count) for i in range(count)])  3.38 us
    ppermute x3, starting transfers between devices, from_near(): return lax.ppermute(value, 'lon', [(i, i ^ 1) for i in range(count)])  3.3 us
    ppermute x4, waiting for transfers between devices, from_far(): lax.ppermute(value, 'lon', [(i, (i - 1 + 2 * (i % 2)) % count) for i in r...  1.87 us
  transfers between devices with their start and end apart: 12, of which 3 were waited for; matrix products, arithmetic and copies ran while one was open for 0% of the time, Pallas kernels for 35%

profile of v3, /device:TPU:0, one launch (start us, length us, event | category | flops | bytes accessed | tf_op | source)
XLA Modules:
  0.0 65.8 jit_solution(13746029558447279090)
XLA Ops:
  0.0 2.2 %prep.1 = (bf16[84,256]{1,0:T(8,128)(2,1)}, bf16[84,256]{1,0:T(8,128)(2,1)}, s32[16,256]{1,0:T(8,128)}) custom-call(bf16[84,16,128]{2,1,0:T(8,128)(2,1)} %refs_0_.2, s32[16,256]{1,0:T(8,128)} %refs_1_.1, s32[1,256]{1,0:T(1,128)} %bitcast.10), custom_call_target="tpu_custom_call" | custom-call | flops 1000000000 | bytes 6000000 | tf_op jit(solution)/shard_map/prep/pallas_call | solution.py:404
  2.2 3.0 %collective-permute-start.2 = (s32[16,256]{1,0:T(8,128)}, s32[16,256]{1,0:T(8,128)S(1)}, u32[]{:S(2)}, u32[]{:S(2)}) collective-permute-start(s32[16,256]{1,0:T(8,128)} %get-tuple-element.30.refs_0_.refs_2_), channel_id=1, source_target_pairs={{0,16},{16,0},{1,17},{17,1},{2,18},{18,2},{3,19},{19,3},{4,20},{20... | collective-permute-start | bytes 49160 | tf_op jit(solution)/shard_map/ppermute | solution.py:38
  5.3 0.0 copy-done.10
  5.3 3.7 %collective-permute-start.4 = (bf16[256,1024]{1,0:T(8,128)(2,1)S(1)}, bf16[256,1024]{1,0:T(8,128)(2,1)S(1)}, u32[]{:S(2)}, u32[]{:S(2)}) collective-permute-start(bf16[256,1024]{1,0:T(8,128)(2,1)S(1)} %copy-done.10), channel_id=1, source_target_pairs={{0,15},{1,2},{2,1},{3,4},{4,3},{5,6},{6,5},{7,8},{8,7},{9,10},{10,... | collective-permute-start | bytes 1572872 | tf_op jit(solution)/shard_map/ppermute | solution.py:50
  9.0 0.5 collective-permute-start.5
  9.5 0.0 collective-permute-start
  9.5 1.0 %collective-permute-start.1 = (bf16[84,256]{1,0:T(8,128)(2,1)}, bf16[84,256]{1,0:T(8,128)(2,1)S(1)}, u32[]{:S(2)}, u32[]{:S(2)}) collective-permute-start(bf16[84,256]{1,0:T(8,128)(2,1)} %get-tuple-element.29), channel_id=1, source_target_pairs={{0,15},{1,2},{2,1},{3,4},{4,3},{5,6},{6,5},{7,8},{8,7},{9,10},{10,... | collective-permute-start | bytes 129032 | tf_op jit(solution)/shard_map/ppermute | solution.py:50
  10.5 1.1 %flat.1.refs_1_ = bf16[84,2048]{1,0:T(8,128)(2,1)S(1)} custom-call(bf16[84,16,128]{2,1,0:T(8,128)(2,1)S(1)} %copy-done), custom_call_target="tpu_custom_call" | custom-call | flops 50000000 | bytes 300000 | tf_op jit(solution)/shard_map/flat/pallas_call | solution.py:404
  11.6 0.7 %copy-done.2 = s32[16,256]{1,0:T(8,128)S(1)} copy-done((s32[16,256]{1,0:T(8,128)S(1)}, s32[16,256]{1,0:T(8,128)}, u32[]{:S(2)}) %copy-start.2) | copy-done | bytes 16408
  12.3 2.6 %encode.2 = (f32[84,256]{1,0:T(8,128)S(1)}, bf16[512,256]{1,0:T(8,128)(2,1)S(1)}) custom-call(s32[16,256]{1,0:T(8,128)S(1)} %copy-done.2, bf16[84,2048]{1,0:T(8,128)(2,1)S(1)} %flat.1.refs_1_), custom_call_target="tpu_custom_call" | custom-call | flops 1500000000 | bytes 9000000 | tf_op jit(solution)/shard_map/encode/pallas_call | solution.py:404
  14.9 0.0 collective-permute-done.2.refs_0_.refs_3_
  14.9 2.6 %encode.3 = (f32[84,256]{1,0:T(8,128)S(1)}, bf16[512,256]{1,0:T(8,128)(2,1)S(1)}) custom-call(s32[16,256]{1,0:T(8,128)S(1)} %collective-permute-done.2.refs_0_.refs_3_, bf16[84,2048]{1,0:T(8,128)(2,1)S(1)} %flat.1.refs_1_), custom_call_target="tpu_custom_call" | custom-call | flops 50000000 | bytes 300000 | tf_op jit(solution)/shard_map/encode/pallas_call | solution.py:404
  17.6 0.0 collective-permute-done.refs_0_
  17.6 0.0 collective-permute-done.1.refs_1_
  17.6 0.2 rim.1.refs_0_
  17.8 1.6 %collective-permute-start.3 = (f32[84,512]{1,0:T(8,128)S(1)}, f32[84,512]{1,0:T(8,128)S(1)}, u32[]{:S(2)}, u32[]{:S(2)}) collective-permute-start(f32[84,512]{1,0:T(8,128)S(1)} %rim.1.refs_0_), channel_id=1, source_target_pairs={{0,16},{16,0},{1,17},{17,1},{2,18},{18,2},{3,19},{19,3},{4,20},{20... | collective-permute-start | bytes 516104 | tf_op jit(solution)/shard_map/ppermute | solution.py:38
  19.4 0.0 copy-start.5
  19.4 0.0 copy-start.6
  19.5 0.0 copy-start.7
  19.5 0.0 copy-start.11
  19.5 0.0 copy-start.14
  19.5 2.0 %bias.1 = (f32[256,512]{1,0:T(8,128)S(1)}, f32[256,1024]{1,0:T(8,128)S(1)}) custom-call(s32[32,256]{1,0:T(8,128)S(1)} %copy-done.13, s32[1,256]{1,0:T(1,128)S(1)} %bitcast.9), custom_call_target="tpu_custom_call" | custom-call | flops 15000000512 | bytes 90000000 | tf_op jit(solution)/shard_map/bias/pallas_call | solution.py:404
  21.5 1.9 %collective-permute-done.3.refs_1_ = f32[84,512]{1,0:T(8,128)S(1)} collective-permute-done((f32[84,512]{1,0:T(8,128)S(1)}, f32[84,512]{1,0:T(8,128)S(1)}, u32[]{:S(2)}, u32[]{:S(2)}) %collective-permute-start.3) | collective-permute-done | bytes 172064 | tf_op jit(solution)/shard_map/ppermute | solution.py:38
  23.4 0.0 collective-permute-done.4.refs_6_
  23.5 2.4 %collective-permute-start.8 = (bf16[256,1024]{1,0:T(8,128)(2,1)S(1)}, bf16[256,1024]{1,0:T(8,128)(2,1)S(1)}, u32[]{:S(2)}, u32[]{:S(2)}) collective-permute-start(bf16[256,1024]{1,0:T(8,128)(2,1)S(1)} %collective-permute-done.4.refs_6_), channel_id=1, source_target_pairs={{0,16},{16,0},{1,17},{17,1},{2,18},{18,2},{3,19},{19,3},{4,20},{20... | collective-permute-start | bytes 1572872 | tf_op jit(solution)/shard_map/ppermute | solution.py:38
  25.9 1.2 %collective-permute-start.7 = (bf16[84,512]{1,0:T(8,128)(2,1)S(1)}, bf16[84,512]{1,0:T(8,128)(2,1)S(1)}, u32[]{:S(2)}, u32[]{:S(2)}) collective-permute-start(bf16[84,512]{1,0:T(8,128)(2,1)S(1)} %mean.1.refs_0_), channel_id=1, source_target_pairs={{0,15},{1,2},{2,1},{3,4},{4,3},{5,6},{6,5},{7,8},{8,7},{9,10},{10,... | collective-permute-start | bytes 258056 | tf_op jit(solution)/shard_map/ppermute | solution.py:50
  27.1 0.0 collective-permute-done.5.refs_9_
  27.1 8.2 %own.1 = (f32[256,1024]{1,0:T(8,128)S(1)}, bf16[256,1024]{1,0:T(8,128)(2,1)S(1)}, bf16[512,2048]{1,0:T(8,128)(2,1)S(1)}, f32[256,1024]{1,0:T(8,128)S(1)}, f32[25...) custom-call(bf16[84,512]{1,0:T(8,128)(2,1)S(1)} %mean.1.refs_0_, f32[256,512]{1,0:T(8,128)S(1)} %get-tuple-element.37.refs_1_, ...), custom_call_target="tpu_custom_call" | custom-call | flops 5000000000 | bytes 30000000 | tf_op jit(solution)/shard_map/own/pallas_call | solution.py:404
  35.3 0.0 copy-start.8
  35.3 0.0 copy-start.9
  35.3 0.0 copy-start.12
  35.3 0.0 copy-start.15
  35.4 3.2 %collective-permute-start.6 = (bf16[512,2048]{1,0:T(8,128)(2,1)S(1)}, bf16[512,2048]{1,0:T(8,128)(2,1)S(1)}, u32[]{:S(2)}, u32[]{:S(2)}) collective-permute-start(bf16[512,2048]{1,0:T(8,128)(2,1)S(1)} %get-tuple-element.41), channel_id=1, source_target_pairs={{0,1},{1,0},{2,3},{3,2},{4,5},{5,4},{6,7},{7,6},{8,9},{9,8},{10,11... | collective-permute-start | bytes 6291464 | tf_op jit(solution)/shard_map/ppermute | solution.py:45
  38.6 0.0 collective-permute-done.7.refs_0_
  38.6 0.0 collective-permute-done.8.refs_7_
  38.6 4.4 %far.1.refs_1_ = bf16[512,2048]{1,0:T(8,128)(2,1)S(1)} custom-call(bf16[84,512]{1,0:T(8,128)(2,1)S(1)} %collective-permute-done.7.refs_0_, bf16[84,1024]{1,0:T(8,128)(2,1)S(1)} %copy-done.11, bf16[1024,1024]{1,0:T(8,128)(2,1)S(1)} %copy-done.5, bf16[1024,1024]{1,0:T(8,128)(2,1)S(1)} %copy-done.6, bf16[1024,1024]{1,0:T(8,128)(2,1)S(1)} %copy-done.7, ...), custom_call_target="tpu_custom_call" | custom-call | flops 30000001024 | bytes 180000000 | tf_op jit(solution)/shard_map/far/pallas_call | solution.py:404
  43.0 0.0 collective-permute-done.6.refs_0_
  43.0 0.0 copy-start.1
  43.0 9.6 %attend.1.refs_0_ = bf16[84,256]{1,0:T(8,128)(2,1)S(1)} custom-call(bf16[512,2048]{1,0:T(8,128)(2,1)S(1)} %collective-permute-done.6.refs_0_, bf16[512,2048]{1,0:T(8,128)(2,1)S(1)} %far.1.refs_1_, f32[256,1024]{1,0:T(8,128)S(1)} %get-tuple-element.44.refs_2_, f32[256,1024]{1,0:T(8,128)S(1)} %get-tuple-element.45.refs_3_, ...), custom_call_target="tpu_custom_call" | custom-call | flops 6000000000 | bytes 36000000 | tf_op jit(solution)/shard_map/attend/pallas_call | solution.py:404
  52.7 2.1 %collective-permute-start.9 = (bf16[84,256]{1,0:T(8,128)(2,1)S(1)}, bf16[84,256]{1,0:T(8,128)(2,1)S(1)}, u32[]{:S(2)}, u32[]{:S(2)}) collective-permute-start(bf16[84,256]{1,0:T(8,128)(2,1)S(1)} %attend.1.refs_0_), channel_id=1, source_target_pairs={{0,16},{16,0},{1,17},{17,1},{2,18},{18,2},{3,19},{19,3},{4,20},{20... | collective-permute-start | bytes 129032 | tf_op jit(solution)/shard_map/ppermute | solution.py:38
  54.8 0.6 decode_own.1.refs_0_
  55.4 1.5 %collective-permute-done.9 = bf16[84,256]{1,0:T(8,128)(2,1)S(1)} collective-permute-done((bf16[84,256]{1,0:T(8,128)(2,1)S(1)}, bf16[84,256]{1,0:T(8,128)(2,1)S(1)}, u32[]{:S(2)}, u32[]{:S(2)}) %collective-permute-start.9) | collective-permute-done | bytes 43040 | tf_op jit(solution)/shard_map/ppermute | solution.py:38
  56.8 0.1 collective-permute-start.10
  56.9 3.5 %collective-permute-start.11 = (bf16[84,512]{1,0:T(8,128)(2,1)S(1)}, bf16[84,512]{1,0:T(8,128)(2,1)S(1)}, u32[]{:S(2)}, u32[]{:S(2)}) collective-permute-start(bf16[84,512]{1,0:T(8,128)(2,1)S(1)} %pad_maximum_fusion.refs_1_), channel_id=1, source_target_pairs={{0,15},{1,2},{2,1},{3,4},{4,3},{5,6},{6,5},{7,8},{8,7},{9,10},{10,... | collective-permute-start | bytes 258056 | tf_op jit(solution)/shard_map/ppermute | solution.py:50
  60.4 0.0 collective-permute-done.10.refs_2_
  60.4 1.3 %decode_near.1.refs_0_ = f32[84,2048]{1,0:T(8,128)S(1)} custom-call(f32[84,2048]{1,0:T(8,128)S(1)} %decode_own.1.refs_0_, bf16[84,512]{1,0:T(8,128)(2,1)S(1)} %pad_maximum_fusion.refs_1_, bf16[84,512]{1,0:T(8,128)(2,1)S(1)} %collective-permute-done.10.refs_2_, s32[3,16,128]{2,1,0:T(8,128)S(1)} %copy-done.1), custom_call_target="tpu_custom_call" | custom-call | flops 50000000 | bytes 300000 | tf_op jit(solution)/shard_map/decode_near/pallas_call | solution.py:404
  61.8 1.9 %collective-permute-done.11.refs_1_ = bf16[84,512]{1,0:T(8,128)(2,1)S(1)} collective-permute-done((bf16[84,512]{1,0:T(8,128)(2,1)S(1)}, bf16[84,512]{1,0:T(8,128)(2,1)S(1)}, u32[]{:S(2)}, u32[]{:S(2)}) %collective-permute-start.11) | collective-permute-done | bytes 86048 | tf_op jit(solution)/shard_map/ppermute | solution.py:50
  63.6 2.0 %decode_far.1 = f32[84,16,128]{2,1,0:T(8,128)} custom-call(f32[84,2048]{1,0:T(8,128)S(1)} %decode_near.1.refs_0_, bf16[84,512]{1,0:T(8,128)(2,1)S(1)} %collective-permute-done.11.refs_1_, s32[3,16,128]{2,1,0:T(8,128)S(1)} %copy-done.1), custom_call_target="tpu_custom_call" | custom-call | flops 50000000 | bytes 300000 | tf_op jit(solution)/shard_map/decode_far/pallas_call | solution.py:404
  (24 shorter events, 0.1 us)
Async XLA Ops:
  0.0 10.5 %copy-start = (bf16[84,16,128]{2,1,0:T(8,128)(2,1)S(1)}, bf16[84,16,128]{2,1,0:T(8,128)(2,1)}, u32[]{:S(2)}) copy-start(bf16[84,16,128]{2,1,0:T(8,128)(2,1)} %refs_0_.2) | copy-start | bytes 1032196
  0.0 5.3 %copy-start.10 = (bf16[256,1024]{1,0:T(8,128)(2,1)S(1)}, bf16[256,1024]{1,0:T(8,128)(2,1)}, u32[]{:S(2)}) copy-start(bf16[256,1024]{1,0:T(8,128)(2,1)} %refs_8_.1) | copy-start | bytes 1572868
  2.2 12.7 %collective-permute-start.2 = (s32[16,256]{1,0:T(8,128)}, s32[16,256]{1,0:T(8,128)S(1)}, u32[]{:S(2)}, u32[]{:S(2)}) collective-permute-start(s32[16,256]{1,0:T(8,128)} %get-tuple-element.30.refs_0_.refs_2_), channel_id=1, source_target_pairs={{0,16},{16,0},{1,17},{17,1},{2,18},{18,2},{3,19},{19,3},{4,20},{20... | collective-permute-start | bytes 49160 | tf_op jit(solution)/shard_map/ppermute | solution.py:38
  5.3 18.2 %collective-permute-start.4 = (bf16[256,1024]{1,0:T(8,128)(2,1)S(1)}, bf16[256,1024]{1,0:T(8,128)(2,1)S(1)}, u32[]{:S(2)}, u32[]{:S(2)}) collective-permute-start(bf16[256,1024]{1,0:T(8,128)(2,1)S(1)} %copy-done.10), channel_id=1, source_target_pairs={{0,15},{1,2},{2,1},{3,4},{4,3},{5,6},{6,5},{7,8},{8,7},{9,10},{10,... | collective-permute-start | bytes 1572872 | tf_op jit(solution)/shard_map/ppermute | solution.py:50
  9.0 18.1 %collective-permute-start.5 = (bf16[256,1024]{1,0:T(8,128)(2,1)S(1)}, bf16[256,1024]{1,0:T(8,128)(2,1)S(1)}, u32[]{:S(2)}, u32[]{:S(2)}) collective-permute-start(bf16[256,1024]{1,0:T(8,128)(2,1)S(1)} %copy-done.10), channel_id=1, source_target_pairs={{0,16},{16,0},{1,17},{17,1},{2,18},{18,2},{3,19},{19,3},{4,20},{20... | collective-permute-start | bytes 1572872 | tf_op jit(solution)/shard_map/ppermute | solution.py:38
  9.5 8.1 %collective-permute-start = (bf16[84,256]{1,0:T(8,128)(2,1)}, bf16[84,256]{1,0:T(8,128)(2,1)S(1)}, u32[]{:S(2)}, u32[]{:S(2)}) collective-permute-start(bf16[84,256]{1,0:T(8,128)(2,1)} %get-tuple-element.28), channel_id=1, source_target_pairs={{0,1},{1,0},{2,3},{3,2},{4,5},{5,4},{6,7},{7,6},{8,9},{9,8},{10,11... | collective-permute-start | bytes 129032 | tf_op jit(solution)/shard_map/ppermute | solution.py:45
  9.5 8.1 %collective-permute-start.1 = (bf16[84,256]{1,0:T(8,128)(2,1)}, bf16[84,256]{1,0:T(8,128)(2,1)S(1)}, u32[]{:S(2)}, u32[]{:S(2)}) collective-permute-start(bf16[84,256]{1,0:T(8,128)(2,1)} %get-tuple-element.29), channel_id=1, source_target_pairs={{0,15},{1,2},{2,1},{3,4},{4,3},{5,6},{6,5},{7,8},{8,7},{9,10},{10,... | collective-permute-start | bytes 129032 | tf_op jit(solution)/shard_map/ppermute | solution.py:50
  11.6 0.7 %copy-start.2 = (s32[16,256]{1,0:T(8,128)S(1)}, s32[16,256]{1,0:T(8,128)}, u32[]{:S(2)}) copy-start(s32[16,256]{1,0:T(8,128)} %get-tuple-element.30.refs_0_.refs_2_) | copy-start | bytes 49156
  12.3 7.1 %copy-start.13 = (s32[32,256]{1,0:T(8,128)S(1)}, s32[32,256]{1,0:T(8,128)}, u32[]{:S(2)}) copy-start(s32[32,256]{1,0:T(8,128)} %refs_0_.3) | copy-start | bytes 98308
  12.3 7.1 %copy-start.16 = (s32[256]{0:T(256)S(1)}, s32[256]{0:T(256)}, u32[]{:S(2)}) copy-start(s32[256]{0:T(256)} %param.22) | copy-start | bytes 3076
  17.8 5.6 %collective-permute-start.3 = (f32[84,512]{1,0:T(8,128)S(1)}, f32[84,512]{1,0:T(8,128)S(1)}, u32[]{:S(2)}, u32[]{:S(2)}) collective-permute-start(f32[84,512]{1,0:T(8,128)S(1)} %rim.1.refs_0_), channel_id=1, source_target_pairs={{0,16},{16,0},{1,17},{17,1},{2,18},{18,2},{3,19},{19,3},{4,20},{20... | collective-permute-start | bytes 516104 | tf_op jit(solution)/shard_map/ppermute | solution.py:38
  19.4 4.0 %copy-start.3 = (s32[16,256]{1,0:T(8,128)S(1)}, s32[16,256]{1,0:T(8,128)}, u32[]{:S(2)}) copy-start(s32[16,256]{1,0:T(8,128)} %get-tuple-element.30.refs_0_.refs_2_) | copy-start | bytes 49156
  19.4 7.7 %copy-start.4 = (bf16[1024,1024]{1,0:T(8,128)(2,1)S(1)}, bf16[1024,1024]{1,0:T(8,128)(2,1)}, u32[]{:S(2)}) copy-start(bf16[1024,1024]{1,0:T(8,128)(2,1)} %refs_4_.2) | copy-start | bytes 6291460
  19.4 7.6 %copy-start.5 = (bf16[1024,1024]{1,0:T(8,128)(2,1)S(1)}, bf16[1024,1024]{1,0:T(8,128)(2,1)}, u32[]{:S(2)}) copy-start(bf16[1024,1024]{1,0:T(8,128)(2,1)} %refs_2_.4) | copy-start | bytes 6291460
  19.4 7.6 %copy-start.6 = (bf16[1024,1024]{1,0:T(8,128)(2,1)S(1)}, bf16[1024,1024]{1,0:T(8,128)(2,1)}, u32[]{:S(2)}) copy-start(bf16[1024,1024]{1,0:T(8,128)(2,1)} %refs_3_.4) | copy-start | bytes 6291460
  19.5 7.6 %copy-start.7 = (bf16[1024,1024]{1,0:T(8,128)(2,1)S(1)}, bf16[1024,1024]{1,0:T(8,128)(2,1)}, u32[]{:S(2)}) copy-start(bf16[1024,1024]{1,0:T(8,128)(2,1)} %refs_4_.3) | copy-start | bytes 6291460
  19.5 7.6 %copy-start.11 = (bf16[84,1024]{1,0:T(8,128)(2,1)S(1)}, bf16[84,1024]{1,0:T(8,128)(2,1)}, u32[]{:S(2)}) copy-start(bf16[84,1024]{1,0:T(8,128)(2,1)} %refs_1_.2) | copy-start | bytes 516100
  19.5 7.6 %copy-start.14 = (f32[1024]{0:T(1024)S(1)}, f32[1024]{0:T(1024)}, u32[]{:S(2)}) copy-start(f32[1024]{0:T(1024)} %param.32) | copy-start | bytes 12292
  23.5 15.1 %collective-permute-start.8 = (bf16[256,1024]{1,0:T(8,128)(2,1)S(1)}, bf16[256,1024]{1,0:T(8,128)(2,1)S(1)}, u32[]{:S(2)}, u32[]{:S(2)}) collective-permute-start(bf16[256,1024]{1,0:T(8,128)(2,1)S(1)} %collective-permute-done.4.refs_6_), channel_id=1, source_target_pairs={{0,16},{16,0},{1,17},{17,1},{2,18},{18,2},{3,19},{19,3},{4,20},{20... | collective-permute-start | bytes 1572872 | tf_op jit(solution)/shard_map/ppermute | solution.py:38
  25.9 12.7 %collective-permute-start.7 = (bf16[84,512]{1,0:T(8,128)(2,1)S(1)}, bf16[84,512]{1,0:T(8,128)(2,1)S(1)}, u32[]{:S(2)}, u32[]{:S(2)}) collective-permute-start(bf16[84,512]{1,0:T(8,128)(2,1)S(1)} %mean.1.refs_0_), channel_id=1, source_target_pairs={{0,15},{1,2},{2,1},{3,4},{4,3},{5,6},{6,5},{7,8},{8,7},{9,10},{10,... | collective-permute-start | bytes 258056 | tf_op jit(solution)/shard_map/ppermute | solution.py:50
  35.3 7.7 %copy-start.8 = (bf16[1024,1024]{1,0:T(8,128)(2,1)S(1)}, bf16[1024,1024]{1,0:T(8,128)(2,1)}, u32[]{:S(2)}) copy-start(bf16[1024,1024]{1,0:T(8,128)(2,1)} %refs_8_.2) | copy-start | bytes 6291460
  35.3 7.7 %copy-start.9 = (bf16[1024,1024]{1,0:T(8,128)(2,1)S(1)}, bf16[1024,1024]{1,0:T(8,128)(2,1)}, u32[]{:S(2)}) copy-start(bf16[1024,1024]{1,0:T(8,128)(2,1)} %refs_9_.1) | copy-start | bytes 6291460
  35.3 7.7 %copy-start.12 = (bf16[1024,84]{0,1:T(8,128)(2,1)S(1)}, bf16[1024,84]{0,1:T(8,128)(2,1)}, u32[]{:S(2)}) copy-start(bf16[1024,84]{0,1:T(8,128)(2,1)} %param.31) | copy-start | bytes 516100
  35.3 7.7 %copy-start.15 = (f32[1024]{0:T(1024)S(1)}, f32[1024]{0:T(1024)}, u32[]{:S(2)}) copy-start(f32[1024]{0:T(1024)} %param.33) | copy-start | bytes 12292
  35.4 7.6 %collective-permute-start.6 = (bf16[512,2048]{1,0:T(8,128)(2,1)S(1)}, bf16[512,2048]{1,0:T(8,128)(2,1)S(1)}, u32[]{:S(2)}, u32[]{:S(2)}) collective-permute-start(bf16[512,2048]{1,0:T(8,128)(2,1)S(1)} %get-tuple-element.41), channel_id=1, source_target_pairs={{0,1},{1,0},{2,3},{3,2},{4,5},{5,4},{6,7},{7,6},{8,9},{9,8},{10,11... | collective-permute-start | bytes 6291464 | tf_op jit(solution)/shard_map/ppermute | solution.py:45
  43.0 11.8 %copy-start.1 = (s32[3,16,128]{2,1,0:T(8,128)S(1)}, s32[3,16,128]{2,1,0:T(8,128)}, u32[]{:S(2)}) copy-start(s32[3,16,128]{2,1,0:T(8,128)} %refs_2_.6) | copy-start | bytes 73732
  52.7 4.1 %collective-permute-start.9 = (bf16[84,256]{1,0:T(8,128)(2,1)S(1)}, bf16[84,256]{1,0:T(8,128)(2,1)S(1)}, u32[]{:S(2)}, u32[]{:S(2)}) collective-permute-start(bf16[84,256]{1,0:T(8,128)(2,1)S(1)} %attend.1.refs_0_), channel_id=1, source_target_pairs={{0,16},{16,0},{1,17},{17,1},{2,18},{18,2},{3,19},{19,3},{4,20},{20... | collective-permute-start | bytes 129032 | tf_op jit(solution)/shard_map/ppermute | solution.py:38
  56.8 3.6 %collective-permute-start.10 = (bf16[84,512]{1,0:T(8,128)(2,1)S(1)}, bf16[84,512]{1,0:T(8,128)(2,1)S(1)}, u32[]{:S(2)}, u32[]{:S(2)}) collective-permute-start(bf16[84,512]{1,0:T(8,128)(2,1)S(1)} %pad_maximum_fusion.refs_1_), channel_id=1, source_target_pairs={{0,1},{1,0},{2,3},{3,2},{4,5},{5,4},{6,7},{7,6},{8,9},{9,8},{10,11... | collective-permute-start | bytes 258056 | tf_op jit(solution)/shard_map/ppermute | solution.py:45
  56.9 6.7 %collective-permute-start.11 = (bf16[84,512]{1,0:T(8,128)(2,1)S(1)}, bf16[84,512]{1,0:T(8,128)(2,1)S(1)}, u32[]{:S(2)}, u32[]{:S(2)}) collective-permute-start(bf16[84,512]{1,0:T(8,128)(2,1)S(1)} %pad_maximum_fusion.refs_1_), channel_id=1, source_target_pairs={{0,15},{1,2},{2,1},{3,4},{4,3},{5,6},{6,5},{7,8},{8,7},{9,10},{10,... | collective-permute-start | bytes 258056 | tf_op jit(solution)/shard_map/ppermute | solution.py:50

commit v4 on v3

--- a/solution.py
+++ b/solution.py
@@ -54,10 +54,13 @@
     return jnp.floor((value_f + 0.5) * (1.0 / divisor))
 
 
-def prep_kernel(grid, src, count, near_ref, far_ref, live_ref, wide):
+def first_kernel(out_ref):
+    out_ref[...] = jnp.zeros(out_ref.shape, F32)
+
+
+def prep_kernel(first_ref, grid_ref, src_ref, count_ref, near_ref, far_ref, live_ref, wide):
     slot = lax.broadcasted_iota(jnp.int32, live_ref.shape, 0)
-    live_ref[...] = jnp.where(slot < count.now()[...], src.now()[...], -1)
-    grid_ref = grid.now()
+    live_ref[...] = jnp.where(slot < count_ref[...], src_ref[...], -1)
     rows, cols = grid_ref.shape[1:]
     per_tile = cols // HALO
     odd = lax.axis_index("lon") % 2
@@ -79,15 +82,14 @@
         far_ref[:, tile * cols : (tile + 1) * cols] = far.astype(BF16)
 
 
-def flat_kernel(grid, flat_ref, wide):
-    grid_ref = grid.now()
+def flat_kernel(grid_ref, flat_ref, wide):
     rows, cols = grid_ref.shape[1:]
     wide[...] = grid_ref[...].astype(F32)
     for row in range(rows):
         flat_ref[:, row * cols : (row + 1) * cols] = wide[:, row, :].astype(BF16)
 
 
-def encode_kernel(src_ref, flat_ref, out_ref, rim_ref, counts):
+def encode_kernel(src_ref, flat_ref, out_ref, rim_ref):
     slots, nodes = src_ref.shape
     cells = flat_ref.shape[1]
     rim = rim_ref.shape[0] // 2
@@ -105,32 +107,38 @@
     none = jnp.zeros((span, lanes), BF16)
     west = pl.multiple_of(jnp.where(even, rim, 0), rim)
     east = pl.multiple_of(jnp.where(even, 0, rim), rim)
-    for row in range(rows):
-        code = jnp.where(row_of == row, col_of, -1.0).astype(BF16)
-        for tile in range(nodes // lanes):
-            at = slice(tile * lanes, (tile + 1) * lanes)
-            total = none
-            for slot in range(slots):
-                total = total + jnp.where(iota == code[slot : slot + 1, at], one, none)
-            counts[row * cols : (row + 1) * cols, at] = total[HALO : HALO + cols]
-            rim_ref[pl.ds(west + row * HALO, HALO), at] = total[:HALO]
-            rim_ref[pl.ds(east + row * HALO, HALO), at] = total[HALO + cols :]
-        if row % 2 == 1:
-            part = slice((row - 1) * cols, (row + 1) * cols)
-            summed = jnp.dot(flat_ref[:, part], counts[part], preferred_element_type=F32)
-            out_ref[...] = summed if row == 1 else out_ref[...] + summed
+    summed = None
+    for row in range(0, rows, 2):
+        parts = []
+        for r in (row, row + 1):
+            code = jnp.where(row_of == r, col_of, -1.0).astype(BF16)
+            line = []
+            for tile in range(nodes // lanes):
+                at = slice(tile * lanes, (tile + 1) * lanes)
+                total = none
+                for slot in range(slots):
+                    total = total + jnp.where(iota == code[slot : slot + 1, at], one, none)
+                rim_ref[pl.ds(west + r * HALO, HALO), at] = total[:HALO]
+                rim_ref[pl.ds(east + r * HALO, HALO), at] = total[HALO + cols :]
+                line.append(total[HALO : HALO + cols])
+            parts.append(jnp.concatenate(line, axis=1))
+        part = slice(row * cols, (row + 2) * cols)
+        got = jnp.dot(flat_ref[:, part], jnp.concatenate(parts, axis=0), preferred_element_type=F32)
+        summed = got if summed is None else summed + got
+    out_ref[...] = summed
 
 
 def rim_kernel(near_ref, far_ref, *refs):
-    out_ref = refs[-1]
+    out_ref, sent_ref = refs[-2:]
     rim = near_ref.shape[1]
-    for part in range(len(refs) // 2):
+    for part in range(len(refs) // 2 - 1):
         summed, counts = refs[2 * part], refs[2 * part + 1]
         nodes = summed.shape[1]
         total = summed[...]
         total += jnp.dot(near_ref[...], counts[:rim], preferred_element_type=F32)
         total += jnp.dot(far_ref[...], counts[rim:], preferred_element_type=F32)
         out_ref[:, part * nodes : (part + 1) * nodes] = total
+    sent_ref[...] = out_ref[...].astype(BF16)
 
 
 def mean_kernel(own_ref, *refs):
@@ -144,7 +152,7 @@
         total = own_ref[:, at]
         for step, other in enumerate(others, 1):
             there = (band - step) % bands
-            total = total + other[:, there * nodes : (there + 1) * nodes]
+            total = total + other[:, there * nodes : (there + 1) * nodes].astype(F32)
         out_ref[:, at] = (total / count).astype(BF16)
 
 
@@ -194,10 +202,11 @@
 def sector_rows(
     mean_ref, gain_ref, w_embed, w_encode, w_query, w_key, w_value, feats, latent_ref, query_ref, pair_ref
 ):
-    nodes, features = feats[0].shape
-    normed = []
+    features = feats[0].shape[1]
+    normed, start = [], 0
     for part, feat in enumerate(feats):
-        at = slice(part * nodes, (part + 1) * nodes)
+        at = slice(start, start + feat.shape[0])
+        start = at.stop
         latent = latent_of(mean_ref[:, at], feat[...], w_embed[...], w_encode[...])
         normed.append(layer_norm(latent, gain_ref[...]).astype(BF16))
         if part == 0 and latent_ref is not None:
@@ -213,7 +222,6 @@
 LANES = 128
 CHUNK = 32
 SLOTS = 2
-PREP_MIB = 62
 
 
 def pair_scores(query_ref, pairs, at, score_ref):
@@ -290,9 +298,9 @@
 
 
 def own_kernel(
-    bands, mean_ref, bias_ref, w_embed, w_encode, w_query, w_key, w_value, gain, *refs
+    count, mean_ref, bias_ref, w_embed, w_encode, w_query, w_key, w_value, gain, *refs
 ):
-    feats, refs = [feat.now() for feat in refs[:bands]], refs[bands:]
+    feats, refs = [feat.now() for feat in refs[:count]], refs[count:]
     latent_ref, query_ref, pair_ref, mixed_ref, peak_ref, sum_ref, score_ref, weight_ref = refs
     nodes, features = query_ref.shape
     sector_rows(
@@ -432,6 +440,7 @@
     cells, rim = rows * cols, rows * HALO
     sector_nodes = bands * nodes
 
+    first = call("first", first_kernel, shape((8, LANES), F32), (), micros=20)
     near_rim, far_rim, live = call(
         "prep",
         prep_kernel,
@@ -440,22 +449,20 @@
             shape((variables, rim), BF16),
             shape((slots, nodes), jnp.int32),
         ],
-        (),
-        late=(grid_state, enc_src, enc_count[None]),
+        (first, grid_state, enc_src, enc_count[None]),
         scratch=[pltpu.VMEM((variables, rows, cols), F32)],
-        mib=PREP_MIB,
         micros=2,
     )
     feat = after(mesh_feat, live)
     far_rim = from_far(far_rim)
+    near_rim = from_near(near_rim)
+    feats = [mesh_feat] + from_bands(mesh_feat)
     lives = [live] + from_bands(live)
-    near_rim = from_near(near_rim)
     flat = call(
         "flat",
         flat_kernel,
         shape((variables, cells), BF16),
-        (),
-        late=(after(grid_state, live),),
+        (after(grid_state, live),),
         scratch=[pltpu.VMEM((variables, rows, cols), F32)],
         micros=0.1,
     )
@@ -466,16 +473,16 @@
             encode_kernel,
             [shape((variables, nodes), F32), shape((2 * rim, nodes), BF16)],
                 (source, flat),
-            scratch=[pltpu.VMEM((cells, nodes), BF16)],
             micros=0.1 if step else 3,
         )
-    feats = [feat] + from_bands(feat)
     feat_far = from_far(feat)
-    summed = call(
-        "rim", rim_kernel, shape((variables, sector_nodes), F32),
+    summed, sent = call(
+        "rim",
+        rim_kernel,
+        [shape((variables, sector_nodes), F32), shape((variables, sector_nodes), BF16)],
         (near_rim, far_rim, *encoded), micros=0.1,
     )
-    received = from_bands(summed)
+    received = from_bands(sent)
     bias_own, bias_rest = call(
         "bias",
         functools.partial(bias_kernel, bands, sectors),
@@ -495,7 +502,7 @@
     mean_far = from_far(mean)
     latent, query, pair, mixed, peak, total = call(
         "own",
-        functools.partial(own_kernel, bands),
+        functools.partial(own_kernel, len(feats)),
         [
             shape((nodes, features), F32),
             shape((nodes, features), BF16),

time: 66 us -> 62 us (0.939)
  Pallas kernels: 36.9 us -> 34.4 us
  starting transfers between devices: 22.3 us -> 19.9 us
  waiting for transfers between devices: 5.26 us -> 5.94 us
    ppermute x4, starting transfers between devices: 9.4 us -> 14.1 us  [from_far(): lax.ppermute(value, 'lon', [(i, (i - 1 + 2 * (i % 2)) % count) for i in r...]
    ppermute x5, starting transfers between devices: 9.61 us -> 5.12 us  [from_bands(): lax.ppermute(value, 'lat', [(i, (i - step) % count) for i in range(count)])]
    ppermute x3, starting transfers between devices: 3.3 us -> 0.66 us  [from_near(): return lax.ppermute(value, 'lon', [(i, i ^ 1) for i in range(count)])]
    pallas_call x13 -> x14, Pallas kernels: 36.9 us -> 34.4 us  [call(): pl.pallas_call(run, name=name, out_shape=outs, in_specs=specs, out_specs=...]
    ppermute x5, waiting for transfers between devices: 3.38 us -> 5.02 us  [from_bands(): lax.ppermute(value, 'lat', [(i, (i - step) % count) for i in range(count)])]
    ppermute x4, waiting for transfers between devices: 1.87 us -> 0.91 us  [from_far(): lax.ppermute(value, 'lon', [(i, (i - 1 + 2 * (i % 2)) % count) for i in r...]
  transfers between devices with their start and end apart: 12 -> 12, of which waited for: 3 -> 3; matrix products, arithmetic and copies ran while one was open for 0% -> 0% of each run, Pallas kernels for 35% -> 36%
where the time goes in v4:
time: 62 us; the launch traced here: 61.9 us
  Pallas kernels  34.4 us (55%)
  starting transfers between devices  19.9 us (32%)
  waiting for transfers between devices  5.94 us (10%)
  local copies, waits for them, and re-layouts  1.05 us (2%)
    pallas_call x14, Pallas kernels, call(): pl.pallas_call(run, name=name, out_shape=outs, in_specs=specs, out_specs=...  34.4 us
    ppermute x4, starting transfers between devices, from_far(): lax.ppermute(value, 'lon', [(i, (i - 1 + 2 * (i % 2)) % count) for i in r...  14.1 us
    ppermute x5, starting transfers between devices, from_bands(): lax.ppermute(value, 'lat', [(i, (i - step) % count) for i in range(count)])  5.12 us
    ppermute x5, waiting for transfers between devices, from_bands(): lax.ppermute(value, 'lat', [(i, (i - step) % count) for i in range(count)])  5.02 us
  transfers between devices with their start and end apart: 12, of which 3 were waited for; matrix products, arithmetic and copies ran while one was open for 0% of the time, Pallas kernels for 36%

profile of v4, /device:TPU:0, one launch (start us, length us, event | category | flops | bytes accessed | tf_op | source)
XLA Modules:
  0.0 61.9 jit_solution(1563575404857415904)
XLA Ops:
  0.0 1.0 %copy-done = bf16[84,16,128]{2,1,0:T(8,128)(2,1)S(1)} copy-done((bf16[84,16,128]{2,1,0:T(8,128)(2,1)S(1)}, bf16[84,16,128]{2,1,0:T(8,128)(2,1)}, u32[]{:S(2)}) %copy-start) | copy-done | bytes 344088
  1.0 0.5 prep.1
  1.5 0.5 collective-permute-start
  2.0 5.7 %collective-permute-start.1 = (bf16[84,256]{1,0:T(8,128)(2,1)S(1)}, bf16[84,256]{1,0:T(8,128)(2,1)S(1)}, u32[]{:S(2)}, u32[]{:S(2)}) collective-permute-start(bf16[84,256]{1,0:T(8,128)(2,1)S(1)} %get-tuple-element.31), channel_id=1, source_target_pairs={{0,15},{1,2},{2,1},{3,4},{4,3},{5,6},{6,5},{7,8},{8,7},{9,10},{10,... | collective-permute-start | bytes 129032 | tf_op jit(solution)/shard_map/ppermute | solution.py:50
  7.7 1.5 %collective-permute-start.2 = (s32[16,256]{1,0:T(8,128)S(1)}, s32[16,256]{1,0:T(8,128)S(1)}, u32[]{:S(2)}, u32[]{:S(2)}) collective-permute-start(s32[16,256]{1,0:T(8,128)S(1)} %get-tuple-element.32.refs_0_.refs_2_), channel_id=1, source_target_pairs={{0,16},{16,0},{1,17},{17,1},{2,18},{18,2},{3,19},{19,3},{4,20},{20... | collective-permute-start | bytes 49160 | tf_op jit(solution)/shard_map/ppermute | solution.py:38
  9.2 0.5 collective-permute-start.5
  9.7 0.0 collective-permute-start.4
  9.7 0.9 %flat.1.refs_1_ = bf16[84,2048]{1,0:T(8,128)(2,1)S(1)} custom-call(bf16[84,16,128]{2,1,0:T(8,128)(2,1)S(1)} %copy-done), custom_call_target="tpu_custom_call" | custom-call | flops 50000000 | bytes 300000 | tf_op jit(solution)/shard_map/flat/pallas_call | solution.py:412
  10.7 0.0 copy-start.11
  10.7 0.0 copy-start.16
  10.7 2.3 %encode.2 = (f32[84,256]{1,0:T(8,128)S(1)}, bf16[512,256]{1,0:T(8,128)(2,1)S(1)}) custom-call(s32[16,256]{1,0:T(8,128)S(1)} %get-tuple-element.32.refs_0_.refs_2_, bf16[84,2048]{1,0:T(8,128)(2,1)S(1)} %flat.1.refs_1_), custom_call_target="tpu_custom_call" | custom-call | flops 1500000000 | bytes 9000000 | tf_op jit(solution)/shard_map/encode/pallas_call | solution.py:412
  13.1 0.0 collective-permute-done.2.refs_0_.refs_3_
  13.1 2.3 %encode.3 = (f32[84,256]{1,0:T(8,128)S(1)}, bf16[512,256]{1,0:T(8,128)(2,1)S(1)}) custom-call(s32[16,256]{1,0:T(8,128)S(1)} %collective-permute-done.2.refs_0_.refs_3_, bf16[84,2048]{1,0:T(8,128)(2,1)S(1)} %flat.1.refs_1_), custom_call_target="tpu_custom_call" | custom-call | flops 50000000 | bytes 300000 | tf_op jit(solution)/shard_map/encode/pallas_call | solution.py:412
  15.4 0.0 collective-permute-done.refs_0_
  15.4 0.0 collective-permute-done.1.refs_1_
  15.4 0.2 rim.1
  15.7 1.6 %collective-permute-start.3 = (bf16[84,512]{1,0:T(8,128)(2,1)S(1)}, bf16[84,512]{1,0:T(8,128)(2,1)S(1)}, u32[]{:S(2)}, u32[]{:S(2)}) collective-permute-start(bf16[84,512]{1,0:T(8,128)(2,1)S(1)} %get-tuple-element.42), channel_id=1, source_target_pairs={{0,16},{16,0},{1,17},{17,1},{2,18},{18,2},{3,19},{19,3},{4,20},{20... | collective-permute-start | bytes 258056 | tf_op jit(solution)/shard_map/ppermute | solution.py:38
  17.2 0.0 copy-start.4
  17.3 0.0 copy-start.5
  17.3 0.0 copy-start.9
  17.3 0.0 copy-start.13
  17.3 2.2 %bias.1 = (f32[256,512]{1,0:T(8,128)S(1)}, f32[256,1024]{1,0:T(8,128)S(1)}) custom-call(s32[32,256]{1,0:T(8,128)S(1)} %copy-done.11, s32[1,256]{1,0:T(1,128)S(1)} %bitcast.10), custom_call_target="tpu_custom_call" | custom-call | flops 15000000512 | bytes 90000000 | tf_op jit(solution)/shard_map/bias/pallas_call | solution.py:412
  19.5 2.8 %collective-permute-done.3.refs_1_ = bf16[84,512]{1,0:T(8,128)(2,1)S(1)} collective-permute-done((bf16[84,512]{1,0:T(8,128)(2,1)S(1)}, bf16[84,512]{1,0:T(8,128)(2,1)S(1)}, u32[]{:S(2)}, u32[]{:S(2)}) %collective-permute-start.3) | collective-permute-done | bytes 86048 | tf_op jit(solution)/shard_map/ppermute | solution.py:38
  22.3 0.0 collective-permute-done.4.refs_6_
  22.4 0.2 collective-permute-start.8
  22.5 2.8 %collective-permute-start.7 = (bf16[84,512]{1,0:T(8,128)(2,1)S(1)}, bf16[84,512]{1,0:T(8,128)(2,1)S(1)}, u32[]{:S(2)}, u32[]{:S(2)}) collective-permute-start(bf16[84,512]{1,0:T(8,128)(2,1)S(1)} %mean.1.refs_0_), channel_id=1, source_target_pairs={{0,15},{1,2},{2,1},{3,4},{4,3},{5,6},{6,5},{7,8},{8,7},{9,10},{10,... | collective-permute-start | bytes 258056 | tf_op jit(solution)/shard_map/ppermute | solution.py:50
  25.3 0.0 collective-permute-done.5.refs_9_
  25.4 8.0 %own.1 = (f32[256,1024]{1,0:T(8,128)S(1)}, bf16[256,1024]{1,0:T(8,128)(2,1)S(1)}, bf16[512,2048]{1,0:T(8,128)(2,1)S(1)}, f32[256,1024]{1,0:T(8,128)S(1)}, f32[25...) custom-call(bf16[84,512]{1,0:T(8,128)(2,1)S(1)} %mean.1.refs_0_, f32[256,512]{1,0:T(8,128)S(1)} %get-tuple-element.40.refs_1_, ...), custom_call_target="tpu_custom_call" | custom-call | flops 5000000000 | bytes 30000000 | tf_op jit(solution)/shard_map/own/pallas_call | solution.py:412
  33.4 0.0 copy-start.6
  33.4 0.0 copy-start.7
  33.4 0.0 copy-start.10
  33.4 0.0 copy-start.14
  33.4 0.1 collective-permute-start.6
  33.5 0.0 collective-permute-done.7.refs_0_
  33.5 0.0 collective-permute-done.8.refs_7_
  33.5 4.4 %far.1.refs_1_ = bf16[512,2048]{1,0:T(8,128)(2,1)S(1)} custom-call(bf16[84,512]{1,0:T(8,128)(2,1)S(1)} %collective-permute-done.7.refs_0_, bf16[84,1024]{1,0:T(8,128)(2,1)S(1)} %copy-done.9, bf16[1024,1024]{1,0:T(8,128)(2,1)S(1)} %copy-done.3, bf16[1024,1024]{1,0:T(8,128)(2,1)S(1)} %copy-done.4, bf16[1024,1024]{1,0:T(8,128)(2,1)S(1)} %copy-done.5, ...), custom_call_target="tpu_custom_call" | custom-call | flops 30000001024 | bytes 180000000 | tf_op jit(solution)/shard_map/far/pallas_call | solution.py:412
  37.9 0.0 collective-permute-done.6.refs_0_
  38.0 0.0 copy-start.1
  38.0 9.6 %attend.1.refs_0_ = bf16[84,256]{1,0:T(8,128)(2,1)S(1)} custom-call(bf16[512,2048]{1,0:T(8,128)(2,1)S(1)} %collective-permute-done.6.refs_0_, bf16[512,2048]{1,0:T(8,128)(2,1)S(1)} %far.1.refs_1_, f32[256,1024]{1,0:T(8,128)S(1)} %get-tuple-element.48.refs_2_, f32[256,1024]{1,0:T(8,128)S(1)} %get-tuple-element.49.refs_3_, ...), custom_call_target="tpu_custom_call" | custom-call | flops 6000000000 | bytes 36000000 | tf_op jit(solution)/shard_map/attend/pallas_call | solution.py:412
  47.6 1.4 %collective-permute-start.9 = (bf16[84,256]{1,0:T(8,128)(2,1)S(1)}, bf16[84,256]{1,0:T(8,128)(2,1)S(1)}, u32[]{:S(2)}, u32[]{:S(2)}) collective-permute-start(bf16[84,256]{1,0:T(8,128)(2,1)S(1)} %attend.1.refs_0_), channel_id=1, source_target_pairs={{0,16},{16,0},{1,17},{17,1},{2,18},{18,2},{3,19},{19,3},{4,20},{20... | collective-permute-start | bytes 129032 | tf_op jit(solution)/shard_map/ppermute | solution.py:38
  49.0 0.6 decode_own.1.refs_0_
  49.6 2.2 %collective-permute-done.9 = bf16[84,256]{1,0:T(8,128)(2,1)S(1)} collective-permute-done((bf16[84,256]{1,0:T(8,128)(2,1)S(1)}, bf16[84,256]{1,0:T(8,128)(2,1)S(1)}, u32[]{:S(2)}, u32[]{:S(2)}) %collective-permute-start.9) | collective-permute-done | bytes 43040 | tf_op jit(solution)/shard_map/ppermute | solution.py:38
  51.7 0.1 collective-permute-start.10
  51.8 5.7 %collective-permute-start.11 = (bf16[84,512]{1,0:T(8,128)(2,1)S(1)}, bf16[84,512]{1,0:T(8,128)(2,1)S(1)}, u32[]{:S(2)}, u32[]{:S(2)}) collective-permute-start(bf16[84,512]{1,0:T(8,128)(2,1)S(1)} %pad_maximum_fusion.refs_1_), channel_id=1, source_target_pairs={{0,15},{1,2},{2,1},{3,4},{4,3},{5,6},{6,5},{7,8},{8,7},{9,10},{10,... | collective-permute-start | bytes 258056 | tf_op jit(solution)/shard_map/ppermute | solution.py:50
  57.5 0.0 collective-permute-done.10.refs_2_
  57.5 1.3 %decode_near.1.refs_0_ = f32[84,2048]{1,0:T(8,128)S(1)} custom-call(f32[84,2048]{1,0:T(8,128)S(1)} %decode_own.1.refs_0_, bf16[84,512]{1,0:T(8,128)(2,1)S(1)} %pad_maximum_fusion.refs_1_, bf16[84,512]{1,0:T(8,128)(2,1)S(1)} %collective-permute-done.10.refs_2_, s32[3,16,128]{2,1,0:T(8,128)S(1)} %copy-done.1), custom_call_target="tpu_custom_call" | custom-call | flops 50000000 | bytes 300000 | tf_op jit(solution)/shard_map/decode_near/pallas_call | solution.py:412
  58.8 0.9 %collective-permute-done.11.refs_1_ = bf16[84,512]{1,0:T(8,128)(2,1)S(1)} collective-permute-done((bf16[84,512]{1,0:T(8,128)(2,1)S(1)}, bf16[84,512]{1,0:T(8,128)(2,1)S(1)}, u32[]{:S(2)}, u32[]{:S(2)}) %collective-permute-start.11) | collective-permute-done | bytes 86048 | tf_op jit(solution)/shard_map/ppermute | solution.py:50
  59.7 2.0 %decode_far.1 = f32[84,16,128]{2,1,0:T(8,128)} custom-call(f32[84,2048]{1,0:T(8,128)S(1)} %decode_near.1.refs_0_, bf16[84,512]{1,0:T(8,128)(2,1)S(1)} %collective-permute-done.11.refs_1_, s32[3,16,128]{2,1,0:T(8,128)S(1)} %copy-done.1), custom_call_target="tpu_custom_call" | custom-call | flops 50000000 | bytes 300000 | tf_op jit(solution)/shard_map/decode_far/pallas_call | solution.py:412
  (25 shorter events, 0.1 us)
Async XLA Ops:
  0.0 1.0 %copy-start = (bf16[84,16,128]{2,1,0:T(8,128)(2,1)S(1)}, bf16[84,16,128]{2,1,0:T(8,128)(2,1)}, u32[]{:S(2)}) copy-start(bf16[84,16,128]{2,1,0:T(8,128)(2,1)} %refs_0_) | copy-start | bytes 1032196
  0.0 1.0 %copy-start.12 = (s32[16,256]{1,0:T(8,128)S(1)}, s32[16,256]{1,0:T(8,128)}, u32[]{:S(2)}) copy-start(s32[16,256]{1,0:T(8,128)} %refs_2_.4) | copy-start | bytes 49156
  0.0 1.0 %copy-start.15 = (s32[256]{0:T(256)S(1)}, s32[256]{0:T(256)}, u32[]{:S(2)}) copy-start(s32[256]{0:T(256)} %param.20) | copy-start | bytes 3076
  0.0 9.2 %copy-start.8 = (bf16[256,1024]{1,0:T(8,128)(2,1)S(1)}, bf16[256,1024]{1,0:T(8,128)(2,1)}, u32[]{:S(2)}) copy-start(bf16[256,1024]{1,0:T(8,128)(2,1)} %refs_8_.2) | copy-start | bytes 1572868
  1.5 13.9 %collective-permute-start = (bf16[84,256]{1,0:T(8,128)(2,1)S(1)}, bf16[84,256]{1,0:T(8,128)(2,1)S(1)}, u32[]{:S(2)}, u32[]{:S(2)}) collective-permute-start(bf16[84,256]{1,0:T(8,128)(2,1)S(1)} %get-tuple-element.30), channel_id=1, source_target_pairs={{0,1},{1,0},{2,3},{3,2},{4,5},{5,4},{6,7},{7,6},{8,9},{9,8},{10,11... | collective-permute-start | bytes 129032 | tf_op jit(solution)/shard_map/ppermute | solution.py:45
  2.0 13.4 %collective-permute-start.1 = (bf16[84,256]{1,0:T(8,128)(2,1)S(1)}, bf16[84,256]{1,0:T(8,128)(2,1)S(1)}, u32[]{:S(2)}, u32[]{:S(2)}) collective-permute-start(bf16[84,256]{1,0:T(8,128)(2,1)S(1)} %get-tuple-element.31), channel_id=1, source_target_pairs={{0,15},{1,2},{2,1},{3,4},{4,3},{5,6},{6,5},{7,8},{8,7},{9,10},{10,... | collective-permute-start | bytes 129032 | tf_op jit(solution)/shard_map/ppermute | solution.py:50
  7.7 5.4 %collective-permute-start.2 = (s32[16,256]{1,0:T(8,128)S(1)}, s32[16,256]{1,0:T(8,128)S(1)}, u32[]{:S(2)}, u32[]{:S(2)}) collective-permute-start(s32[16,256]{1,0:T(8,128)S(1)} %get-tuple-element.32.refs_0_.refs_2_), channel_id=1, source_target_pairs={{0,16},{16,0},{1,17},{17,1},{2,18},{18,2},{3,19},{19,3},{4,20},{20... | collective-permute-start | bytes 49160 | tf_op jit(solution)/shard_map/ppermute | solution.py:38
  9.2 16.1 %collective-permute-start.5 = (bf16[256,1024]{1,0:T(8,128)(2,1)S(1)}, bf16[256,1024]{1,0:T(8,128)(2,1)S(1)}, u32[]{:S(2)}, u32[]{:S(2)}) collective-permute-start(bf16[256,1024]{1,0:T(8,128)(2,1)S(1)} %copy-done.8), channel_id=1, source_target_pairs={{0,16},{16,0},{1,17},{17,1},{2,18},{18,2},{3,19},{19,3},{4,20},{20... | collective-permute-start | bytes 1572872 | tf_op jit(solution)/shard_map/ppermute | solution.py:38
  9.7 12.6 %collective-permute-start.4 = (bf16[256,1024]{1,0:T(8,128)(2,1)S(1)}, bf16[256,1024]{1,0:T(8,128)(2,1)S(1)}, u32[]{:S(2)}, u32[]{:S(2)}) collective-permute-start(bf16[256,1024]{1,0:T(8,128)(2,1)S(1)} %copy-done.8), channel_id=1, source_target_pairs={{0,15},{1,2},{2,1},{3,4},{4,3},{5,6},{6,5},{7,8},{8,7},{9,10},{10,... | collective-permute-start | bytes 1572872 | tf_op jit(solution)/shard_map/ppermute | solution.py:50
  10.7 6.5 %copy-start.11 = (s32[32,256]{1,0:T(8,128)S(1)}, s32[32,256]{1,0:T(8,128)}, u32[]{:S(2)}) copy-start(s32[32,256]{1,0:T(8,128)} %refs_0_.1) | copy-start | bytes 98308
  10.7 6.5 %copy-start.16 = (s32[256]{0:T(256)S(1)}, s32[256]{0:T(256)}, u32[]{:S(2)}) copy-start(s32[256]{0:T(256)} %param.22) | copy-start | bytes 3076
  15.7 6.6 %collective-permute-start.3 = (bf16[84,512]{1,0:T(8,128)(2,1)S(1)}, bf16[84,512]{1,0:T(8,128)(2,1)S(1)}, u32[]{:S(2)}, u32[]{:S(2)}) collective-permute-start(bf16[84,512]{1,0:T(8,128)(2,1)S(1)} %get-tuple-element.42), channel_id=1, source_target_pairs={{0,16},{16,0},{1,17},{17,1},{2,18},{18,2},{3,19},{19,3},{4,20},{20... | collective-permute-start | bytes 258056 | tf_op jit(solution)/shard_map/ppermute | solution.py:38
  17.2 8.1 %copy-start.2 = (bf16[1024,1024]{1,0:T(8,128)(2,1)S(1)}, bf16[1024,1024]{1,0:T(8,128)(2,1)}, u32[]{:S(2)}) copy-start(bf16[1024,1024]{1,0:T(8,128)(2,1)} %refs_4_.2) | copy-start | bytes 6291460
  17.2 8.1 %copy-start.3 = (bf16[1024,1024]{1,0:T(8,128)(2,1)S(1)}, bf16[1024,1024]{1,0:T(8,128)(2,1)}, u32[]{:S(2)}) copy-start(bf16[1024,1024]{1,0:T(8,128)(2,1)} %refs_2_.6) | copy-start | bytes 6291460
  17.2 8.1 %copy-start.4 = (bf16[1024,1024]{1,0:T(8,128)(2,1)S(1)}, bf16[1024,1024]{1,0:T(8,128)(2,1)}, u32[]{:S(2)}) copy-start(bf16[1024,1024]{1,0:T(8,128)(2,1)} %refs_3_.4) | copy-start | bytes 6291460
  17.3 8.1 %copy-start.5 = (bf16[1024,1024]{1,0:T(8,128)(2,1)S(1)}, bf16[1024,1024]{1,0:T(8,128)(2,1)}, u32[]{:S(2)}) copy-start(bf16[1024,1024]{1,0:T(8,128)(2,1)} %refs_4_.3) | copy-start | bytes 6291460
  17.3 8.1 %copy-start.9 = (bf16[84,1024]{1,0:T(8,128)(2,1)S(1)}, bf16[84,1024]{1,0:T(8,128)(2,1)}, u32[]{:S(2)}) copy-start(bf16[84,1024]{1,0:T(8,128)(2,1)} %refs_1_.2) | copy-start | bytes 516100
  17.3 8.1 %copy-start.13 = (f32[1024]{0:T(1024)S(1)}, f32[1024]{0:T(1024)}, u32[]{:S(2)}) copy-start(f32[1024]{0:T(1024)} %param.32) | copy-start | bytes 12292
  22.4 11.2 %collective-permute-start.8 = (bf16[256,1024]{1,0:T(8,128)(2,1)S(1)}, bf16[256,1024]{1,0:T(8,128)(2,1)S(1)}, u32[]{:S(2)}, u32[]{:S(2)}) collective-permute-start(bf16[256,1024]{1,0:T(8,128)(2,1)S(1)} %collective-permute-done.4.refs_6_), channel_id=1, source_target_pairs={{0,16},{16,0},{1,17},{17,1},{2,18},{18,2},{3,19},{19,3},{4,20},{20... | collective-permute-start | bytes 1572872 | tf_op jit(solution)/shard_map/ppermute | solution.py:38
  22.5 11.0 %collective-permute-start.7 = (bf16[84,512]{1,0:T(8,128)(2,1)S(1)}, bf16[84,512]{1,0:T(8,128)(2,1)S(1)}, u32[]{:S(2)}, u32[]{:S(2)}) collective-permute-start(bf16[84,512]{1,0:T(8,128)(2,1)S(1)} %mean.1.refs_0_), channel_id=1, source_target_pairs={{0,15},{1,2},{2,1},{3,4},{4,3},{5,6},{6,5},{7,8},{8,7},{9,10},{10,... | collective-permute-start | bytes 258056 | tf_op jit(solution)/shard_map/ppermute | solution.py:50
  33.4 4.6 %copy-start.6 = (bf16[1024,1024]{1,0:T(8,128)(2,1)S(1)}, bf16[1024,1024]{1,0:T(8,128)(2,1)}, u32[]{:S(2)}) copy-start(bf16[1024,1024]{1,0:T(8,128)(2,1)} %refs_8_.3) | copy-start | bytes 6291460
  33.4 4.6 %copy-start.7 = (bf16[1024,1024]{1,0:T(8,128)(2,1)S(1)}, bf16[1024,1024]{1,0:T(8,128)(2,1)}, u32[]{:S(2)}) copy-start(bf16[1024,1024]{1,0:T(8,128)(2,1)} %refs_9_.1) | copy-start | bytes 6291460
  33.4 4.6 %copy-start.10 = (bf16[1024,84]{0,1:T(8,128)(2,1)S(1)}, bf16[1024,84]{0,1:T(8,128)(2,1)}, u32[]{:S(2)}) copy-start(bf16[1024,84]{0,1:T(8,128)(2,1)} %param.31) | copy-start | bytes 516100
  33.4 4.6 %copy-start.14 = (f32[1024]{0:T(1024)S(1)}, f32[1024]{0:T(1024)}, u32[]{:S(2)}) copy-start(f32[1024]{0:T(1024)} %param.33) | copy-start | bytes 12292
  33.4 4.5 %collective-permute-start.6 = (bf16[512,2048]{1,0:T(8,128)(2,1)S(1)}, bf16[512,2048]{1,0:T(8,128)(2,1)S(1)}, u32[]{:S(2)}, u32[]{:S(2)}) collective-permute-start(bf16[512,2048]{1,0:T(8,128)(2,1)S(1)} %get-tuple-element.45), channel_id=1, source_target_pairs={{0,1},{1,0},{2,3},{3,2},{4,5},{5,4},{6,7},{7,6},{8,9},{9,8},{10,11... | collective-permute-start | bytes 6291464 | tf_op jit(solution)/shard_map/ppermute | solution.py:45
  38.0 11.0 %copy-start.1 = (s32[3,16,128]{2,1,0:T(8,128)S(1)}, s32[3,16,128]{2,1,0:T(8,128)}, u32[]{:S(2)}) copy-start(s32[3,16,128]{2,1,0:T(8,128)} %refs_2_.8) | copy-start | bytes 73732
  47.6 4.1 %collective-permute-start.9 = (bf16[84,256]{1,0:T(8,128)(2,1)S(1)}, bf16[84,256]{1,0:T(8,128)(2,1)S(1)}, u32[]{:S(2)}, u32[]{:S(2)}) collective-permute-start(bf16[84,256]{1,0:T(8,128)(2,1)S(1)} %attend.1.refs_0_), channel_id=1, source_target_pairs={{0,16},{16,0},{1,17},{17,1},{2,18},{18,2},{3,19},{19,3},{4,20},{20... | collective-permute-start | bytes 129032 | tf_op jit(solution)/shard_map/ppermute | solution.py:38
  51.7 5.8 %collective-permute-start.10 = (bf16[84,512]{1,0:T(8,128)(2,1)S(1)}, bf16[84,512]{1,0:T(8,128)(2,1)S(1)}, u32[]{:S(2)}, u32[]{:S(2)}) collective-permute-start(bf16[84,512]{1,0:T(8,128)(2,1)S(1)} %pad_maximum_fusion.refs_1_), channel_id=1, source_target_pairs={{0,1},{1,0},{2,3},{3,2},{4,5},{5,4},{6,7},{7,6},{8,9},{9,8},{10,11... | collective-permute-start | bytes 258056 | tf_op jit(solution)/shard_map/ppermute | solution.py:45
  51.8 7.9 %collective-permute-start.11 = (bf16[84,512]{1,0:T(8,128)(2,1)S(1)}, bf16[84,512]{1,0:T(8,128)(2,1)S(1)}, u32[]{:S(2)}, u32[]{:S(2)}) collective-permute-start(bf16[84,512]{1,0:T(8,128)(2,1)S(1)} %pad_maximum_fusion.refs_1_), channel_id=1, source_target_pairs={{0,15},{1,2},{2,1},{3,4},{4,3},{5,6},{6,5},{7,8},{8,7},{9,10},{10,... | collective-permute-start | bytes 258056 | tf_op jit(solution)/shard_map/ppermute | solution.py:50

commit v5 on v4

--- a/solution.py
+++ b/solution.py
@@ -290,10 +290,10 @@
         store(at, *(jnp.where(first, a[:nodes], a[nodes:]) for a in (values, sums, peaks)))
 
 
-def far_kernel(mean_ref, w_embed, w_encode, w_key, w_value, gain, *refs):
-    feats, pair_ref = [feat.now() for feat in refs[:-1]], refs[-1]
+def far_kernel(at, mean_ref, w_embed, w_encode, w_key, w_value, gain, feat, pair_ref):
     sector_rows(
-        mean_ref, gain.now(), w_embed, w_encode, None, w_key, w_value, feats, None, None, pair_ref
+        mean_ref.at[:, at], gain.now(), w_embed, w_encode, None, w_key, w_value, [feat.now()],
+        None, None, pair_ref,
     )
 
 
@@ -317,7 +317,13 @@
 
 
 def attend_kernel(
-    near_ref, far_ref, bias_ref, latent_ref, query_ref, mixed_ref, peak_ref, sum_ref,
+    bands, near_ref, *refs
+):
+    attend_rows([near_ref, *refs[:bands]], *refs[bands:])
+
+
+def attend_rows(
+    pairs, bias_ref, latent_ref, query_ref, mixed_ref, peak_ref, sum_ref,
     w_output, w_decode, gain_dec, w_read, out_ref, score_ref, weight_ref, context_ref,
 ):
     nodes, features = latent_ref.shape
@@ -327,7 +333,7 @@
         values = values + fade * mixed_ref[:, at]
         context_ref[:, at] = (values / (sums + fade * sum_ref[:, at])).astype(BF16)
 
-    attention(query_ref, [near_ref, far_ref], bias_ref, score_ref, weight_ref, peak_ref, store)
+    attention(query_ref, pairs, bias_ref, score_ref, weight_ref, peak_ref, store)
     mixed = latent_ref[...] + jnp.dot(context_ref[...], w_output[...], preferred_element_type=F32)
     normed_out = layer_norm(mixed, gain_dec.now()[...]).astype(BF16)
     decoded = silu(jnp.dot(normed_out, w_decode[...], preferred_element_type=F32)).astype(BF16)
@@ -336,30 +342,44 @@
     ).astype(BF16)
 
 
-def decode_kernel(bands, sectors, parts, dec, reads, base_ref, out_ref, wide=None, signals=None):
+def cell_counts(block, member, part, row, nodes):
+    lanes = 2 * block.shape[2]
+    iota = lax.broadcasted_iota(jnp.int32, (nodes, lanes), 0).astype(F32).astype(BF16)
+    one, none = jnp.ones((nodes, lanes), BF16), jnp.zeros((nodes, lanes), BF16)
+    code = jnp.where(block == part, member, -1.0)
+    code = jnp.concatenate([code[:, row], code[:, row + 1]], axis=1).astype(BF16)
+    counts = none
+    for slot in range(code.shape[0]):
+        counts = counts + jnp.where(iota == code[slot : slot + 1], one, none)
+    return counts
+
+
+def decode_kernel(bands, sectors, parts, later, dec, reads, base_ref, out_ref, *refs):
     dec_ref = dec.now()
     rows, cols = dec_ref.shape[1:]
     nodes = parts[0][1].stop - parts[0][1].start
-    iota = lax.broadcasted_iota(jnp.int32, (nodes, 2 * cols), 0).astype(F32).astype(BF16)
-    one = jnp.ones((nodes, 2 * cols), BF16)
-    none = jnp.zeros((nodes, 2 * cols), BF16)
     block, member = place_of(dec_ref[...], nodes, bands, sectors)
-    copies, half = [], rows // 2
     for row in range(0, rows, 2):
         at = slice(row * cols, (row + 2) * cols)
         update = None
         for (part, there), read_ref in zip(parts, reads):
-            code = jnp.where(block == part, member, -1.0)
-            code = jnp.concatenate([code[:, row], code[:, row + 1]], axis=1).astype(BF16)
-            counts = none
-            for slot in range(code.shape[0]):
-                counts = counts + jnp.where(iota == code[slot : slot + 1], one, none)
+            counts = cell_counts(block, member, part, row, nodes)
             share = jnp.dot(read_ref[:, there], counts, preferred_element_type=F32)
             update = share if update is None else update + share
-        update = base_ref[:, at].astype(F32) + update / 3.0
-        if wide is None:
-            out_ref[:, at] = update
-            continue
+        out_ref[:, at] = base_ref[:, at].astype(F32) + update / 3.0
+        for index, part in enumerate(later):
+            refs[0][index * nodes : (index + 1) * nodes, at] = cell_counts(
+                block, member, part, row, nodes
+            )
+
+
+def finish_kernel(base_ref, read_ref, counts_ref, out_ref, wide, signals):
+    rows, cols = wide.shape[1:]
+    copies, half = [], rows // 2
+    for row in range(0, rows, 2):
+        at = slice(row * cols, (row + 2) * cols)
+        update = jnp.dot(read_ref[...], counts_ref[:, at], preferred_element_type=F32)
+        update = base_ref[:, at] + update / 3.0
         wide[:, row, :] = update[:, :cols]
         wide[:, row + 1, :] = update[:, cols:]
         if (row + 2) % half == 0:
@@ -519,20 +539,25 @@
         micros=10,
     )
     pair_near = from_near(pair)
-    pair_far = call(
-        "far",
-        far_kernel,
-        shape((sector_nodes, 2 * features), BF16),
-        (mean_far, after(w_embed, pair), w_encode, w_key, w_value),
-        late=(norm_attn[None], *feats_far),
-        mib=16,
-        micros=60,
-    )
+    pairs_far = []
+    for band, source in enumerate(feats_far):
+        at = slice(band * nodes, (band + 1) * nodes)
+        pairs_far.append(
+            call(
+                "far",
+                functools.partial(far_kernel, at),
+                shape((nodes, 2 * features), BF16),
+                (mean_far, after(w_embed, pair, *pairs_far), w_encode, w_key, w_value),
+                late=(norm_attn[None], source),
+                mib=16,
+                micros=60 if band else 0.1,
+            )
+        )
     readout = call(
         "attend",
-        attend_kernel,
+        functools.partial(attend_kernel, bands),
         shape((variables, nodes), BF16),
-        (pair_near, pair_far, bias_rest, latent, query, mixed, peak, total, w_output, w_decode),
+        (pair_near, *pairs_far, bias_rest, latent, query, mixed, peak, total, w_output, w_decode),
         late=(norm_dec[None], w_readout.T),
         scratch=[
             pltpu.VMEM((SLOTS, 2 * nodes, 2 * sector_nodes), F32),
@@ -547,7 +572,7 @@
     spots = [slice(band * nodes, (band + 1) * nodes) for band in range(bands)]
     own_sums = call(
         "decode_own",
-        lambda read, base, dec, out: decode([(0, spots[0])], dec, [read], base, out),
+        lambda read, base, dec, out: decode([(0, spots[0])], [], dec, [read], base, out),
         sums,
         (readout, flat),
         late=(dec_src,),
@@ -557,25 +582,24 @@
     reads = after(reads, own_sums)
     read_far = from_far(reads)
     read_near = from_near(reads)
-    near_sums = call(
+    far_blocks = [2 * bands + band for band in range(bands)]
+    near_sums, far_counts = call(
         "decode_near",
-        lambda base, own, near, dec, out: decode(
+        lambda base, own, near, dec, out, counts: decode(
             list(enumerate(spots))[1:] + list(enumerate(spots, bands)),
-            dec, [own] * (bands - 1) + [near] * bands, base, out,
+            far_blocks, dec, [own] * (bands - 1) + [near] * bands, base, out, counts,
         ),
-        sums,
+        [sums, shape((sector_nodes, cells), BF16)],
         (own_sums, reads, read_near),
         late=(dec_src,),
+        mib=12,
         micros=0.1,
     )
     return call(
-        "decode_far",
-        lambda base, far, dec, out, *more: decode(
-            list(enumerate(spots, 2 * bands)), dec, [far] * bands, base, out, *more
-        ),
+        "finish",
+        finish_kernel,
         shape(grid_state.shape, F32),
-        (near_sums, read_far),
-        late=(dec_src,),
+        (near_sums, read_far, far_counts),
         scratch=[pltpu.VMEM(grid_state.shape, F32), pltpu.SemaphoreType.DMA((2,))],
         out_memory=pltpu.HBM,
         micros=0.1,

time: 62 us -> 60.8 us (0.981)
  starting transfers between devices: 19.9 us -> 17.4 us
  Pallas kernels: 34.4 us -> 35.5 us
    ppermute x4, starting transfers between devices: 14.1 us -> 11.7 us  [from_far(): lax.ppermute(value, 'lon', [(i, (i - 1 + 2 * (i % 2)) % count) for i in r...]
    pallas_call x14 -> x15, Pallas kernels: 34.4 us -> 35.5 us  [call(): pl.pallas_call(run, name=name, out_shape=outs, in_specs=specs, out_specs=...]
  transfers between devices with their start and end apart: 12 -> 12, of which waited for: 3 -> 3; matrix products, arithmetic and copies ran while one was open for 0% -> 0% of each run, Pallas kernels for 36% -> 40%
where the time goes in v5:
time: 60.8 us; the launch traced here: 60.6 us
  Pallas kernels  35.5 us (58%)
  starting transfers between devices  17.4 us (29%)
  waiting for transfers between devices  6.09 us (10%)
  local copies, waits for them, and re-layouts  1.05 us (2%)
    pallas_call x15, Pallas kernels, call(): pl.pallas_call(run, name=name, out_shape=outs, in_specs=specs, out_specs=...  35.5 us
    ppermute x4, starting transfers between devices, from_far(): lax.ppermute(value, 'lon', [(i, (i - 1 + 2 * (i % 2)) % count) for i in r...  11.7 us
    ppermute x5, starting transfers between devices, from_bands(): lax.ppermute(value, 'lat', [(i, (i - step) % count) for i in range(count)])  5.12 us
    ppermute x5, waiting for transfers between devices, from_bands(): lax.ppermute(value, 'lat', [(i, (i - step) % count) for i in range(count)])  5.02 us
  transfers between devices with their start and end apart: 12, of which 3 were waited for; matrix products, arithmetic and copies ran while one was open for 0% of the time, Pallas kernels for 40%

profile of v5, /device:TPU:0, one launch (start us, length us, event | category | flops | bytes accessed | tf_op | source)
XLA Modules:
  0.0 60.6 jit_solution(17692412064271682083)
XLA Ops:
  0.0 1.0 %copy-done.3 = bf16[84,16,128]{2,1,0:T(8,128)(2,1)S(1)} copy-done((bf16[84,16,128]{2,1,0:T(8,128)(2,1)S(1)}, bf16[84,16,128]{2,1,0:T(8,128)(2,1)}, u32[]{:S(2)}) %copy-start.3) | copy-done | bytes 344088
  1.0 0.5 prep.1
  1.5 0.5 collective-permute-start
  2.0 5.7 %collective-permute-start.1 = (bf16[84,256]{1,0:T(8,128)(2,1)S(1)}, bf16[84,256]{1,0:T(8,128)(2,1)S(1)}, u32[]{:S(2)}, u32[]{:S(2)}) collective-permute-start(bf16[84,256]{1,0:T(8,128)(2,1)S(1)} %get-tuple-element.34), channel_id=1, source_target_pairs={{0,15},{1,2},{2,1},{3,4},{4,3},{5,6},{6,5},{7,8},{8,7},{9,10},{10,... | collective-permute-start | bytes 129032 | tf_op jit(solution)/shard_map/ppermute | solution.py:50
  7.7 1.5 %collective-permute-start.2 = (s32[16,256]{1,0:T(8,128)S(1)}, s32[16,256]{1,0:T(8,128)S(1)}, u32[]{:S(2)}, u32[]{:S(2)}) collective-permute-start(s32[16,256]{1,0:T(8,128)S(1)} %get-tuple-element.35.refs_0_.refs_2_), channel_id=1, source_target_pairs={{0,16},{16,0},{1,17},{17,1},{2,18},{18,2},{3,19},{19,3},{4,20},{20... | collective-permute-start | bytes 49160 | tf_op jit(solution)/shard_map/ppermute | solution.py:38
  9.2 0.5 collective-permute-start.5
  9.7 0.0 collective-permute-start.4
  9.7 0.9 %flat.1.refs_1_ = bf16[84,2048]{1,0:T(8,128)(2,1)S(1)} custom-call(bf16[84,16,128]{2,1,0:T(8,128)(2,1)S(1)} %copy-done.3), custom_call_target="tpu_custom_call" | custom-call | flops 50000000 | bytes 300000 | tf_op jit(solution)/shard_map/flat/pallas_call | solution.py:432
  10.7 0.0 copy-start.12
  10.7 0.0 copy-start.16
  10.7 2.3 %encode.2 = (f32[84,256]{1,0:T(8,128)S(1)}, bf16[512,256]{1,0:T(8,128)(2,1)S(1)}) custom-call(s32[16,256]{1,0:T(8,128)S(1)} %get-tuple-element.35.refs_0_.refs_2_, bf16[84,2048]{1,0:T(8,128)(2,1)S(1)} %flat.1.refs_1_), custom_call_target="tpu_custom_call" | custom-call | flops 1500000000 | bytes 9000000 | tf_op jit(solution)/shard_map/encode/pallas_call | solution.py:432
  13.1 0.0 collective-permute-done.2.refs_0_.refs_3_
  13.1 2.3 %encode.3 = (f32[84,256]{1,0:T(8,128)S(1)}, bf16[512,256]{1,0:T(8,128)(2,1)S(1)}) custom-call(s32[16,256]{1,0:T(8,128)S(1)} %collective-permute-done.2.refs_0_.refs_3_, bf16[84,2048]{1,0:T(8,128)(2,1)S(1)} %flat.1.refs_1_), custom_call_target="tpu_custom_call" | custom-call | flops 50000000 | bytes 300000 | tf_op jit(solution)/shard_map/encode/pallas_call | solution.py:432
  15.4 0.0 collective-permute-done.refs_0_
  15.4 0.0 collective-permute-done.1.refs_1_
  15.4 0.2 rim.1
  15.7 1.6 %collective-permute-start.3 = (bf16[84,512]{1,0:T(8,128)(2,1)S(1)}, bf16[84,512]{1,0:T(8,128)(2,1)S(1)}, u32[]{:S(2)}, u32[]{:S(2)}) collective-permute-start(bf16[84,512]{1,0:T(8,128)(2,1)S(1)} %get-tuple-element.45), channel_id=1, source_target_pairs={{0,16},{16,0},{1,17},{17,1},{2,18},{18,2},{3,19},{19,3},{4,20},{20... | collective-permute-start | bytes 258056 | tf_op jit(solution)/shard_map/ppermute | solution.py:38
  17.2 0.0 copy-start.2
  17.3 0.0 copy-start.4
  17.3 0.0 copy-start.6
  17.3 0.0 copy-start.7
  17.3 2.2 %bias.1 = (f32[256,512]{1,0:T(8,128)S(1)}, f32[256,1024]{1,0:T(8,128)S(1)}) custom-call(s32[32,256]{1,0:T(8,128)S(1)} %copy-done.12, s32[1,256]{1,0:T(1,128)S(1)} %bitcast.11), custom_call_target="tpu_custom_call" | custom-call | flops 15000000512 | bytes 90000000 | tf_op jit(solution)/shard_map/bias/pallas_call | solution.py:432
  19.5 2.8 %collective-permute-done.3.refs_1_ = bf16[84,512]{1,0:T(8,128)(2,1)S(1)} collective-permute-done((bf16[84,512]{1,0:T(8,128)(2,1)S(1)}, bf16[84,512]{1,0:T(8,128)(2,1)S(1)}, u32[]{:S(2)}, u32[]{:S(2)}) %collective-permute-start.3) | collective-permute-done | bytes 86048 | tf_op jit(solution)/shard_map/ppermute | solution.py:38
  22.3 0.0 collective-permute-done.4.refs_6_
  22.4 0.2 collective-permute-start.8
  22.5 2.8 %collective-permute-start.7 = (bf16[84,512]{1,0:T(8,128)(2,1)S(1)}, bf16[84,512]{1,0:T(8,128)(2,1)S(1)}, u32[]{:S(2)}, u32[]{:S(2)}) collective-permute-start(bf16[84,512]{1,0:T(8,128)(2,1)S(1)} %mean.1.refs_0_), channel_id=1, source_target_pairs={{0,15},{1,2},{2,1},{3,4},{4,3},{5,6},{6,5},{7,8},{8,7},{9,10},{10,... | collective-permute-start | bytes 258056 | tf_op jit(solution)/shard_map/ppermute | solution.py:50
  25.3 0.0 collective-permute-done.5.refs_9_
  25.4 8.0 %own.1 = (f32[256,1024]{1,0:T(8,128)S(1)}, bf16[256,1024]{1,0:T(8,128)(2,1)S(1)}, bf16[512,2048]{1,0:T(8,128)(2,1)S(1)}, f32[256,1024]{1,0:T(8,128)S(1)}, f32[25...) custom-call(bf16[84,512]{1,0:T(8,128)(2,1)S(1)} %mean.1.refs_0_, f32[256,512]{1,0:T(8,128)S(1)} %get-tuple-element.43.refs_1_, ...), custom_call_target="tpu_custom_call" | custom-call | flops 5000000000 | bytes 30000000 | tf_op jit(solution)/shard_map/own/pallas_call | solution.py:432
  33.4 0.1 collective-permute-start.6
  33.5 0.0 collective-permute-done.7.refs_0_
  33.5 2.4 %far.2.refs_1_ = bf16[256,2048]{1,0:T(8,128)(2,1)S(1)} custom-call(bf16[84,512]{1,0:T(8,128)(2,1)S(1)} %collective-permute-done.7.refs_0_, bf16[84,1024]{1,0:T(8,128)(2,1)S(1)} %copy-done.4, bf16[1024,1024]{1,0:T(8,128)(2,1)S(1)} %copy-done, bf16[1024,1024]{1,0:T(8,128)(2,1)S(1)} %copy-done.1, bf16[1024,1024]{1,0:T(8,128)(2,1)S(1)} %copy-done.2, ...), custom_call_target="tpu_custom_call" | custom-call | flops 50000000 | bytes 300000 | tf_op jit(solution)/shard_map/far/pallas_call | solution.py:432
  35.9 0.0 copy-start.8
  35.9 0.0 copy-start.9
  36.0 0.0 copy-start.11
  36.0 0.0 copy-start.14
  36.0 2.7 %far.3.refs_2_ = bf16[256,2048]{1,0:T(8,128)(2,1)S(1)} custom-call(bf16[84,512]{1,0:T(8,128)(2,1)S(1)} %collective-permute-done.7.refs_0_, bf16[84,1024]{1,0:T(8,128)(2,1)S(1)} %copy-done.4, bf16[1024,1024]{1,0:T(8,128)(2,1)S(1)} %copy-done, bf16[1024,1024]{1,0:T(8,128)(2,1)S(1)} %copy-done.1, bf16[1024,1024]{1,0:T(8,128)(2,1)S(1)} %copy-done.2, ...), custom_call_target="tpu_custom_call" | custom-call | flops 30000001024 | bytes 180000000 | tf_op jit(solution)/shard_map/far/pallas_call | solution.py:432
  38.7 0.0 collective-permute-done.6.refs_0_
  38.7 0.0 copy-start.5
  38.7 9.3 %attend.1.refs_0_ = bf16[84,256]{1,0:T(8,128)(2,1)S(1)} custom-call(bf16[512,2048]{1,0:T(8,128)(2,1)S(1)} %collective-permute-done.6.refs_0_, bf16[256,2048]{1,0:T(8,128)(2,1)S(1)} %far.2.refs_1_, bf16[256,2048]{1,0:T(8,128)(2,1)S(1)} %far.3.refs_2_, f32[256,1024]{1,0:T(8,128)S(1)} %get-tuple-element.52.refs_3_, f32[256,1024]{1,0:T(8,128)S(1)} %get-tuple-element.53.refs_4_, ...), custom_call_target="tpu_custom_call" | custom-call | flops 6000000000 | bytes 36000000 | tf_op jit(solution)/shard_map/attend/pallas_call | solution.py:432
  48.0 1.4 %collective-permute-start.9 = (bf16[84,256]{1,0:T(8,128)(2,1)S(1)}, bf16[84,256]{1,0:T(8,128)(2,1)S(1)}, u32[]{:S(2)}, u32[]{:S(2)}) collective-permute-start(bf16[84,256]{1,0:T(8,128)(2,1)S(1)} %attend.1.refs_0_), channel_id=1, source_target_pairs={{0,16},{16,0},{1,17},{17,1},{2,18},{18,2},{3,19},{19,3},{4,20},{20... | collective-permute-start | bytes 129032 | tf_op jit(solution)/shard_map/ppermute | solution.py:38
  49.4 0.6 decode_own.1.refs_0_
  50.0 2.2 %collective-permute-done.9 = bf16[84,256]{1,0:T(8,128)(2,1)S(1)} collective-permute-done((bf16[84,256]{1,0:T(8,128)(2,1)S(1)}, bf16[84,256]{1,0:T(8,128)(2,1)S(1)}, u32[]{:S(2)}, u32[]{:S(2)}) %collective-permute-start.9) | collective-permute-done | bytes 43040 | tf_op jit(solution)/shard_map/ppermute | solution.py:38
  52.2 0.1 collective-permute-start.10
  52.2 3.2 %collective-permute-start.11 = (bf16[84,512]{1,0:T(8,128)(2,1)S(1)}, bf16[84,512]{1,0:T(8,128)(2,1)S(1)}, u32[]{:S(2)}, u32[]{:S(2)}) collective-permute-start(bf16[84,512]{1,0:T(8,128)(2,1)S(1)} %pad_maximum_fusion.refs_1_), channel_id=1, source_target_pairs={{0,15},{1,2},{2,1},{3,4},{4,3},{5,6},{6,5},{7,8},{8,7},{9,10},{10,... | collective-permute-start | bytes 258056 | tf_op jit(solution)/shard_map/ppermute | solution.py:50
  55.4 0.0 collective-permute-done.10.refs_2_
  55.4 2.5 %decode_near.1 = (f32[84,2048]{1,0:T(8,128)S(1)}, bf16[512,2048]{1,0:T(8,128)(2,1)S(1)}) custom-call(f32[84,2048]{1,0:T(8,128)S(1)} %decode_own.1.refs_0_, bf16[84,512]{1,0:T(8,128)(2,1)S(1)} %pad_maximum_fusion.refs_1_, bf16[84,512]{1,0:T(8,128)(2,1)S(1)} %collective-permute-done.10.refs_2_, s32[3,16,128]{2,1,0:T(8,128)S(1)} %copy-done.5), custom_call_target="tpu_custom_call" | custom-call | flops 50000000 | bytes 300000 | tf_op jit(solution)/shard_map/decode_near/pallas_call | solution.py:432
  57.9 1.1 %collective-permute-done.11.refs_1_ = bf16[84,512]{1,0:T(8,128)(2,1)S(1)} collective-permute-done((bf16[84,512]{1,0:T(8,128)(2,1)S(1)}, bf16[84,512]{1,0:T(8,128)(2,1)S(1)}, u32[]{:S(2)}, u32[]{:S(2)}) %collective-permute-start.11) | collective-permute-done | bytes 86048 | tf_op jit(solution)/shard_map/ppermute | solution.py:50
  59.0 1.5 %finish.1 = f32[84,16,128]{2,1,0:T(8,128)} custom-call(f32[84,2048]{1,0:T(8,128)S(1)} %get-tuple-element.59.refs_0_, bf16[84,512]{1,0:T(8,128)(2,1)S(1)} %collective-permute-done.11.refs_1_, bf16[512,2048]{1,0:T(8,128)(2,1)S(1)} %get-tuple-element.60.refs_2_), custom_call_target="tpu_custom_call" | custom-call | flops 50000000 | bytes 300000 | tf_op jit(solution)/shard_map/finish/pallas_call | solution.py:432
  (26 shorter events, 0.1 us)
Async XLA Ops:
  0.0 1.0 %copy-start.3 = (bf16[84,16,128]{2,1,0:T(8,128)(2,1)S(1)}, bf16[84,16,128]{2,1,0:T(8,128)(2,1)}, u32[]{:S(2)}) copy-start(bf16[84,16,128]{2,1,0:T(8,128)(2,1)} %refs_0_) | copy-start | bytes 1032196
  0.0 1.0 %copy-start.13 = (s32[16,256]{1,0:T(8,128)S(1)}, s32[16,256]{1,0:T(8,128)}, u32[]{:S(2)}) copy-start(s32[16,256]{1,0:T(8,128)} %refs_2_.4) | copy-start | bytes 49156
  0.0 1.0 %copy-start.15 = (s32[256]{0:T(256)S(1)}, s32[256]{0:T(256)}, u32[]{:S(2)}) copy-start(s32[256]{0:T(256)} %param.20) | copy-start | bytes 3076
  0.0 9.2 %copy-start.10 = (bf16[256,1024]{1,0:T(8,128)(2,1)S(1)}, bf16[256,1024]{1,0:T(8,128)(2,1)}, u32[]{:S(2)}) copy-start(bf16[256,1024]{1,0:T(8,128)(2,1)} %refs_8_.1) | copy-start | bytes 1572868
  1.5 13.9 %collective-permute-start = (bf16[84,256]{1,0:T(8,128)(2,1)S(1)}, bf16[84,256]{1,0:T(8,128)(2,1)S(1)}, u32[]{:S(2)}, u32[]{:S(2)}) collective-permute-start(bf16[84,256]{1,0:T(8,128)(2,1)S(1)} %get-tuple-element.33), channel_id=1, source_target_pairs={{0,1},{1,0},{2,3},{3,2},{4,5},{5,4},{6,7},{7,6},{8,9},{9,8},{10,11... | collective-permute-start | bytes 129032 | tf_op jit(solution)/shard_map/ppermute | solution.py:45
  2.0 13.4 %collective-permute-start.1 = (bf16[84,256]{1,0:T(8,128)(2,1)S(1)}, bf16[84,256]{1,0:T(8,128)(2,1)S(1)}, u32[]{:S(2)}, u32[]{:S(2)}) collective-permute-start(bf16[84,256]{1,0:T(8,128)(2,1)S(1)} %get-tuple-element.34), channel_id=1, source_target_pairs={{0,15},{1,2},{2,1},{3,4},{4,3},{5,6},{6,5},{7,8},{8,7},{9,10},{10,... | collective-permute-start | bytes 129032 | tf_op jit(solution)/shard_map/ppermute | solution.py:50
  7.7 5.4 %collective-permute-start.2 = (s32[16,256]{1,0:T(8,128)S(1)}, s32[16,256]{1,0:T(8,128)S(1)}, u32[]{:S(2)}, u32[]{:S(2)}) collective-permute-start(s32[16,256]{1,0:T(8,128)S(1)} %get-tuple-element.35.refs_0_.refs_2_), channel_id=1, source_target_pairs={{0,16},{16,0},{1,17},{17,1},{2,18},{18,2},{3,19},{19,3},{4,20},{20... | collective-permute-start | bytes 49160 | tf_op jit(solution)/shard_map/ppermute | solution.py:38
  9.2 16.1 %collective-permute-start.5 = (bf16[256,1024]{1,0:T(8,128)(2,1)S(1)}, bf16[256,1024]{1,0:T(8,128)(2,1)S(1)}, u32[]{:S(2)}, u32[]{:S(2)}) collective-permute-start(bf16[256,1024]{1,0:T(8,128)(2,1)S(1)} %copy-done.10), channel_id=1, source_target_pairs={{0,16},{16,0},{1,17},{17,1},{2,18},{18,2},{3,19},{19,3},{4,20},{20... | collective-permute-start | bytes 1572872 | tf_op jit(solution)/shard_map/ppermute | solution.py:38
  9.7 12.6 %collective-permute-start.4 = (bf16[256,1024]{1,0:T(8,128)(2,1)S(1)}, bf16[256,1024]{1,0:T(8,128)(2,1)S(1)}, u32[]{:S(2)}, u32[]{:S(2)}) collective-permute-start(bf16[256,1024]{1,0:T(8,128)(2,1)S(1)} %copy-done.10), channel_id=1, source_target_pairs={{0,15},{1,2},{2,1},{3,4},{4,3},{5,6},{6,5},{7,8},{8,7},{9,10},{10,... | collective-permute-start | bytes 1572872 | tf_op jit(solution)/shard_map/ppermute | solution.py:50
  10.7 6.5 %copy-start.12 = (s32[32,256]{1,0:T(8,128)S(1)}, s32[32,256]{1,0:T(8,128)}, u32[]{:S(2)}) copy-start(s32[32,256]{1,0:T(8,128)} %refs_0_.1) | copy-start | bytes 98308
  10.7 6.5 %copy-start.16 = (s32[256]{0:T(256)S(1)}, s32[256]{0:T(256)}, u32[]{:S(2)}) copy-start(s32[256]{0:T(256)} %param.22) | copy-start | bytes 3076
  15.7 6.6 %collective-permute-start.3 = (bf16[84,512]{1,0:T(8,128)(2,1)S(1)}, bf16[84,512]{1,0:T(8,128)(2,1)S(1)}, u32[]{:S(2)}, u32[]{:S(2)}) collective-permute-start(bf16[84,512]{1,0:T(8,128)(2,1)S(1)} %get-tuple-element.45), channel_id=1, source_target_pairs={{0,16},{16,0},{1,17},{17,1},{2,18},{18,2},{3,19},{19,3},{4,20},{20... | collective-permute-start | bytes 258056 | tf_op jit(solution)/shard_map/ppermute | solution.py:38
  17.2 8.1 %copy-start = (bf16[1024,1024]{1,0:T(8,128)(2,1)S(1)}, bf16[1024,1024]{1,0:T(8,128)(2,1)}, u32[]{:S(2)}) copy-start(bf16[1024,1024]{1,0:T(8,128)(2,1)} %refs_2_.7) | copy-start | bytes 6291460
  17.2 8.1 %copy-start.1 = (bf16[1024,1024]{1,0:T(8,128)(2,1)S(1)}, bf16[1024,1024]{1,0:T(8,128)(2,1)}, u32[]{:S(2)}) copy-start(bf16[1024,1024]{1,0:T(8,128)(2,1)} %refs_3_.6) | copy-start | bytes 6291460
  17.2 8.1 %copy-start.2 = (bf16[1024,1024]{1,0:T(8,128)(2,1)S(1)}, bf16[1024,1024]{1,0:T(8,128)(2,1)}, u32[]{:S(2)}) copy-start(bf16[1024,1024]{1,0:T(8,128)(2,1)} %refs_4_.5) | copy-start | bytes 6291460
  17.3 8.1 %copy-start.4 = (bf16[84,1024]{1,0:T(8,128)(2,1)S(1)}, bf16[84,1024]{1,0:T(8,128)(2,1)}, u32[]{:S(2)}) copy-start(bf16[84,1024]{1,0:T(8,128)(2,1)} %refs_1_.3) | copy-start | bytes 516100
  17.3 8.1 %copy-start.6 = (f32[1024]{0:T(1024)S(1)}, f32[1024]{0:T(1024)}, u32[]{:S(2)}) copy-start(f32[1024]{0:T(1024)} %param.32) | copy-start | bytes 12292
  17.3 8.1 %copy-start.7 = (bf16[1024,1024]{1,0:T(8,128)(2,1)S(1)}, bf16[1024,1024]{1,0:T(8,128)(2,1)}, u32[]{:S(2)}) copy-start(bf16[1024,1024]{1,0:T(8,128)(2,1)} %refs_4_.3) | copy-start | bytes 6291460
  22.4 13.6 %collective-permute-start.8 = (bf16[256,1024]{1,0:T(8,128)(2,1)S(1)}, bf16[256,1024]{1,0:T(8,128)(2,1)S(1)}, u32[]{:S(2)}, u32[]{:S(2)}) collective-permute-start(bf16[256,1024]{1,0:T(8,128)(2,1)S(1)} %collective-permute-done.4.refs_6_), channel_id=1, source_target_pairs={{0,16},{16,0},{1,17},{17,1},{2,18},{18,2},{3,19},{19,3},{4,20},{20... | collective-permute-start | bytes 1572872 | tf_op jit(solution)/shard_map/ppermute | solution.py:38
  22.5 10.9 %collective-permute-start.7 = (bf16[84,512]{1,0:T(8,128)(2,1)S(1)}, bf16[84,512]{1,0:T(8,128)(2,1)S(1)}, u32[]{:S(2)}, u32[]{:S(2)}) collective-permute-start(bf16[84,512]{1,0:T(8,128)(2,1)S(1)} %mean.1.refs_0_), channel_id=1, source_target_pairs={{0,15},{1,2},{2,1},{3,4},{4,3},{5,6},{6,5},{7,8},{8,7},{9,10},{10,... | collective-permute-start | bytes 258056 | tf_op jit(solution)/shard_map/ppermute | solution.py:50
  33.4 5.3 %collective-permute-start.6 = (bf16[512,2048]{1,0:T(8,128)(2,1)S(1)}, bf16[512,2048]{1,0:T(8,128)(2,1)S(1)}, u32[]{:S(2)}, u32[]{:S(2)}) collective-permute-start(bf16[512,2048]{1,0:T(8,128)(2,1)S(1)} %get-tuple-element.48), channel_id=1, source_target_pairs={{0,1},{1,0},{2,3},{3,2},{4,5},{5,4},{6,7},{7,6},{8,9},{9,8},{10,11... | collective-permute-start | bytes 6291464 | tf_op jit(solution)/shard_map/ppermute | solution.py:45
  35.9 2.7 %copy-start.8 = (bf16[1024,1024]{1,0:T(8,128)(2,1)S(1)}, bf16[1024,1024]{1,0:T(8,128)(2,1)}, u32[]{:S(2)}) copy-start(bf16[1024,1024]{1,0:T(8,128)(2,1)} %refs_9_.1) | copy-start | bytes 6291460
  35.9 2.7 %copy-start.9 = (bf16[1024,1024]{1,0:T(8,128)(2,1)S(1)}, bf16[1024,1024]{1,0:T(8,128)(2,1)}, u32[]{:S(2)}) copy-start(bf16[1024,1024]{1,0:T(8,128)(2,1)} %refs_10_.1) | copy-start | bytes 6291460
  36.0 2.7 %copy-start.11 = (bf16[1024,84]{0,1:T(8,128)(2,1)S(1)}, bf16[1024,84]{0,1:T(8,128)(2,1)}, u32[]{:S(2)}) copy-start(bf16[1024,84]{0,1:T(8,128)(2,1)} %param.31) | copy-start | bytes 516100
  36.0 2.7 %copy-start.14 = (f32[1024]{0:T(1024)S(1)}, f32[1024]{0:T(1024)}, u32[]{:S(2)}) copy-start(f32[1024]{0:T(1024)} %param.33) | copy-start | bytes 12292
  38.7 10.7 %copy-start.5 = (s32[3,16,128]{2,1,0:T(8,128)S(1)}, s32[3,16,128]{2,1,0:T(8,128)}, u32[]{:S(2)}) copy-start(s32[3,16,128]{2,1,0:T(8,128)} %refs_3_.7) | copy-start | bytes 73732
  48.0 4.1 %collective-permute-start.9 = (bf16[84,256]{1,0:T(8,128)(2,1)S(1)}, bf16[84,256]{1,0:T(8,128)(2,1)S(1)}, u32[]{:S(2)}, u32[]{:S(2)}) collective-permute-start(bf16[84,256]{1,0:T(8,128)(2,1)S(1)} %attend.1.refs_0_), channel_id=1, source_target_pairs={{0,16},{16,0},{1,17},{17,1},{2,18},{18,2},{3,19},{19,3},{4,20},{20... | collective-permute-start | bytes 129032 | tf_op jit(solution)/shard_map/ppermute | solution.py:38
  52.2 3.3 %collective-permute-start.10 = (bf16[84,512]{1,0:T(8,128)(2,1)S(1)}, bf16[84,512]{1,0:T(8,128)(2,1)S(1)}, u32[]{:S(2)}, u32[]{:S(2)}) collective-permute-start(bf16[84,512]{1,0:T(8,128)(2,1)S(1)} %pad_maximum_fusion.refs_1_), channel_id=1, source_target_pairs={{0,1},{1,0},{2,3},{3,2},{4,5},{5,4},{6,7},{7,6},{8,9},{9,8},{10,11... | collective-permute-start | bytes 258056 | tf_op jit(solution)/shard_map/ppermute | solution.py:45
  52.2 6.7 %collective-permute-start.11 = (bf16[84,512]{1,0:T(8,128)(2,1)S(1)}, bf16[84,512]{1,0:T(8,128)(2,1)S(1)}, u32[]{:S(2)}, u32[]{:S(2)}) collective-permute-start(bf16[84,512]{1,0:T(8,128)(2,1)S(1)} %pad_maximum_fusion.refs_1_), channel_id=1, source_target_pairs={{0,15},{1,2},{2,1},{3,4},{4,3},{5,6},{6,5},{7,8},{8,7},{9,10},{10,... | collective-permute-start | bytes 258056 | tf_op jit(solution)/shard_map/ppermute | solution.py:50

commit v6 on v5

--- a/solution.py
+++ b/solution.py
@@ -564,7 +564,7 @@
             pltpu.VMEM((SLOTS, 2 * nodes, 2 * sector_nodes), BF16),
             pltpu.VMEM((nodes, features), BF16),
         ],
-        mib=28,
+        mib=40,
         micros=12,
     )
     sums = shape((variables, cells), F32)

time: 60.8 us -> 60.4 us (level)
  no operation moved by 1% of the time
where the time goes in v6:
time: 60.4 us; the launch traced here: 60.3 us
  Pallas kernels  35.1 us (58%)
  starting transfers between devices  17.6 us (29%)
  waiting for transfers between devices  5.98 us (10%)
  local copies, waits for them, and re-layouts  1.05 us (2%)
    pallas_call x15, Pallas kernels, call(): pl.pallas_call(run, name=name, out_shape=outs, in_specs=specs, out_specs=...  35.1 us
    ppermute x4, starting transfers between devices, from_far(): lax.ppermute(value, 'lon', [(i, (i - 1 + 2 * (i % 2)) % count) for i in r...  11.8 us
    ppermute x5, starting transfers between devices, from_bands(): lax.ppermute(value, 'lat', [(i, (i - step) % count) for i in range(count)])  5.12 us
    ppermute x5, waiting for transfers between devices, from_bands(): lax.ppermute(value, 'lat', [(i, (i - step) % count) for i in range(count)])  5.03 us
  transfers between devices with their start and end apart: 12, of which 3 were waited for; matrix products, arithmetic and copies ran while one was open for 0% of the time, Pallas kernels for 40%

profile of v6, /device:TPU:0, one launch (start us, length us, event | category | flops | bytes accessed | tf_op | source)
XLA Modules:
  0.0 60.3 jit_solution(16146612238968952213)
XLA Ops:
  0.0 1.0 %copy-done.3 = bf16[84,16,128]{2,1,0:T(8,128)(2,1)S(1)} copy-done((bf16[84,16,128]{2,1,0:T(8,128)(2,1)S(1)}, bf16[84,16,128]{2,1,0:T(8,128)(2,1)}, u32[]{:S(2)}) %copy-start.3) | copy-done | bytes 344088
  1.0 0.5 prep.1
  1.5 0.5 collective-permute-start
  2.0 5.7 %collective-permute-start.1 = (bf16[84,256]{1,0:T(8,128)(2,1)S(1)}, bf16[84,256]{1,0:T(8,128)(2,1)S(1)}, u32[]{:S(2)}, u32[]{:S(2)}) collective-permute-start(bf16[84,256]{1,0:T(8,128)(2,1)S(1)} %get-tuple-element.34), channel_id=1, source_target_pairs={{0,15},{1,2},{2,1},{3,4},{4,3},{5,6},{6,5},{7,8},{8,7},{9,10},{10,... | collective-permute-start | bytes 129032 | tf_op jit(solution)/shard_map/ppermute | solution.py:50
  7.7 1.5 %collective-permute-start.2 = (s32[16,256]{1,0:T(8,128)S(1)}, s32[16,256]{1,0:T(8,128)S(1)}, u32[]{:S(2)}, u32[]{:S(2)}) collective-permute-start(s32[16,256]{1,0:T(8,128)S(1)} %get-tuple-element.35.refs_0_.refs_2_), channel_id=1, source_target_pairs={{0,16},{16,0},{1,17},{17,1},{2,18},{18,2},{3,19},{19,3},{4,20},{20... | collective-permute-start | bytes 49160 | tf_op jit(solution)/shard_map/ppermute | solution.py:38
  9.2 0.5 collective-permute-start.5
  9.7 0.0 collective-permute-start.4
  9.7 0.9 %flat.1.refs_1_ = bf16[84,2048]{1,0:T(8,128)(2,1)S(1)} custom-call(bf16[84,16,128]{2,1,0:T(8,128)(2,1)S(1)} %copy-done.3), custom_call_target="tpu_custom_call" | custom-call | flops 50000000 | bytes 300000 | tf_op jit(solution)/shard_map/flat/pallas_call | solution.py:432
  10.7 0.0 copy-start.12
  10.7 0.0 copy-start.16
  10.7 2.3 %encode.2 = (f32[84,256]{1,0:T(8,128)S(1)}, bf16[512,256]{1,0:T(8,128)(2,1)S(1)}) custom-call(s32[16,256]{1,0:T(8,128)S(1)} %get-tuple-element.35.refs_0_.refs_2_, bf16[84,2048]{1,0:T(8,128)(2,1)S(1)} %flat.1.refs_1_), custom_call_target="tpu_custom_call" | custom-call | flops 1500000000 | bytes 9000000 | tf_op jit(solution)/shard_map/encode/pallas_call | solution.py:432
  13.0 0.0 collective-permute-done.2.refs_0_.refs_3_
  13.1 2.3 %encode.3 = (f32[84,256]{1,0:T(8,128)S(1)}, bf16[512,256]{1,0:T(8,128)(2,1)S(1)}) custom-call(s32[16,256]{1,0:T(8,128)S(1)} %collective-permute-done.2.refs_0_.refs_3_, bf16[84,2048]{1,0:T(8,128)(2,1)S(1)} %flat.1.refs_1_), custom_call_target="tpu_custom_call" | custom-call | flops 50000000 | bytes 300000 | tf_op jit(solution)/shard_map/encode/pallas_call | solution.py:432
  15.4 0.0 collective-permute-done.refs_0_
  15.4 0.0 collective-permute-done.1.refs_1_
  15.4 0.2 rim.1
  15.7 1.6 %collective-permute-start.3 = (bf16[84,512]{1,0:T(8,128)(2,1)S(1)}, bf16[84,512]{1,0:T(8,128)(2,1)S(1)}, u32[]{:S(2)}, u32[]{:S(2)}) collective-permute-start(bf16[84,512]{1,0:T(8,128)(2,1)S(1)} %get-tuple-element.45), channel_id=1, source_target_pairs={{0,16},{16,0},{1,17},{17,1},{2,18},{18,2},{3,19},{19,3},{4,20},{20... | collective-permute-start | bytes 258056 | tf_op jit(solution)/shard_map/ppermute | solution.py:38
  17.2 0.0 copy-start.2
  17.2 0.0 copy-start.4
  17.3 0.0 copy-start.6
  17.3 0.0 copy-start.7
  17.3 2.2 %bias.1 = (f32[256,512]{1,0:T(8,128)S(1)}, f32[256,1024]{1,0:T(8,128)S(1)}) custom-call(s32[32,256]{1,0:T(8,128)S(1)} %copy-done.12, s32[1,256]{1,0:T(1,128)S(1)} %bitcast.11), custom_call_target="tpu_custom_call" | custom-call | flops 15000000512 | bytes 90000000 | tf_op jit(solution)/shard_map/bias/pallas_call | solution.py:432
  19.5 2.9 %collective-permute-done.3.refs_1_ = bf16[84,512]{1,0:T(8,128)(2,1)S(1)} collective-permute-done((bf16[84,512]{1,0:T(8,128)(2,1)S(1)}, bf16[84,512]{1,0:T(8,128)(2,1)S(1)}, u32[]{:S(2)}, u32[]{:S(2)}) %collective-permute-start.3) | collective-permute-done | bytes 86048 | tf_op jit(solution)/shard_map/ppermute | solution.py:38
  22.4 0.2 collective-permute-start.8
  22.5 2.8 %collective-permute-start.7 = (bf16[84,512]{1,0:T(8,128)(2,1)S(1)}, bf16[84,512]{1,0:T(8,128)(2,1)S(1)}, u32[]{:S(2)}, u32[]{:S(2)}) collective-permute-start(bf16[84,512]{1,0:T(8,128)(2,1)S(1)} %mean.1.refs_0_), channel_id=1, source_target_pairs={{0,15},{1,2},{2,1},{3,4},{4,3},{5,6},{6,5},{7,8},{8,7},{9,10},{10,... | collective-permute-start | bytes 258056 | tf_op jit(solution)/shard_map/ppermute | solution.py:50
  25.3 0.0 collective-permute-done.5.refs_9_
  25.4 7.9 %own.1 = (f32[256,1024]{1,0:T(8,128)S(1)}, bf16[256,1024]{1,0:T(8,128)(2,1)S(1)}, bf16[512,2048]{1,0:T(8,128)(2,1)S(1)}, f32[256,1024]{1,0:T(8,128)S(1)}, f32[25...) custom-call(bf16[84,512]{1,0:T(8,128)(2,1)S(1)} %mean.1.refs_0_, f32[256,512]{1,0:T(8,128)S(1)} %get-tuple-element.43.refs_1_, ...), custom_call_target="tpu_custom_call" | custom-call | flops 5000000000 | bytes 30000000 | tf_op jit(solution)/shard_map/own/pallas_call | solution.py:432
  33.3 0.1 collective-permute-start.6
  33.4 0.0 collective-permute-done.7.refs_0_
  33.4 2.4 %far.2.refs_1_ = bf16[256,2048]{1,0:T(8,128)(2,1)S(1)} custom-call(bf16[84,512]{1,0:T(8,128)(2,1)S(1)} %collective-permute-done.7.refs_0_, bf16[84,1024]{1,0:T(8,128)(2,1)S(1)} %copy-done.4, bf16[1024,1024]{1,0:T(8,128)(2,1)S(1)} %copy-done, bf16[1024,1024]{1,0:T(8,128)(2,1)S(1)} %copy-done.1, bf16[1024,1024]{1,0:T(8,128)(2,1)S(1)} %copy-done.2, ...), custom_call_target="tpu_custom_call" | custom-call | flops 50000000 | bytes 300000 | tf_op jit(solution)/shard_map/far/pallas_call | solution.py:432
  35.8 0.0 copy-start.8
  35.9 0.0 copy-start.9
  35.9 0.0 copy-start.11
  35.9 0.0 copy-start.14
  35.9 0.0 collective-permute-done.8.refs_6_
  35.9 2.7 %far.3.refs_2_ = bf16[256,2048]{1,0:T(8,128)(2,1)S(1)} custom-call(bf16[84,512]{1,0:T(8,128)(2,1)S(1)} %collective-permute-done.7.refs_0_, bf16[84,1024]{1,0:T(8,128)(2,1)S(1)} %copy-done.4, bf16[1024,1024]{1,0:T(8,128)(2,1)S(1)} %copy-done, bf16[1024,1024]{1,0:T(8,128)(2,1)S(1)} %copy-done.1, bf16[1024,1024]{1,0:T(8,128)(2,1)S(1)} %copy-done.2, ...), custom_call_target="tpu_custom_call" | custom-call | flops 30000001024 | bytes 180000000 | tf_op jit(solution)/shard_map/far/pallas_call | solution.py:432
  38.6 0.0 collective-permute-done.6.refs_0_
  38.6 0.0 copy-start.5
  38.6 9.0 %attend.1.refs_0_ = bf16[84,256]{1,0:T(8,128)(2,1)S(1)} custom-call(bf16[512,2048]{1,0:T(8,128)(2,1)S(1)} %collective-permute-done.6.refs_0_, bf16[256,2048]{1,0:T(8,128)(2,1)S(1)} %far.2.refs_1_, bf16[256,2048]{1,0:T(8,128)(2,1)S(1)} %far.3.refs_2_, f32[256,1024]{1,0:T(8,128)S(1)} %get-tuple-element.52.refs_3_, f32[256,1024]{1,0:T(8,128)S(1)} %get-tuple-element.53.refs_4_, ...), custom_call_target="tpu_custom_call" | custom-call | flops 6000000000 | bytes 36000000 | tf_op jit(solution)/shard_map/attend/pallas_call | solution.py:432
  47.7 1.4 %collective-permute-start.9 = (bf16[84,256]{1,0:T(8,128)(2,1)S(1)}, bf16[84,256]{1,0:T(8,128)(2,1)S(1)}, u32[]{:S(2)}, u32[]{:S(2)}) collective-permute-start(bf16[84,256]{1,0:T(8,128)(2,1)S(1)} %attend.1.refs_0_), channel_id=1, source_target_pairs={{0,16},{16,0},{1,17},{17,1},{2,18},{18,2},{3,19},{19,3},{4,20},{20... | collective-permute-start | bytes 129032 | tf_op jit(solution)/shard_map/ppermute | solution.py:38
  49.1 0.6 decode_own.1.refs_0_
  49.6 2.2 %collective-permute-done.9 = bf16[84,256]{1,0:T(8,128)(2,1)S(1)} collective-permute-done((bf16[84,256]{1,0:T(8,128)(2,1)S(1)}, bf16[84,256]{1,0:T(8,128)(2,1)S(1)}, u32[]{:S(2)}, u32[]{:S(2)}) %collective-permute-start.9) | collective-permute-done | bytes 43040 | tf_op jit(solution)/shard_map/ppermute | solution.py:38
  51.8 0.1 collective-permute-start.10
  51.9 3.3 %collective-permute-start.11 = (bf16[84,512]{1,0:T(8,128)(2,1)S(1)}, bf16[84,512]{1,0:T(8,128)(2,1)S(1)}, u32[]{:S(2)}, u32[]{:S(2)}) collective-permute-start(bf16[84,512]{1,0:T(8,128)(2,1)S(1)} %pad_maximum_fusion.refs_1_), channel_id=1, source_target_pairs={{0,15},{1,2},{2,1},{3,4},{4,3},{5,6},{6,5},{7,8},{8,7},{9,10},{10,... | collective-permute-start | bytes 258056 | tf_op jit(solution)/shard_map/ppermute | solution.py:50
  55.2 0.0 collective-permute-done.10.refs_2_
  55.2 2.5 %decode_near.1 = (f32[84,2048]{1,0:T(8,128)S(1)}, bf16[512,2048]{1,0:T(8,128)(2,1)S(1)}) custom-call(f32[84,2048]{1,0:T(8,128)S(1)} %decode_own.1.refs_0_, bf16[84,512]{1,0:T(8,128)(2,1)S(1)} %pad_maximum_fusion.refs_1_, bf16[84,512]{1,0:T(8,128)(2,1)S(1)} %collective-permute-done.10.refs_2_, s32[3,16,128]{2,1,0:T(8,128)S(1)} %copy-done.5), custom_call_target="tpu_custom_call" | custom-call | flops 50000000 | bytes 300000 | tf_op jit(solution)/shard_map/decode_near/pallas_call | solution.py:432
  57.7 0.9 %collective-permute-done.11.refs_1_ = bf16[84,512]{1,0:T(8,128)(2,1)S(1)} collective-permute-done((bf16[84,512]{1,0:T(8,128)(2,1)S(1)}, bf16[84,512]{1,0:T(8,128)(2,1)S(1)}, u32[]{:S(2)}, u32[]{:S(2)}) %collective-permute-start.11) | collective-permute-done | bytes 86048 | tf_op jit(solution)/shard_map/ppermute | solution.py:50
  58.6 1.5 %finish.1 = f32[84,16,128]{2,1,0:T(8,128)} custom-call(f32[84,2048]{1,0:T(8,128)S(1)} %get-tuple-element.59.refs_0_, bf16[84,512]{1,0:T(8,128)(2,1)S(1)} %collective-permute-done.11.refs_1_, bf16[512,2048]{1,0:T(8,128)(2,1)S(1)} %get-tuple-element.60.refs_2_), custom_call_target="tpu_custom_call" | custom-call | flops 50000000 | bytes 300000 | tf_op jit(solution)/shard_map/finish/pallas_call | solution.py:432
  (26 shorter events, 0.1 us)
Async XLA Ops:
  0.0 1.0 %copy-start.3 = (bf16[84,16,128]{2,1,0:T(8,128)(2,1)S(1)}, bf16[84,16,128]{2,1,0:T(8,128)(2,1)}, u32[]{:S(2)}) copy-start(bf16[84,16,128]{2,1,0:T(8,128)(2,1)} %refs_0_) | copy-start | bytes 1032196
  0.0 1.0 %copy-start.13 = (s32[16,256]{1,0:T(8,128)S(1)}, s32[16,256]{1,0:T(8,128)}, u32[]{:S(2)}) copy-start(s32[16,256]{1,0:T(8,128)} %refs_2_.4) | copy-start | bytes 49156
  0.0 1.0 %copy-start.15 = (s32[256]{0:T(256)S(1)}, s32[256]{0:T(256)}, u32[]{:S(2)}) copy-start(s32[256]{0:T(256)} %param.20) | copy-start | bytes 3076
  0.0 9.2 %copy-start.10 = (bf16[256,1024]{1,0:T(8,128)(2,1)S(1)}, bf16[256,1024]{1,0:T(8,128)(2,1)}, u32[]{:S(2)}) copy-start(bf16[256,1024]{1,0:T(8,128)(2,1)} %refs_8_.1) | copy-start | bytes 1572868
  1.5 13.9 %collective-permute-start = (bf16[84,256]{1,0:T(8,128)(2,1)S(1)}, bf16[84,256]{1,0:T(8,128)(2,1)S(1)}, u32[]{:S(2)}, u32[]{:S(2)}) collective-permute-start(bf16[84,256]{1,0:T(8,128)(2,1)S(1)} %get-tuple-element.33), channel_id=1, source_target_pairs={{0,1},{1,0},{2,3},{3,2},{4,5},{5,4},{6,7},{7,6},{8,9},{9,8},{10,11... | collective-permute-start | bytes 129032 | tf_op jit(solution)/shard_map/ppermute | solution.py:45
  2.0 13.4 %collective-permute-start.1 = (bf16[84,256]{1,0:T(8,128)(2,1)S(1)}, bf16[84,256]{1,0:T(8,128)(2,1)S(1)}, u32[]{:S(2)}, u32[]{:S(2)}) collective-permute-start(bf16[84,256]{1,0:T(8,128)(2,1)S(1)} %get-tuple-element.34), channel_id=1, source_target_pairs={{0,15},{1,2},{2,1},{3,4},{4,3},{5,6},{6,5},{7,8},{8,7},{9,10},{10,... | collective-permute-start | bytes 129032 | tf_op jit(solution)/shard_map/ppermute | solution.py:50
  7.7 5.4 %collective-permute-start.2 = (s32[16,256]{1,0:T(8,128)S(1)}, s32[16,256]{1,0:T(8,128)S(1)}, u32[]{:S(2)}, u32[]{:S(2)}) collective-permute-start(s32[16,256]{1,0:T(8,128)S(1)} %get-tuple-element.35.refs_0_.refs_2_), channel_id=1, source_target_pairs={{0,16},{16,0},{1,17},{17,1},{2,18},{18,2},{3,19},{19,3},{4,20},{20... | collective-permute-start | bytes 49160 | tf_op jit(solution)/shard_map/ppermute | solution.py:38
  9.2 16.1 %collective-permute-start.5 = (bf16[256,1024]{1,0:T(8,128)(2,1)S(1)}, bf16[256,1024]{1,0:T(8,128)(2,1)S(1)}, u32[]{:S(2)}, u32[]{:S(2)}) collective-permute-start(bf16[256,1024]{1,0:T(8,128)(2,1)S(1)} %copy-done.10), channel_id=1, source_target_pairs={{0,16},{16,0},{1,17},{17,1},{2,18},{18,2},{3,19},{19,3},{4,20},{20... | collective-permute-start | bytes 1572872 | tf_op jit(solution)/shard_map/ppermute | solution.py:38
  9.7 12.6 %collective-permute-start.4 = (bf16[256,1024]{1,0:T(8,128)(2,1)S(1)}, bf16[256,1024]{1,0:T(8,128)(2,1)S(1)}, u32[]{:S(2)}, u32[]{:S(2)}) collective-permute-start(bf16[256,1024]{1,0:T(8,128)(2,1)S(1)} %copy-done.10), channel_id=1, source_target_pairs={{0,15},{1,2},{2,1},{3,4},{4,3},{5,6},{6,5},{7,8},{8,7},{9,10},{10,... | collective-permute-start | bytes 1572872 | tf_op jit(solution)/shard_map/ppermute | solution.py:50
  10.7 6.5 %copy-start.12 = (s32[32,256]{1,0:T(8,128)S(1)}, s32[32,256]{1,0:T(8,128)}, u32[]{:S(2)}) copy-start(s32[32,256]{1,0:T(8,128)} %refs_0_.1) | copy-start | bytes 98308
  10.7 6.5 %copy-start.16 = (s32[256]{0:T(256)S(1)}, s32[256]{0:T(256)}, u32[]{:S(2)}) copy-start(s32[256]{0:T(256)} %param.22) | copy-start | bytes 3076
  15.7 6.6 %collective-permute-start.3 = (bf16[84,512]{1,0:T(8,128)(2,1)S(1)}, bf16[84,512]{1,0:T(8,128)(2,1)S(1)}, u32[]{:S(2)}, u32[]{:S(2)}) collective-permute-start(bf16[84,512]{1,0:T(8,128)(2,1)S(1)} %get-tuple-element.45), channel_id=1, source_target_pairs={{0,16},{16,0},{1,17},{17,1},{2,18},{18,2},{3,19},{19,3},{4,20},{20... | collective-permute-start | bytes 258056 | tf_op jit(solution)/shard_map/ppermute | solution.py:38
  17.2 8.1 %copy-start = (bf16[1024,1024]{1,0:T(8,128)(2,1)S(1)}, bf16[1024,1024]{1,0:T(8,128)(2,1)}, u32[]{:S(2)}) copy-start(bf16[1024,1024]{1,0:T(8,128)(2,1)} %refs_2_.7) | copy-start | bytes 6291460
  17.2 8.1 %copy-start.1 = (bf16[1024,1024]{1,0:T(8,128)(2,1)S(1)}, bf16[1024,1024]{1,0:T(8,128)(2,1)}, u32[]{:S(2)}) copy-start(bf16[1024,1024]{1,0:T(8,128)(2,1)} %refs_3_.6) | copy-start | bytes 6291460
  17.2 8.1 %copy-start.2 = (bf16[1024,1024]{1,0:T(8,128)(2,1)S(1)}, bf16[1024,1024]{1,0:T(8,128)(2,1)}, u32[]{:S(2)}) copy-start(bf16[1024,1024]{1,0:T(8,128)(2,1)} %refs_4_.5) | copy-start | bytes 6291460
  17.2 8.1 %copy-start.4 = (bf16[84,1024]{1,0:T(8,128)(2,1)S(1)}, bf16[84,1024]{1,0:T(8,128)(2,1)}, u32[]{:S(2)}) copy-start(bf16[84,1024]{1,0:T(8,128)(2,1)} %refs_1_.3) | copy-start | bytes 516100
  17.3 8.1 %copy-start.6 = (f32[1024]{0:T(1024)S(1)}, f32[1024]{0:T(1024)}, u32[]{:S(2)}) copy-start(f32[1024]{0:T(1024)} %param.32) | copy-start | bytes 12292
  17.3 8.1 %copy-start.7 = (bf16[1024,1024]{1,0:T(8,128)(2,1)S(1)}, bf16[1024,1024]{1,0:T(8,128)(2,1)}, u32[]{:S(2)}) copy-start(bf16[1024,1024]{1,0:T(8,128)(2,1)} %refs_4_.3) | copy-start | bytes 6291460
  22.4 13.5 %collective-permute-start.8 = (bf16[256,1024]{1,0:T(8,128)(2,1)S(1)}, bf16[256,1024]{1,0:T(8,128)(2,1)S(1)}, u32[]{:S(2)}, u32[]{:S(2)}) collective-permute-start(bf16[256,1024]{1,0:T(8,128)(2,1)S(1)} %collective-permute-done.4.refs_6_), channel_id=1, source_target_pairs={{0,16},{16,0},{1,17},{17,1},{2,18},{18,2},{3,19},{19,3},{4,20},{20... | collective-permute-start | bytes 1572872 | tf_op jit(solution)/shard_map/ppermute | solution.py:38
  22.5 10.8 %collective-permute-start.7 = (bf16[84,512]{1,0:T(8,128)(2,1)S(1)}, bf16[84,512]{1,0:T(8,128)(2,1)S(1)}, u32[]{:S(2)}, u32[]{:S(2)}) collective-permute-start(bf16[84,512]{1,0:T(8,128)(2,1)S(1)} %mean.1.refs_0_), channel_id=1, source_target_pairs={{0,15},{1,2},{2,1},{3,4},{4,3},{5,6},{6,5},{7,8},{8,7},{9,10},{10,... | collective-permute-start | bytes 258056 | tf_op jit(solution)/shard_map/ppermute | solution.py:50
  33.3 5.3 %collective-permute-start.6 = (bf16[512,2048]{1,0:T(8,128)(2,1)S(1)}, bf16[512,2048]{1,0:T(8,128)(2,1)S(1)}, u32[]{:S(2)}, u32[]{:S(2)}) collective-permute-start(bf16[512,2048]{1,0:T(8,128)(2,1)S(1)} %get-tuple-element.48), channel_id=1, source_target_pairs={{0,1},{1,0},{2,3},{3,2},{4,5},{5,4},{6,7},{7,6},{8,9},{9,8},{10,11... | collective-permute-start | bytes 6291464 | tf_op jit(solution)/shard_map/ppermute | solution.py:45
  35.8 2.7 %copy-start.8 = (bf16[1024,1024]{1,0:T(8,128)(2,1)S(1)}, bf16[1024,1024]{1,0:T(8,128)(2,1)}, u32[]{:S(2)}) copy-start(bf16[1024,1024]{1,0:T(8,128)(2,1)} %refs_9_.1) | copy-start | bytes 6291460
  35.9 2.7 %copy-start.9 = (bf16[1024,1024]{1,0:T(8,128)(2,1)S(1)}, bf16[1024,1024]{1,0:T(8,128)(2,1)}, u32[]{:S(2)}) copy-start(bf16[1024,1024]{1,0:T(8,128)(2,1)} %refs_10_.1) | copy-start | bytes 6291460
  35.9 2.7 %copy-start.11 = (bf16[1024,84]{0,1:T(8,128)(2,1)S(1)}, bf16[1024,84]{0,1:T(8,128)(2,1)}, u32[]{:S(2)}) copy-start(bf16[1024,84]{0,1:T(8,128)(2,1)} %param.31) | copy-start | bytes 516100
  35.9 2.7 %copy-start.14 = (f32[1024]{0:T(1024)S(1)}, f32[1024]{0:T(1024)}, u32[]{:S(2)}) copy-start(f32[1024]{0:T(1024)} %param.33) | copy-start | bytes 12292
  38.6 10.4 %copy-start.5 = (s32[3,16,128]{2,1,0:T(8,128)S(1)}, s32[3,16,128]{2,1,0:T(8,128)}, u32[]{:S(2)}) copy-start(s32[3,16,128]{2,1,0:T(8,128)} %refs_3_.7) | copy-start | bytes 73732
  47.7 4.1 %collective-permute-start.9 = (bf16[84,256]{1,0:T(8,128)(2,1)S(1)}, bf16[84,256]{1,0:T(8,128)(2,1)S(1)}, u32[]{:S(2)}, u32[]{:S(2)}) collective-permute-start(bf16[84,256]{1,0:T(8,128)(2,1)S(1)} %attend.1.refs_0_), channel_id=1, source_target_pairs={{0,16},{16,0},{1,17},{17,1},{2,18},{18,2},{3,19},{19,3},{4,20},{20... | collective-permute-start | bytes 129032 | tf_op jit(solution)/shard_map/ppermute | solution.py:38
  51.8 3.4 %collective-permute-start.10 = (bf16[84,512]{1,0:T(8,128)(2,1)S(1)}, bf16[84,512]{1,0:T(8,128)(2,1)S(1)}, u32[]{:S(2)}, u32[]{:S(2)}) collective-permute-start(bf16[84,512]{1,0:T(8,128)(2,1)S(1)} %pad_maximum_fusion.refs_1_), channel_id=1, source_target_pairs={{0,1},{1,0},{2,3},{3,2},{4,5},{5,4},{6,7},{7,6},{8,9},{9,8},{10,11... | collective-permute-start | bytes 258056 | tf_op jit(solution)/shard_map/ppermute | solution.py:45
  51.9 6.7 %collective-permute-start.11 = (bf16[84,512]{1,0:T(8,128)(2,1)S(1)}, bf16[84,512]{1,0:T(8,128)(2,1)S(1)}, u32[]{:S(2)}, u32[]{:S(2)}) collective-permute-start(bf16[84,512]{1,0:T(8,128)(2,1)S(1)} %pad_maximum_fusion.refs_1_), channel_id=1, source_target_pairs={{0,15},{1,2},{2,1},{3,4},{4,3},{5,6},{6,5},{7,8},{8,7},{9,10},{10,... | collective-permute-start | bytes 258056 | tf_op jit(solution)/shard_map/ppermute | solution.py:50

commit v7 on v6

--- a/solution.py
+++ b/solution.py
@@ -535,7 +535,7 @@
             pltpu.VMEM((SLOTS, 2 * nodes, sector_nodes), F32),
             pltpu.VMEM((SLOTS, 2 * nodes, sector_nodes), BF16),
         ],
-        mib=30,
+        mib=20,
         micros=10,
     )
     pair_near = from_near(pair)

time: 60.4 us -> 59.9 us (level)
  transfers between devices with their start and end apart: 12 -> 12, of which waited for: 3 -> 3; matrix products, arithmetic and copies ran while one was open for 0% -> 0% of each run, Pallas kernels for 40% -> 41%
where the time goes in v7:
time: 59.9 us; the launch traced here: 59.7 us
  Pallas kernels  34.6 us (58%)
  starting transfers between devices  17.5 us (29%)
  waiting for transfers between devices  6.07 us (10%)
  local copies, waits for them, and re-layouts  1.05 us (2%)
    pallas_call x15, Pallas kernels, call(): pl.pallas_call(run, name=name, out_shape=outs, in_specs=specs, out_specs=...  34.6 us
    ppermute x4, starting transfers between devices, from_far(): lax.ppermute(value, 'lon', [(i, (i - 1 + 2 * (i % 2)) % count) for i in r...  11.7 us
    ppermute x5, starting transfers between devices, from_bands(): lax.ppermute(value, 'lat', [(i, (i - step) % count) for i in range(count)])  5.14 us
    ppermute x5, waiting for transfers between devices, from_bands(): lax.ppermute(value, 'lat', [(i, (i - step) % count) for i in range(count)])  5.02 us
  transfers between devices with their start and end apart: 12, of which 3 were waited for; matrix products, arithmetic and copies ran while one was open for 0% of the time, Pallas kernels for 41%

profile of v7, /device:TPU:0, one launch (start us, length us, event | category | flops | bytes accessed | tf_op | source)
XLA Modules:
  0.0 59.7 jit_solution(6022181447966432459)
XLA Ops:
  0.0 1.0 %copy-done.3 = bf16[84,16,128]{2,1,0:T(8,128)(2,1)S(1)} copy-done((bf16[84,16,128]{2,1,0:T(8,128)(2,1)S(1)}, bf16[84,16,128]{2,1,0:T(8,128)(2,1)}, u32[]{:S(2)}) %copy-start.3) | copy-done | bytes 344088
  1.0 0.5 prep.1
  1.5 0.5 collective-permute-start
  2.0 5.7 %collective-permute-start.1 = (bf16[84,256]{1,0:T(8,128)(2,1)S(1)}, bf16[84,256]{1,0:T(8,128)(2,1)S(1)}, u32[]{:S(2)}, u32[]{:S(2)}) collective-permute-start(bf16[84,256]{1,0:T(8,128)(2,1)S(1)} %get-tuple-element.34), channel_id=1, source_target_pairs={{0,15},{1,2},{2,1},{3,4},{4,3},{5,6},{6,5},{7,8},{8,7},{9,10},{10,... | collective-permute-start | bytes 129032 | tf_op jit(solution)/shard_map/ppermute | solution.py:50
  7.7 1.5 %collective-permute-start.2 = (s32[16,256]{1,0:T(8,128)S(1)}, s32[16,256]{1,0:T(8,128)S(1)}, u32[]{:S(2)}, u32[]{:S(2)}) collective-permute-start(s32[16,256]{1,0:T(8,128)S(1)} %get-tuple-element.35.refs_0_.refs_2_), channel_id=1, source_target_pairs={{0,16},{16,0},{1,17},{17,1},{2,18},{18,2},{3,19},{19,3},{4,20},{20... | collective-permute-start | bytes 49160 | tf_op jit(solution)/shard_map/ppermute | solution.py:38
  9.2 0.5 collective-permute-start.5
  9.7 0.0 collective-permute-start.4
  9.7 0.9 %flat.1.refs_1_ = bf16[84,2048]{1,0:T(8,128)(2,1)S(1)} custom-call(bf16[84,16,128]{2,1,0:T(8,128)(2,1)S(1)} %copy-done.3), custom_call_target="tpu_custom_call" | custom-call | flops 50000000 | bytes 300000 | tf_op jit(solution)/shard_map/flat/pallas_call | solution.py:432
  10.7 0.0 copy-start.12
  10.7 0.0 copy-start.16
  10.7 2.3 %encode.2 = (f32[84,256]{1,0:T(8,128)S(1)}, bf16[512,256]{1,0:T(8,128)(2,1)S(1)}) custom-call(s32[16,256]{1,0:T(8,128)S(1)} %get-tuple-element.35.refs_0_.refs_2_, bf16[84,2048]{1,0:T(8,128)(2,1)S(1)} %flat.1.refs_1_), custom_call_target="tpu_custom_call" | custom-call | flops 1500000000 | bytes 9000000 | tf_op jit(solution)/shard_map/encode/pallas_call | solution.py:432
  13.0 0.0 collective-permute-done.2.refs_0_.refs_3_
  13.1 2.3 %encode.3 = (f32[84,256]{1,0:T(8,128)S(1)}, bf16[512,256]{1,0:T(8,128)(2,1)S(1)}) custom-call(s32[16,256]{1,0:T(8,128)S(1)} %collective-permute-done.2.refs_0_.refs_3_, bf16[84,2048]{1,0:T(8,128)(2,1)S(1)} %flat.1.refs_1_), custom_call_target="tpu_custom_call" | custom-call | flops 50000000 | bytes 300000 | tf_op jit(solution)/shard_map/encode/pallas_call | solution.py:432
  15.4 0.0 collective-permute-done.refs_0_
  15.4 0.0 collective-permute-done.1.refs_1_
  15.4 0.2 rim.1
  15.7 1.6 %collective-permute-start.3 = (bf16[84,512]{1,0:T(8,128)(2,1)S(1)}, bf16[84,512]{1,0:T(8,128)(2,1)S(1)}, u32[]{:S(2)}, u32[]{:S(2)}) collective-permute-start(bf16[84,512]{1,0:T(8,128)(2,1)S(1)} %get-tuple-element.45), channel_id=1, source_target_pairs={{0,16},{16,0},{1,17},{17,1},{2,18},{18,2},{3,19},{19,3},{4,20},{20... | collective-permute-start | bytes 258056 | tf_op jit(solution)/shard_map/ppermute | solution.py:38
  17.2 0.0 copy-start.2
  17.2 0.0 copy-start.4
  17.3 0.0 copy-start.6
  17.3 0.0 copy-start.7
  17.3 2.2 %bias.1 = (f32[256,512]{1,0:T(8,128)S(1)}, f32[256,1024]{1,0:T(8,128)S(1)}) custom-call(s32[32,256]{1,0:T(8,128)S(1)} %copy-done.12, s32[1,256]{1,0:T(1,128)S(1)} %bitcast.11), custom_call_target="tpu_custom_call" | custom-call | flops 15000000512 | bytes 90000000 | tf_op jit(solution)/shard_map/bias/pallas_call | solution.py:432
  19.5 2.9 %collective-permute-done.3.refs_1_ = bf16[84,512]{1,0:T(8,128)(2,1)S(1)} collective-permute-done((bf16[84,512]{1,0:T(8,128)(2,1)S(1)}, bf16[84,512]{1,0:T(8,128)(2,1)S(1)}, u32[]{:S(2)}, u32[]{:S(2)}) %collective-permute-start.3) | collective-permute-done | bytes 86048 | tf_op jit(solution)/shard_map/ppermute | solution.py:38
  22.3 0.0 collective-permute-done.4.refs_6_
  22.4 0.2 collective-permute-start.8
  22.5 2.8 %collective-permute-start.7 = (bf16[84,512]{1,0:T(8,128)(2,1)S(1)}, bf16[84,512]{1,0:T(8,128)(2,1)S(1)}, u32[]{:S(2)}, u32[]{:S(2)}) collective-permute-start(bf16[84,512]{1,0:T(8,128)(2,1)S(1)} %mean.1.refs_0_), channel_id=1, source_target_pairs={{0,15},{1,2},{2,1},{3,4},{4,3},{5,6},{6,5},{7,8},{8,7},{9,10},{10,... | collective-permute-start | bytes 258056 | tf_op jit(solution)/shard_map/ppermute | solution.py:50
  25.3 0.0 collective-permute-done.5.refs_9_
  25.4 8.0 %own.1 = (f32[256,1024]{1,0:T(8,128)S(1)}, bf16[256,1024]{1,0:T(8,128)(2,1)S(1)}, bf16[512,2048]{1,0:T(8,128)(2,1)S(1)}, f32[256,1024]{1,0:T(8,128)S(1)}, f32[25...) custom-call(bf16[84,512]{1,0:T(8,128)(2,1)S(1)} %mean.1.refs_0_, f32[256,512]{1,0:T(8,128)S(1)} %get-tuple-element.43.refs_1_, ...), custom_call_target="tpu_custom_call" | custom-call | flops 5000000000 | bytes 30000000 | tf_op jit(solution)/shard_map/own/pallas_call | solution.py:432
  33.4 0.1 collective-permute-start.6
  33.4 0.0 collective-permute-done.7.refs_0_
  33.5 2.5 %far.2.refs_1_ = bf16[256,2048]{1,0:T(8,128)(2,1)S(1)} custom-call(bf16[84,512]{1,0:T(8,128)(2,1)S(1)} %collective-permute-done.7.refs_0_, bf16[84,1024]{1,0:T(8,128)(2,1)S(1)} %copy-done.4, bf16[1024,1024]{1,0:T(8,128)(2,1)S(1)} %copy-done, bf16[1024,1024]{1,0:T(8,128)(2,1)S(1)} %copy-done.1, bf16[1024,1024]{1,0:T(8,128)(2,1)S(1)} %copy-done.2, ...), custom_call_target="tpu_custom_call" | custom-call | flops 50000000 | bytes 300000 | tf_op jit(solution)/shard_map/far/pallas_call | solution.py:432
  35.9 0.0 copy-start.8
  35.9 0.0 copy-start.9
  36.0 0.0 copy-start.11
  36.0 0.0 copy-start.14
  36.0 0.0 collective-permute-done.8.refs_6_
  36.0 2.7 %far.3.refs_2_ = bf16[256,2048]{1,0:T(8,128)(2,1)S(1)} custom-call(bf16[84,512]{1,0:T(8,128)(2,1)S(1)} %collective-permute-done.7.refs_0_, bf16[84,1024]{1,0:T(8,128)(2,1)S(1)} %copy-done.4, bf16[1024,1024]{1,0:T(8,128)(2,1)S(1)} %copy-done, bf16[1024,1024]{1,0:T(8,128)(2,1)S(1)} %copy-done.1, bf16[1024,1024]{1,0:T(8,128)(2,1)S(1)} %copy-done.2, ...), custom_call_target="tpu_custom_call" | custom-call | flops 30000001024 | bytes 180000000 | tf_op jit(solution)/shard_map/far/pallas_call | solution.py:432
  38.7 0.0 collective-permute-done.6.refs_0_
  38.7 0.0 copy-start.5
  38.7 8.4 %attend.1.refs_0_ = bf16[84,256]{1,0:T(8,128)(2,1)S(1)} custom-call(bf16[512,2048]{1,0:T(8,128)(2,1)S(1)} %collective-permute-done.6.refs_0_, bf16[256,2048]{1,0:T(8,128)(2,1)S(1)} %far.2.refs_1_, bf16[256,2048]{1,0:T(8,128)(2,1)S(1)} %far.3.refs_2_, f32[256,1024]{1,0:T(8,128)S(1)} %get-tuple-element.52.refs_3_, f32[256,1024]{1,0:T(8,128)S(1)} %get-tuple-element.53.refs_4_, ...), custom_call_target="tpu_custom_call" | custom-call | flops 6000000000 | bytes 36000000 | tf_op jit(solution)/shard_map/attend/pallas_call | solution.py:432
  47.1 1.4 %collective-permute-start.9 = (bf16[84,256]{1,0:T(8,128)(2,1)S(1)}, bf16[84,256]{1,0:T(8,128)(2,1)S(1)}, u32[]{:S(2)}, u32[]{:S(2)}) collective-permute-start(bf16[84,256]{1,0:T(8,128)(2,1)S(1)} %attend.1.refs_0_), channel_id=1, source_target_pairs={{0,16},{16,0},{1,17},{17,1},{2,18},{18,2},{3,19},{19,3},{4,20},{20... | collective-permute-start | bytes 129032 | tf_op jit(solution)/shard_map/ppermute | solution.py:38
  48.5 0.6 decode_own.1.refs_0_
  49.1 2.2 %collective-permute-done.9 = bf16[84,256]{1,0:T(8,128)(2,1)S(1)} collective-permute-done((bf16[84,256]{1,0:T(8,128)(2,1)S(1)}, bf16[84,256]{1,0:T(8,128)(2,1)S(1)}, u32[]{:S(2)}, u32[]{:S(2)}) %collective-permute-start.9) | collective-permute-done | bytes 43040 | tf_op jit(solution)/shard_map/ppermute | solution.py:38
  51.2 0.1 collective-permute-start.10
  51.3 3.2 %collective-permute-start.11 = (bf16[84,512]{1,0:T(8,128)(2,1)S(1)}, bf16[84,512]{1,0:T(8,128)(2,1)S(1)}, u32[]{:S(2)}, u32[]{:S(2)}) collective-permute-start(bf16[84,512]{1,0:T(8,128)(2,1)S(1)} %pad_maximum_fusion.refs_1_), channel_id=1, source_target_pairs={{0,15},{1,2},{2,1},{3,4},{4,3},{5,6},{6,5},{7,8},{8,7},{9,10},{10,... | collective-permute-start | bytes 258056 | tf_op jit(solution)/shard_map/ppermute | solution.py:50
  54.6 2.5 %decode_near.1 = (f32[84,2048]{1,0:T(8,128)S(1)}, bf16[512,2048]{1,0:T(8,128)(2,1)S(1)}) custom-call(f32[84,2048]{1,0:T(8,128)S(1)} %decode_own.1.refs_0_, bf16[84,512]{1,0:T(8,128)(2,1)S(1)} %pad_maximum_fusion.refs_1_, bf16[84,512]{1,0:T(8,128)(2,1)S(1)} %collective-permute-done.10.refs_2_, s32[3,16,128]{2,1,0:T(8,128)S(1)} %copy-done.5), custom_call_target="tpu_custom_call" | custom-call | flops 50000000 | bytes 300000 | tf_op jit(solution)/shard_map/decode_near/pallas_call | solution.py:432
  57.0 1.0 %collective-permute-done.11.refs_1_ = bf16[84,512]{1,0:T(8,128)(2,1)S(1)} collective-permute-done((bf16[84,512]{1,0:T(8,128)(2,1)S(1)}, bf16[84,512]{1,0:T(8,128)(2,1)S(1)}, u32[]{:S(2)}, u32[]{:S(2)}) %collective-permute-start.11) | collective-permute-done | bytes 86048 | tf_op jit(solution)/shard_map/ppermute | solution.py:50
  58.0 1.5 %finish.1 = f32[84,16,128]{2,1,0:T(8,128)} custom-call(f32[84,2048]{1,0:T(8,128)S(1)} %get-tuple-element.59.refs_0_, bf16[84,512]{1,0:T(8,128)(2,1)S(1)} %collective-permute-done.11.refs_1_, bf16[512,2048]{1,0:T(8,128)(2,1)S(1)} %get-tuple-element.60.refs_2_), custom_call_target="tpu_custom_call" | custom-call | flops 50000000 | bytes 300000 | tf_op jit(solution)/shard_map/finish/pallas_call | solution.py:432
  (26 shorter events, 0.1 us)
Async XLA Ops:
  0.0 1.0 %copy-start.3 = (bf16[84,16,128]{2,1,0:T(8,128)(2,1)S(1)}, bf16[84,16,128]{2,1,0:T(8,128)(2,1)}, u32[]{:S(2)}) copy-start(bf16[84,16,128]{2,1,0:T(8,128)(2,1)} %refs_0_) | copy-start | bytes 1032196
  0.0 1.0 %copy-start.13 = (s32[16,256]{1,0:T(8,128)S(1)}, s32[16,256]{1,0:T(8,128)}, u32[]{:S(2)}) copy-start(s32[16,256]{1,0:T(8,128)} %refs_2_.4) | copy-start | bytes 49156
  0.0 1.0 %copy-start.15 = (s32[256]{0:T(256)S(1)}, s32[256]{0:T(256)}, u32[]{:S(2)}) copy-start(s32[256]{0:T(256)} %param.20) | copy-start | bytes 3076
  0.0 9.2 %copy-start.10 = (bf16[256,1024]{1,0:T(8,128)(2,1)S(1)}, bf16[256,1024]{1,0:T(8,128)(2,1)}, u32[]{:S(2)}) copy-start(bf16[256,1024]{1,0:T(8,128)(2,1)} %refs_8_.1) | copy-start | bytes 1572868
  1.5 13.9 %collective-permute-start = (bf16[84,256]{1,0:T(8,128)(2,1)S(1)}, bf16[84,256]{1,0:T(8,128)(2,1)S(1)}, u32[]{:S(2)}, u32[]{:S(2)}) collective-permute-start(bf16[84,256]{1,0:T(8,128)(2,1)S(1)} %get-tuple-element.33), channel_id=1, source_target_pairs={{0,1},{1,0},{2,3},{3,2},{4,5},{5,4},{6,7},{7,6},{8,9},{9,8},{10,11... | collective-permute-start | bytes 129032 | tf_op jit(solution)/shard_map/ppermute | solution.py:45
  2.0 13.4 %collective-permute-start.1 = (bf16[84,256]{1,0:T(8,128)(2,1)S(1)}, bf16[84,256]{1,0:T(8,128)(2,1)S(1)}, u32[]{:S(2)}, u32[]{:S(2)}) collective-permute-start(bf16[84,256]{1,0:T(8,128)(2,1)S(1)} %get-tuple-element.34), channel_id=1, source_target_pairs={{0,15},{1,2},{2,1},{3,4},{4,3},{5,6},{6,5},{7,8},{8,7},{9,10},{10,... | collective-permute-start | bytes 129032 | tf_op jit(solution)/shard_map/ppermute | solution.py:50
  7.7 5.4 %collective-permute-start.2 = (s32[16,256]{1,0:T(8,128)S(1)}, s32[16,256]{1,0:T(8,128)S(1)}, u32[]{:S(2)}, u32[]{:S(2)}) collective-permute-start(s32[16,256]{1,0:T(8,128)S(1)} %get-tuple-element.35.refs_0_.refs_2_), channel_id=1, source_target_pairs={{0,16},{16,0},{1,17},{17,1},{2,18},{18,2},{3,19},{19,3},{4,20},{20... | collective-permute-start | bytes 49160 | tf_op jit(solution)/shard_map/ppermute | solution.py:38
  9.2 16.1 %collective-permute-start.5 = (bf16[256,1024]{1,0:T(8,128)(2,1)S(1)}, bf16[256,1024]{1,0:T(8,128)(2,1)S(1)}, u32[]{:S(2)}, u32[]{:S(2)}) collective-permute-start(bf16[256,1024]{1,0:T(8,128)(2,1)S(1)} %copy-done.10), channel_id=1, source_target_pairs={{0,16},{16,0},{1,17},{17,1},{2,18},{18,2},{3,19},{19,3},{4,20},{20... | collective-permute-start | bytes 1572872 | tf_op jit(solution)/shard_map/ppermute | solution.py:38
  9.7 12.6 %collective-permute-start.4 = (bf16[256,1024]{1,0:T(8,128)(2,1)S(1)}, bf16[256,1024]{1,0:T(8,128)(2,1)S(1)}, u32[]{:S(2)}, u32[]{:S(2)}) collective-permute-start(bf16[256,1024]{1,0:T(8,128)(2,1)S(1)} %copy-done.10), channel_id=1, source_target_pairs={{0,15},{1,2},{2,1},{3,4},{4,3},{5,6},{6,5},{7,8},{8,7},{9,10},{10,... | collective-permute-start | bytes 1572872 | tf_op jit(solution)/shard_map/ppermute | solution.py:50
  10.7 6.5 %copy-start.12 = (s32[32,256]{1,0:T(8,128)S(1)}, s32[32,256]{1,0:T(8,128)}, u32[]{:S(2)}) copy-start(s32[32,256]{1,0:T(8,128)} %refs_0_.1) | copy-start | bytes 98308
  10.7 6.5 %copy-start.16 = (s32[256]{0:T(256)S(1)}, s32[256]{0:T(256)}, u32[]{:S(2)}) copy-start(s32[256]{0:T(256)} %param.22) | copy-start | bytes 3076
  15.7 6.6 %collective-permute-start.3 = (bf16[84,512]{1,0:T(8,128)(2,1)S(1)}, bf16[84,512]{1,0:T(8,128)(2,1)S(1)}, u32[]{:S(2)}, u32[]{:S(2)}) collective-permute-start(bf16[84,512]{1,0:T(8,128)(2,1)S(1)} %get-tuple-element.45), channel_id=1, source_target_pairs={{0,16},{16,0},{1,17},{17,1},{2,18},{18,2},{3,19},{19,3},{4,20},{20... | collective-permute-start | bytes 258056 | tf_op jit(solution)/shard_map/ppermute | solution.py:38
  17.2 8.1 %copy-start = (bf16[1024,1024]{1,0:T(8,128)(2,1)S(1)}, bf16[1024,1024]{1,0:T(8,128)(2,1)}, u32[]{:S(2)}) copy-start(bf16[1024,1024]{1,0:T(8,128)(2,1)} %refs_2_.7) | copy-start | bytes 6291460
  17.2 8.1 %copy-start.1 = (bf16[1024,1024]{1,0:T(8,128)(2,1)S(1)}, bf16[1024,1024]{1,0:T(8,128)(2,1)}, u32[]{:S(2)}) copy-start(bf16[1024,1024]{1,0:T(8,128)(2,1)} %refs_3_.6) | copy-start | bytes 6291460
  17.2 8.1 %copy-start.2 = (bf16[1024,1024]{1,0:T(8,128)(2,1)S(1)}, bf16[1024,1024]{1,0:T(8,128)(2,1)}, u32[]{:S(2)}) copy-start(bf16[1024,1024]{1,0:T(8,128)(2,1)} %refs_4_.5) | copy-start | bytes 6291460
  17.2 8.1 %copy-start.4 = (bf16[84,1024]{1,0:T(8,128)(2,1)S(1)}, bf16[84,1024]{1,0:T(8,128)(2,1)}, u32[]{:S(2)}) copy-start(bf16[84,1024]{1,0:T(8,128)(2,1)} %refs_1_.3) | copy-start | bytes 516100
  17.3 8.1 %copy-start.6 = (f32[1024]{0:T(1024)S(1)}, f32[1024]{0:T(1024)}, u32[]{:S(2)}) copy-start(f32[1024]{0:T(1024)} %param.32) | copy-start | bytes 12292
  17.3 8.1 %copy-start.7 = (bf16[1024,1024]{1,0:T(8,128)(2,1)S(1)}, bf16[1024,1024]{1,0:T(8,128)(2,1)}, u32[]{:S(2)}) copy-start(bf16[1024,1024]{1,0:T(8,128)(2,1)} %refs_4_.3) | copy-start | bytes 6291460
  22.4 13.6 %collective-permute-start.8 = (bf16[256,1024]{1,0:T(8,128)(2,1)S(1)}, bf16[256,1024]{1,0:T(8,128)(2,1)S(1)}, u32[]{:S(2)}, u32[]{:S(2)}) collective-permute-start(bf16[256,1024]{1,0:T(8,128)(2,1)S(1)} %collective-permute-done.4.refs_6_), channel_id=1, source_target_pairs={{0,16},{16,0},{1,17},{17,1},{2,18},{18,2},{3,19},{19,3},{4,20},{20... | collective-permute-start | bytes 1572872 | tf_op jit(solution)/shard_map/ppermute | solution.py:38
  22.5 10.9 %collective-permute-start.7 = (bf16[84,512]{1,0:T(8,128)(2,1)S(1)}, bf16[84,512]{1,0:T(8,128)(2,1)S(1)}, u32[]{:S(2)}, u32[]{:S(2)}) collective-permute-start(bf16[84,512]{1,0:T(8,128)(2,1)S(1)} %mean.1.refs_0_), channel_id=1, source_target_pairs={{0,15},{1,2},{2,1},{3,4},{4,3},{5,6},{6,5},{7,8},{8,7},{9,10},{10,... | collective-permute-start | bytes 258056 | tf_op jit(solution)/shard_map/ppermute | solution.py:50
  33.4 5.3 %collective-permute-start.6 = (bf16[512,2048]{1,0:T(8,128)(2,1)S(1)}, bf16[512,2048]{1,0:T(8,128)(2,1)S(1)}, u32[]{:S(2)}, u32[]{:S(2)}) collective-permute-start(bf16[512,2048]{1,0:T(8,128)(2,1)S(1)} %get-tuple-element.48), channel_id=1, source_target_pairs={{0,1},{1,0},{2,3},{3,2},{4,5},{5,4},{6,7},{7,6},{8,9},{9,8},{10,11... | collective-permute-start | bytes 6291464 | tf_op jit(solution)/shard_map/ppermute | solution.py:45
  35.9 2.8 %copy-start.8 = (bf16[1024,1024]{1,0:T(8,128)(2,1)S(1)}, bf16[1024,1024]{1,0:T(8,128)(2,1)}, u32[]{:S(2)}) copy-start(bf16[1024,1024]{1,0:T(8,128)(2,1)} %refs_9_.1) | copy-start | bytes 6291460
  35.9 2.8 %copy-start.9 = (bf16[1024,1024]{1,0:T(8,128)(2,1)S(1)}, bf16[1024,1024]{1,0:T(8,128)(2,1)}, u32[]{:S(2)}) copy-start(bf16[1024,1024]{1,0:T(8,128)(2,1)} %refs_10_.1) | copy-start | bytes 6291460
  36.0 2.8 %copy-start.11 = (bf16[1024,84]{0,1:T(8,128)(2,1)S(1)}, bf16[1024,84]{0,1:T(8,128)(2,1)}, u32[]{:S(2)}) copy-start(bf16[1024,84]{0,1:T(8,128)(2,1)} %param.31) | copy-start | bytes 516100
  36.0 2.8 %copy-start.14 = (f32[1024]{0:T(1024)S(1)}, f32[1024]{0:T(1024)}, u32[]{:S(2)}) copy-start(f32[1024]{0:T(1024)} %param.33) | copy-start | bytes 12292
  38.7 9.8 %copy-start.5 = (s32[3,16,128]{2,1,0:T(8,128)S(1)}, s32[3,16,128]{2,1,0:T(8,128)}, u32[]{:S(2)}) copy-start(s32[3,16,128]{2,1,0:T(8,128)} %refs_3_.7) | copy-start | bytes 73732
  47.1 4.1 %collective-permute-start.9 = (bf16[84,256]{1,0:T(8,128)(2,1)S(1)}, bf16[84,256]{1,0:T(8,128)(2,1)S(1)}, u32[]{:S(2)}, u32[]{:S(2)}) collective-permute-start(bf16[84,256]{1,0:T(8,128)(2,1)S(1)} %attend.1.refs_0_), channel_id=1, source_target_pairs={{0,16},{16,0},{1,17},{17,1},{2,18},{18,2},{3,19},{19,3},{4,20},{20... | collective-permute-start | bytes 129032 | tf_op jit(solution)/shard_map/ppermute | solution.py:38
  51.2 3.3 %collective-permute-start.10 = (bf16[84,512]{1,0:T(8,128)(2,1)S(1)}, bf16[84,512]{1,0:T(8,128)(2,1)S(1)}, u32[]{:S(2)}, u32[]{:S(2)}) collective-permute-start(bf16[84,512]{1,0:T(8,128)(2,1)S(1)} %pad_maximum_fusion.refs_1_), channel_id=1, source_target_pairs={{0,1},{1,0},{2,3},{3,2},{4,5},{5,4},{6,7},{7,6},{8,9},{9,8},{10,11... | collective-permute-start | bytes 258056 | tf_op jit(solution)/shard_map/ppermute | solution.py:45
  51.3 6.7 %collective-permute-start.11 = (bf16[84,512]{1,0:T(8,128)(2,1)S(1)}, bf16[84,512]{1,0:T(8,128)(2,1)S(1)}, u32[]{:S(2)}, u32[]{:S(2)}) collective-permute-start(bf16[84,512]{1,0:T(8,128)(2,1)S(1)} %pad_maximum_fusion.refs_1_), channel_id=1, source_target_pairs={{0,15},{1,2},{2,1},{3,4},{4,3},{5,6},{6,5},{7,8},{8,7},{9,10},{10,... | collective-permute-start | bytes 258056 | tf_op jit(solution)/shard_map/ppermute | solution.py:50
